TPU v7x, 32 devices: a whole 2x2x4 slice. The times are simulated.
32 devices in a mesh: row: 4 (over y, x), col: 8 (over z, core).
Axes of the slice: x: 2, y: 2, z: 4, core: 2. Of those that a mesh axis runs over, the one named last changes fastest.
Arguments:
- three_center: bfloat16 [4096, 6144], P(('row', 'col')), may hold values from -6 to 6
- density: bfloat16 [4096, 4096], P('row', 'col'), may hold values from -0.1875 to 0.1875
- block_mask: int32 [128, 48], P(('row', 'col')), may hold values 0 or 1
- density_mask: int32 [128, 128], P('row', 'col'), may hold values 0 or 1
- basis_count: int32 [128], replicated, may hold values from 8 to 32
- ri_count: int32 [48], replicated, may hold values from 16 to 128
Outputs:
- contracted: bfloat16 [4096, 6144], P('row', 'col')
All inputs are finite; a program needn't handle non-finite values. No bound on the sum of `block_mask` or of `density_mask` on one device may be relied on, other than what follows from the above.
Results may differ from a plain program's by a relative error of at most 0.001.
Values may be sent and summed in bfloat16 or wider, within the bound.
No kernel may reach another device: no remote copies, remote signals or barrier semaphores. Data moves between devices by JAX's collectives and lax.ppermute only.
A program may use at most 64 MiB of HBM per device.

v0:
```python
import jax
import jax.numpy as jnp
from jax import lax
from jax.sharding import PartitionSpec as P

BW = 32
RW = 128


def from_behind(x, axis, by):
    peers = lax.axis_size(axis)
    return lax.ppermute(x, axis, [(i, (i + by) % peers) for i in range(peers)])


def shards(three_center, density, block_mask, density_mask, basis_count, ri_count):
    ncols = lax.axis_size("col")
    row_idx = lax.axis_index("row")
    col_idx = lax.axis_index("col")
    bf16 = jnp.bfloat16
    local_atoms = block_mask.shape[0]
    col_blocks = block_mask.shape[1]
    first = (row_idx * ncols + col_idx) * local_atoms
    own_count = lax.dynamic_slice_in_dim(basis_count, first, local_atoms)
    row_ok = jnp.arange(BW)[None, :] < own_count[:, None]
    col_ok = jnp.arange(RW)[None, :] < ri_count[:, None]
    keep = row_ok[:, :, None, None] & col_ok[None, None, :, :] & (block_mask[:, None, :, None] > 0)
    screened = (three_center.reshape(local_atoms, BW, col_blocks, RW) * keep.astype(bf16)).reshape(
        three_center.shape
    )
    blocks = lax.all_to_all(screened, "col", split_axis=1, concat_axis=0, tiled=True)
    lam_atoms = density_mask.shape[0]
    sum_atoms = density_mask.shape[1]
    lam_count = lax.dynamic_slice_in_dim(basis_count, row_idx * lam_atoms, lam_atoms)
    sum_count = lax.dynamic_slice_in_dim(basis_count, col_idx * sum_atoms, sum_atoms)
    lam_ok = jnp.arange(BW)[None, :] < lam_count[:, None]
    sum_ok = jnp.arange(BW)[None, :] < sum_count[:, None]
    dkeep = (
        lam_ok[:, :, None, None] & sum_ok[None, None, :, :] & (density_mask[:, None, :, None] > 0)
    )
    dens = (density.reshape(lam_atoms, BW, sum_atoms, BW) * dkeep.astype(bf16)).reshape(
        density.shape
    )
    empty = jnp.zeros((dens.shape[0], blocks.shape[1]), jnp.float32)
    half = blocks.shape[0] // 2
    levels = ncols.bit_length() - 1
    current = dens
    for level in range(1, levels):
        moved = from_behind(current, "col", -(1 << level))
        current = jnp.where(2 * row_idx >> level & 1 == 1, moved, current)
    paired = blocks
    arrived = from_behind(paired[:half], "row", -1)
    advanced = jnp.concatenate([paired[half:], arrived], axis=0)
    paired = jnp.where(col_idx & 1 == 1, advanced, paired)
    for level in range(1, levels):
        moved = from_behind(paired, "row", -(1 << level - 1))
        paired = jnp.where(col_idx >> level & 1 == 1, moved, paired)

    def one_turn(step, carry):
        dcur, pairs, total = carry
        total = total + jnp.dot(dcur, pairs[:half], preferred_element_type=jnp.float32)
        dcur = from_behind(dcur, "col", -1)
        front = from_behind(pairs[:half], "row", -1)
        pairs = jnp.concatenate([pairs[half:], front], axis=0)
        return (dcur, pairs, total)

    current, paired, total = lax.fori_loop(0, ncols - 1, one_turn, (current, paired, empty))
    total = total + jnp.dot(current, paired[:half], preferred_element_type=jnp.float32)
    return total.astype(bf16)


def solution(mesh):
    in_specs = (
        P(("row", "col"), None),
        P("row", "col"),
        P(("row", "col"), None),
        P("row", "col"),
        P(),
        P(),
    )
    out_specs = P("row", "col")
    return jax.shard_map(shards, mesh=mesh, in_specs=in_specs, out_specs=out_specs, check_vma=False)
```

profile of v0, /device:TPU:0, one launch (start us, length us, event | category | flops | bytes accessed | tf_op | source)
XLA Modules:
  0.0 336.7 jit_solution(16690322530847357498)
XLA Ops:
  4.9 44.0 %all_to_all.19 = bf16[128,8,768]{2,0,1:T(8,128)(2,1)S(1)} all-to-all(bf16[128,8,768]{2,0,1:T(8,128)(2,1)S(1)} %bitcast.27), channel_id=1, replica_groups=mesh['row'=4,'col'=8] {'col'}, dimensions={1} | all-to-all | bytes 3145728 | tf_op jit(solution)/shard_map/all_to_all | solution.py:30
  49.9 2.4 collective-permute-start.4
  52.3 16.8 %collective-permute-done.4 = bf16[512,768]{1,0:T(8,128)(2,1)S(1)} collective-permute-done((bf16[512,768]{1,0:T(8,128)(2,1)}, bf16[512,768]{1,0:T(8,128)(2,1)S(1)}, u32[]{:S(2)}, u32[]{:S(2)}) %collective-permute-start.4) | collective-permute-done | bytes 786464 | tf_op jit(solution)/shard_map/ppermute | solution.py:12
  70.7 3.3 collective-permute-start.5
  75.3 4.2 %and.73 = pred[1024,512]{1,0:T(8,128)(4,1)S(1)} reshape(pred[32,32,16,32]{3,2,1,0:T(8,128)(4,1)S(1)} %and.72) | data formatting | bytes 1048576 | tf_op jit(solution)/shard_map/and | solution.py:38
  83.1 23.5 %collective-permute-done.5 = bf16[1024,768]{1,0:T(8,128)(2,1)} collective-permute-done((bf16[1024,768]{1,0:T(8,128)(2,1)}, bf16[1024,768]{1,0:T(8,128)(2,1)}, u32[]{:S(2)}, u32[]{:S(2)}) %collective-permute-start.5) | collective-permute-done | bytes 1572896 | tf_op jit(solution)/shard_map/ppermute | solution.py:12
  110.7 46.3 %collective-permute-done.3 = bf16[1024,512]{1,0:T(8,128)(2,1)S(1)} collective-permute-done((bf16[1024,512]{1,0:T(8,128)(2,1)}, bf16[1024,512]{1,0:T(8,128)(2,1)S(1)}, u32[]{:S(2)}, u32[]{:S(2)}) %collective-permute-start.3) | collective-permute-done | bytes 1048608 | tf_op jit(solution)/shard_map/ppermute | solution.py:12
  157.0 2.3 broadcast_select_fusion.3
  159.5 173.4 %while.15 = (s32[]{:T(128)}, bf16[1024,512]{1,0:T(8,128)(2,1)}, bf16[1024,768]{1,0:T(8,128)(2,1)S(1)}, f32[1024,768]{1,0:T(8,128)}, s32[]{:T(128)}, /*index=5*/s32[]{:T(128)}) while((s32[]{:T(128)}, bf16[1024,512]{1,0:T(8,128)(2,1)}, bf16[1024,768]{1,0:T(8,128)(2,1)S(1)}, f32[1024,768]{1,0:T(8,128)}, s32[]{:T(128)}, ...), condition=%wide.region_1.2_spmd.clone, body=%wide.region_0.1_spmd.clone.sunk | while | flops 810024960 | bytes 23855264 | solution.py:66
  166.2 2.6 select_add_fusion.2
  168.8 15.0 %collective-permute-done.1 = bf16[512,768]{1,0:T(8,128)(2,1)} collective-permute-done((bf16[512,768]{1,0:T(8,128)(2,1)}, bf16[512,768]{1,0:T(8,128)(2,1)}, u32[]{:S(2)}, u32[]{:S(2)}) %collective-permute-start.1) | collective-permute-done | bytes 786464 | tf_op jit(solution)/shard_map/while/body/eval_jaxpr/ppermute | solution.py:12
  190.6 4.5 %select_add_fusion.2 = f32[1024,768]{1,0:T(8,128)} fusion(f32[1024,768]{1,0:T(8,128)} %get-tuple-element.97, bf16[1024,512]{1,0:T(8,128)(2,1)S(1)} %copy.19, pred[]{:T(512)S(6)} %compare.3, bf16[1024,768]{1,0:T(8,128)(2,1)S(1)} %get-tuple-element.96), kind=kOutput, calls=%fused_computation.clone.1 | convolution fusion | flops 806879232 | bytes 8126465 | tf_op jit(solution)/shard_map/while/body/eval_jaxpr/dot_general | solution.py:60
  195.1 13.4 %collective-permute-done.1 = bf16[512,768]{1,0:T(8,128)(2,1)} collective-permute-done((bf16[512,768]{1,0:T(8,128)(2,1)}, bf16[512,768]{1,0:T(8,128)(2,1)}, u32[]{:S(2)}, u32[]{:S(2)}) %collective-permute-start.1) | collective-permute-done | bytes 786464 | tf_op jit(solution)/shard_map/while/body/eval_jaxpr/ppermute | solution.py:12
  215.2 4.5 %select_add_fusion.2 = f32[1024,768]{1,0:T(8,128)} fusion(f32[1024,768]{1,0:T(8,128)} %get-tuple-element.97, bf16[1024,512]{1,0:T(8,128)(2,1)S(1)} %copy.19, pred[]{:T(512)S(6)} %compare.3, bf16[1024,768]{1,0:T(8,128)(2,1)S(1)} %get-tuple-element.96), kind=kOutput, calls=%fused_computation.clone.1 | convolution fusion | flops 806879232 | bytes 8126465 | tf_op jit(solution)/shard_map/while/body/eval_jaxpr/dot_general | solution.py:60
  219.7 13.4 %collective-permute-done.1 = bf16[512,768]{1,0:T(8,128)(2,1)} collective-permute-done((bf16[512,768]{1,0:T(8,128)(2,1)}, bf16[512,768]{1,0:T(8,128)(2,1)}, u32[]{:S(2)}, u32[]{:S(2)}) %collective-permute-start.1) | collective-permute-done | bytes 786464 | tf_op jit(solution)/shard_map/while/body/eval_jaxpr/ppermute | solution.py:12
  239.8 4.5 %select_add_fusion.2 = f32[1024,768]{1,0:T(8,128)} fusion(f32[1024,768]{1,0:T(8,128)} %get-tuple-element.97, bf16[1024,512]{1,0:T(8,128)(2,1)S(1)} %copy.19, pred[]{:T(512)S(6)} %compare.3, bf16[1024,768]{1,0:T(8,128)(2,1)S(1)} %get-tuple-element.96), kind=kOutput, calls=%fused_computation.clone.1 | convolution fusion | flops 806879232 | bytes 8126465 | tf_op jit(solution)/shard_map/while/body/eval_jaxpr/dot_general | solution.py:60
  244.4 13.4 %collective-permute-done.1 = bf16[512,768]{1,0:T(8,128)(2,1)} collective-permute-done((bf16[512,768]{1,0:T(8,128)(2,1)}, bf16[512,768]{1,0:T(8,128)(2,1)}, u32[]{:S(2)}, u32[]{:S(2)}) %collective-permute-start.1) | collective-permute-done | bytes 786464 | tf_op jit(solution)/shard_map/while/body/eval_jaxpr/ppermute | solution.py:12
  264.5 4.5 %select_add_fusion.2 = f32[1024,768]{1,0:T(8,128)} fusion(f32[1024,768]{1,0:T(8,128)} %get-tuple-element.97, bf16[1024,512]{1,0:T(8,128)(2,1)S(1)} %copy.19, pred[]{:T(512)S(6)} %compare.3, bf16[1024,768]{1,0:T(8,128)(2,1)S(1)} %get-tuple-element.96), kind=kOutput, calls=%fused_computation.clone.1 | convolution fusion | flops 806879232 | bytes 8126465 | tf_op jit(solution)/shard_map/while/body/eval_jaxpr/dot_general | solution.py:60
  269.0 13.4 %collective-permute-done.1 = bf16[512,768]{1,0:T(8,128)(2,1)} collective-permute-done((bf16[512,768]{1,0:T(8,128)(2,1)}, bf16[512,768]{1,0:T(8,128)(2,1)}, u32[]{:S(2)}, u32[]{:S(2)}) %collective-permute-start.1) | collective-permute-done | bytes 786464 | tf_op jit(solution)/shard_map/while/body/eval_jaxpr/ppermute | solution.py:12
  289.1 4.5 %select_add_fusion.2 = f32[1024,768]{1,0:T(8,128)} fusion(f32[1024,768]{1,0:T(8,128)} %get-tuple-element.97, bf16[1024,512]{1,0:T(8,128)(2,1)S(1)} %copy.19, pred[]{:T(512)S(6)} %compare.3, bf16[1024,768]{1,0:T(8,128)(2,1)S(1)} %get-tuple-element.96), kind=kOutput, calls=%fused_computation.clone.1 | convolution fusion | flops 806879232 | bytes 8126465 | tf_op jit(solution)/shard_map/while/body/eval_jaxpr/dot_general | solution.py:60
  293.6 13.4 %collective-permute-done.1 = bf16[512,768]{1,0:T(8,128)(2,1)} collective-permute-done((bf16[512,768]{1,0:T(8,128)(2,1)}, bf16[512,768]{1,0:T(8,128)(2,1)}, u32[]{:S(2)}, u32[]{:S(2)}) %collective-permute-start.1) | collective-permute-done | bytes 786464 | tf_op jit(solution)/shard_map/while/body/eval_jaxpr/ppermute | solution.py:12
  313.8 4.5 %select_add_fusion.2 = f32[1024,768]{1,0:T(8,128)} fusion(f32[1024,768]{1,0:T(8,128)} %get-tuple-element.97, bf16[1024,512]{1,0:T(8,128)(2,1)S(1)} %copy.19, pred[]{:T(512)S(6)} %compare.3, bf16[1024,768]{1,0:T(8,128)(2,1)S(1)} %get-tuple-element.96), kind=kOutput, calls=%fused_computation.clone.1 | convolution fusion | flops 806879232 | bytes 8126465 | tf_op jit(solution)/shard_map/while/body/eval_jaxpr/dot_general | solution.py:60
  318.3 13.4 %collective-permute-done.1 = bf16[512,768]{1,0:T(8,128)(2,1)} collective-permute-done((bf16[512,768]{1,0:T(8,128)(2,1)}, bf16[512,768]{1,0:T(8,128)(2,1)}, u32[]{:S(2)}, u32[]{:S(2)}) %collective-permute-start.1) | collective-permute-done | bytes 786464 | tf_op jit(solution)/shard_map/while/body/eval_jaxpr/ppermute | solution.py:12
  332.9 2.4 fusion.2
  (82 shorter events, 66.4 us)
Async XLA Ops:
  49.9 19.2 %collective-permute-start.4 = (bf16[512,768]{1,0:T(8,128)(2,1)}, bf16[512,768]{1,0:T(8,128)(2,1)S(1)}, u32[]{:S(2)}, u32[]{:S(2)}) collective-permute-start(bf16[512,768]{1,0:T(8,128)(2,1)} %bitcast.4), channel_id=1, source_target_pairs={{0,24},{8,0},{16,8},{24,16},{1,25},{9,1},{17,9},{25,17},{2,26},{10... | collective-permute-start | bytes 2359304 | tf_op jit(solution)/shard_map/ppermute | solution.py:12
  69.1 4.9 %copy-start.2 = (s32[128]{0:T(128)S(1)}, s32[128]{0:T(128)}, u32[]{:S(2)}) copy-start(s32[128]{0:T(128)} %param.12) | copy-start | bytes 1540
  69.1 5.0 %copy-start.1 = (s32[32,16]{0,1:T(8,128)S(1)}, s32[32,16]{0,1:T(8,128)}, u32[]{:S(2)}) copy-start(s32[32,16]{0,1:T(8,128)} %param.11) | copy-start | bytes 6148
  70.7 36.0 %collective-permute-start.5 = (bf16[1024,768]{1,0:T(8,128)(2,1)}, bf16[1024,768]{1,0:T(8,128)(2,1)}, u32[]{:S(2)}, u32[]{:S(2)}) collective-permute-start(bf16[1024,768]{1,0:T(8,128)(2,1)} %maximum_select_fusion), channel_id=1, source_target_pairs={{0,24},{8,0},{16,8},{24,16},{1,25},{9,1},{17,9},{25,17},{2,26},{10... | collective-permute-start | bytes 4718600 | tf_op jit(solution)/shard_map/ppermute | solution.py:12
  81.2 28.4 %collective-permute-start.2 = (bf16[1024,512]{1,0:T(8,128)(2,1)S(1)}, bf16[1024,512]{1,0:T(8,128)(2,1)}, u32[]{:S(2)}, u32[]{:S(2)}) collective-permute-start(bf16[1024,512]{1,0:T(8,128)(2,1)S(1)} %and_select_fusion), channel_id=1, source_target_pairs={{0,6},{1,7},{2,0},{3,1},{4,2},{5,3},{6,4},{7,5},{8,14},{9,15},{10,... | collective-permute-start | bytes 3145736 | tf_op jit(solution)/shard_map/ppermute | solution.py:12
  108.2 51.1 %collective-permute-start.6 = (bf16[1024,768]{1,0:T(8,128)(2,1)S(1)}, bf16[1024,768]{1,0:T(8,128)(2,1)}, u32[]{:S(2)}, u32[]{:S(2)}) collective-permute-start(bf16[1024,768]{1,0:T(8,128)(2,1)S(1)} %broadcast_select_fusion), channel_id=1, source_target_pairs={{0,16},{8,24},{16,0},{24,8},{1,17},{9,25},{17,1},{25,9},{2,18},{10... | collective-permute-start | bytes 4718600 | tf_op jit(solution)/shard_map/ppermute | solution.py:12
  110.7 46.3 %collective-permute-start.3 = (bf16[1024,512]{1,0:T(8,128)(2,1)}, bf16[1024,512]{1,0:T(8,128)(2,1)S(1)}, u32[]{:S(2)}, u32[]{:S(2)}) collective-permute-start(bf16[1024,512]{1,0:T(8,128)(2,1)} %broadcast_select_fusion.2), channel_id=1, source_target_pairs={{0,4},{1,5},{2,6},{3,7},{4,0},{5,1},{6,2},{7,3},{8,12},{9,13},{10,... | collective-permute-start | bytes 3145736 | tf_op jit(solution)/shard_map/ppermute | solution.py:12
  160.7 24.3 %collective-permute-start = (bf16[1024,512]{1,0:T(8,128)(2,1)S(1)}, bf16[1024,512]{1,0:T(8,128)(2,1)}, u32[]{:S(2)}, u32[]{:S(2)}) collective-permute-start(bf16[1024,512]{1,0:T(8,128)(2,1)S(1)} %copy.19), channel_id=1, source_target_pairs={{0,7},{1,0},{2,1},{3,2},{4,3},{5,4},{6,5},{7,6},{8,15},{9,8},{10,9... | collective-permute-start | bytes 3145736 | tf_op jit(solution)/shard_map/while/body/eval_jaxpr/ppermute | solution.py:12
  163.9 19.9 %collective-permute-start.1 = (bf16[512,768]{1,0:T(8,128)(2,1)}, bf16[512,768]{1,0:T(8,128)(2,1)}, u32[]{:S(2)}, u32[]{:S(2)}) collective-permute-start(bf16[512,768]{1,0:T(8,128)(2,1)} %get-tuple-element.86), channel_id=1, source_target_pairs={{0,24},{8,0},{16,8},{24,16},{1,25},{9,1},{17,9},{25,17},{2,26},{10... | collective-permute-start | bytes 2359304 | tf_op jit(solution)/shard_map/while/body/eval_jaxpr/ppermute | solution.py:12
  186.3 23.4 %collective-permute-start = (bf16[1024,512]{1,0:T(8,128)(2,1)S(1)}, bf16[1024,512]{1,0:T(8,128)(2,1)}, u32[]{:S(2)}, u32[]{:S(2)}) collective-permute-start(bf16[1024,512]{1,0:T(8,128)(2,1)S(1)} %copy.19), channel_id=1, source_target_pairs={{0,7},{1,0},{2,1},{3,2},{4,3},{5,4},{6,5},{7,6},{8,15},{9,8},{10,9... | collective-permute-start | bytes 3145736 | tf_op jit(solution)/shard_map/while/body/eval_jaxpr/ppermute | solution.py:12
  189.4 19.1 %collective-permute-start.1 = (bf16[512,768]{1,0:T(8,128)(2,1)}, bf16[512,768]{1,0:T(8,128)(2,1)}, u32[]{:S(2)}, u32[]{:S(2)}) collective-permute-start(bf16[512,768]{1,0:T(8,128)(2,1)} %get-tuple-element.86), channel_id=1, source_target_pairs={{0,24},{8,0},{16,8},{24,16},{1,25},{9,1},{17,9},{25,17},{2,26},{10... | collective-permute-start | bytes 2359304 | tf_op jit(solution)/shard_map/while/body/eval_jaxpr/ppermute | solution.py:12
  210.9 23.4 %collective-permute-start = (bf16[1024,512]{1,0:T(8,128)(2,1)S(1)}, bf16[1024,512]{1,0:T(8,128)(2,1)}, u32[]{:S(2)}, u32[]{:S(2)}) collective-permute-start(bf16[1024,512]{1,0:T(8,128)(2,1)S(1)} %copy.19), channel_id=1, source_target_pairs={{0,7},{1,0},{2,1},{3,2},{4,3},{5,4},{6,5},{7,6},{8,15},{9,8},{10,9... | collective-permute-start | bytes 3145736 | tf_op jit(solution)/shard_map/while/body/eval_jaxpr/ppermute | solution.py:12
  214.0 19.1 %collective-permute-start.1 = (bf16[512,768]{1,0:T(8,128)(2,1)}, bf16[512,768]{1,0:T(8,128)(2,1)}, u32[]{:S(2)}, u32[]{:S(2)}) collective-permute-start(bf16[512,768]{1,0:T(8,128)(2,1)} %get-tuple-element.86), channel_id=1, source_target_pairs={{0,24},{8,0},{16,8},{24,16},{1,25},{9,1},{17,9},{25,17},{2,26},{10... | collective-permute-start | bytes 2359304 | tf_op jit(solution)/shard_map/while/body/eval_jaxpr/ppermute | solution.py:12
  235.6 23.4 %collective-permute-start = (bf16[1024,512]{1,0:T(8,128)(2,1)S(1)}, bf16[1024,512]{1,0:T(8,128)(2,1)}, u32[]{:S(2)}, u32[]{:S(2)}) collective-permute-start(bf16[1024,512]{1,0:T(8,128)(2,1)S(1)} %copy.19), channel_id=1, source_target_pairs={{0,7},{1,0},{2,1},{3,2},{4,3},{5,4},{6,5},{7,6},{8,15},{9,8},{10,9... | collective-permute-start | bytes 3145736 | tf_op jit(solution)/shard_map/while/body/eval_jaxpr/ppermute | solution.py:12
  238.7 19.1 %collective-permute-start.1 = (bf16[512,768]{1,0:T(8,128)(2,1)}, bf16[512,768]{1,0:T(8,128)(2,1)}, u32[]{:S(2)}, u32[]{:S(2)}) collective-permute-start(bf16[512,768]{1,0:T(8,128)(2,1)} %get-tuple-element.86), channel_id=1, source_target_pairs={{0,24},{8,0},{16,8},{24,16},{1,25},{9,1},{17,9},{25,17},{2,26},{10... | collective-permute-start | bytes 2359304 | tf_op jit(solution)/shard_map/while/body/eval_jaxpr/ppermute | solution.py:12
  260.2 23.4 %collective-permute-start = (bf16[1024,512]{1,0:T(8,128)(2,1)S(1)}, bf16[1024,512]{1,0:T(8,128)(2,1)}, u32[]{:S(2)}, u32[]{:S(2)}) collective-permute-start(bf16[1024,512]{1,0:T(8,128)(2,1)S(1)} %copy.19), channel_id=1, source_target_pairs={{0,7},{1,0},{2,1},{3,2},{4,3},{5,4},{6,5},{7,6},{8,15},{9,8},{10,9... | collective-permute-start | bytes 3145736 | tf_op jit(solution)/shard_map/while/body/eval_jaxpr/ppermute | solution.py:12
  263.3 19.1 %collective-permute-start.1 = (bf16[512,768]{1,0:T(8,128)(2,1)}, bf16[512,768]{1,0:T(8,128)(2,1)}, u32[]{:S(2)}, u32[]{:S(2)}) collective-permute-start(bf16[512,768]{1,0:T(8,128)(2,1)} %get-tuple-element.86), channel_id=1, source_target_pairs={{0,24},{8,0},{16,8},{24,16},{1,25},{9,1},{17,9},{25,17},{2,26},{10... | collective-permute-start | bytes 2359304 | tf_op jit(solution)/shard_map/while/body/eval_jaxpr/ppermute | solution.py:12
  284.9 23.4 %collective-permute-start = (bf16[1024,512]{1,0:T(8,128)(2,1)S(1)}, bf16[1024,512]{1,0:T(8,128)(2,1)}, u32[]{:S(2)}, u32[]{:S(2)}) collective-permute-start(bf16[1024,512]{1,0:T(8,128)(2,1)S(1)} %copy.19), channel_id=1, source_target_pairs={{0,7},{1,0},{2,1},{3,2},{4,3},{5,4},{6,5},{7,6},{8,15},{9,8},{10,9... | collective-permute-start | bytes 3145736 | tf_op jit(solution)/shard_map/while/body/eval_jaxpr/ppermute | solution.py:12
  288.0 19.1 %collective-permute-start.1 = (bf16[512,768]{1,0:T(8,128)(2,1)}, bf16[512,768]{1,0:T(8,128)(2,1)}, u32[]{:S(2)}, u32[]{:S(2)}) collective-permute-start(bf16[512,768]{1,0:T(8,128)(2,1)} %get-tuple-element.86), channel_id=1, source_target_pairs={{0,24},{8,0},{16,8},{24,16},{1,25},{9,1},{17,9},{25,17},{2,26},{10... | collective-permute-start | bytes 2359304 | tf_op jit(solution)/shard_map/while/body/eval_jaxpr/ppermute | solution.py:12
  309.5 23.4 %collective-permute-start = (bf16[1024,512]{1,0:T(8,128)(2,1)S(1)}, bf16[1024,512]{1,0:T(8,128)(2,1)}, u32[]{:S(2)}, u32[]{:S(2)}) collective-permute-start(bf16[1024,512]{1,0:T(8,128)(2,1)S(1)} %copy.19), channel_id=1, source_target_pairs={{0,7},{1,0},{2,1},{3,2},{4,3},{5,4},{6,5},{7,6},{8,15},{9,8},{10,9... | collective-permute-start | bytes 3145736 | tf_op jit(solution)/shard_map/while/body/eval_jaxpr/ppermute | solution.py:12
  312.6 19.1 %collective-permute-start.1 = (bf16[512,768]{1,0:T(8,128)(2,1)}, bf16[512,768]{1,0:T(8,128)(2,1)}, u32[]{:S(2)}, u32[]{:S(2)}) collective-permute-start(bf16[512,768]{1,0:T(8,128)(2,1)} %get-tuple-element.86), channel_id=1, source_target_pairs={{0,24},{8,0},{16,8},{24,16},{1,25},{9,1},{17,9},{25,17},{2,26},{10... | collective-permute-start | bytes 2359304 | tf_op jit(solution)/shard_map/while/body/eval_jaxpr/ppermute | solution.py:12
  332.9 2.4 copy-start
where the time goes:
time: 338 us; the launch traced here: 337 us
  waiting for transfers between devices  182 us (54%)
  blocking collectives  44 us (13%)
  starting transfers between devices  33.2 us (10%)
  matrix products  32 us (9%)
  local copies, waits for them, and re-layouts  23.8 us (7%)
  other arithmetic  21.6 us (6%)
    ppermute x19, waiting for transfers between devices, from_behind(): return lax.ppermute(x, axis, [(i, (i + by) % peers) for i in range(peers)])  182 us
    all_to_all x1, blocking collectives, shards(): lax.all_to_all(screened, 'col', split_axis=1, concat_axis=0, tiled=True)  44 us
    ppermute x19, starting transfers between devices, from_behind(): return lax.ppermute(x, axis, [(i, (i + by) % peers) for i in range(peers)])  33.2 us
    dot_general x7, matrix products, one_turn(): jnp.dot(dcur, pairs[:half], preferred_element_type=jnp.float32)  29.6 us
    concatenate x7, other arithmetic, one_turn(): pairs = jnp.concatenate([pairs[half:], front], axis=0)  8.65 us
    while x7, local copies, waits for them, and re-layouts  8.58 us
    slice x7, local copies, waits for them, and re-layouts, one_turn(): pairs = jnp.concatenate([pairs[half:], front], axis=0)  6.86 us
  transfers between devices with their start and end apart: 19, of which 10 were waited for; matrix products, arithmetic and copies ran while one was open for 17% of the time, Pallas kernels for 0%

commit v1 on v0

v1 whole, which is shorter than its diff:
```python
import functools

import jax
import jax.numpy as jnp
from jax import lax
from jax.experimental import pallas as pl
from jax.experimental.pallas import tpu as pltpu
from jax.sharding import PartitionSpec as P

BW = 32
RW = 128
VMEM = 48 * 1024 * 1024


def screen_integrals(tc, own_count, ri_count, block_mask, ncols):
    rows, cols = tc.shape
    atoms = rows // BW
    wide = cols // ncols
    blocks = wide // RW

    def body(count_ref, ri_ref, mask_ref, x_ref, o_ref):
        dest = pl.program_id(0)
        row = lax.broadcasted_iota(jnp.int32, (BW, RW), 0)
        col = lax.broadcasted_iota(jnp.int32, (BW, RW), 1)
        for b in range(blocks):
            block = dest * blocks + b
            inside = col < ri_ref[block]
            for a in range(atoms):
                limit = jnp.where(mask_ref[a, block] > 0, count_ref[a], 0)
                at = (pl.ds(a * BW, BW), pl.ds(b * RW, RW))
                x = x_ref[at].astype(jnp.float32)
                o_ref[(0,) + at] = jnp.where(inside & (row < limit), x, 0.0).astype(jnp.bfloat16)

    smem = pl.BlockSpec(memory_space=pltpu.SMEM)
    return pl.pallas_call(
        body,
        out_shape=jax.ShapeDtypeStruct((ncols, rows, wide), jnp.bfloat16),
        grid=(ncols,),
        in_specs=[smem, smem, smem, pl.BlockSpec((rows, wide), lambda i: (0, i))],
        out_specs=pl.BlockSpec((1, rows, wide), lambda i: (i, 0, 0)),
        compiler_params=pltpu.CompilerParams(vmem_limit_bytes=VMEM),
        name="screen_integrals",
    )(own_count, ri_count, block_mask, tc)


def spread(values, size, axis):
    shape = (values.shape[0], size) if axis == 1 else (size, values.shape[1])
    long = lax.broadcasted_iota(jnp.int32, shape, axis) // BW
    short = lax.broadcasted_iota(jnp.int32, shape, 1 - axis)
    return (long == short).astype(jnp.bfloat16)


def screen_density(dens, lam_count, sum_count, mask):
    rows, cols = dens.shape
    lam_atoms, sum_atoms = mask.shape

    def body(lam_ref, sum_ref, mask_ref, x_ref, o_ref):
        def member(atoms, size, count, slot_axis):
            shape = (size, atoms) if slot_axis == 0 else (atoms, size)
            place = lax.broadcasted_iota(jnp.int32, shape, slot_axis)
            atom = lax.broadcasted_iota(jnp.int32, shape, 1 - slot_axis)
            first = atom * BW
            return jnp.where((place >= first) & (place < first + count), 1.0, 0.0).astype(jnp.bfloat16)

        left = member(lam_atoms, rows, lam_ref[...], 0)
        right = member(sum_atoms, cols, sum_ref[...], 1)
        keep = jnp.where(mask_ref[...] > 0, 1.0, 0.0).astype(jnp.bfloat16)
        keep = jnp.dot(left, keep, preferred_element_type=jnp.float32).astype(jnp.bfloat16)
        keep = jnp.dot(keep, right, preferred_element_type=jnp.float32)
        o_ref[...] = jnp.where(keep > 0.5, x_ref[...].astype(jnp.float32), 0.0).astype(jnp.bfloat16)

    return pl.pallas_call(
        body,
        out_shape=jax.ShapeDtypeStruct((rows, cols), jnp.bfloat16),
        compiler_params=pltpu.CompilerParams(vmem_limit_bytes=VMEM),
        name="screen_density",
    )(lam_count.reshape(1, -1), sum_count.reshape(-1, 1), mask, dens)


def contract(dens, integrals):
    parts, rows, depth = dens.shape
    cols = integrals.shape[2]

    def body(d_ref, s_ref, o_ref, total):
        step = pl.program_id(0)
        part = jnp.dot(d_ref[0], s_ref[0], preferred_element_type=jnp.float32)

        @pl.when(step == 0)
        def _():
            total[...] = part

        @pl.when(step > 0)
        def _():
            total[...] += part

        @pl.when(step == parts - 1)
        def _():
            o_ref[...] = total[...].astype(jnp.bfloat16)

    return pl.pallas_call(
        body,
        out_shape=jax.ShapeDtypeStruct((rows, cols), jnp.bfloat16),
        grid=(parts,),
        in_specs=[
            pl.BlockSpec((1, rows, depth), lambda i: (i, 0, 0)),
            pl.BlockSpec((1, depth, cols), lambda i: (i, 0, 0)),
        ],
        out_specs=pl.BlockSpec((rows, cols), lambda i: (0, 0)),
        scratch_shapes=[pltpu.VMEM((rows, cols), jnp.float32)],
        compiler_params=pltpu.CompilerParams(vmem_limit_bytes=VMEM),
        cost_estimate=pl.CostEstimate(
            flops=2 * parts * rows * depth * cols,
            bytes_accessed=2 * parts * depth * (rows + cols) + 2 * rows * cols,
            transcendentals=0,
        ),
        name="contract",
    )(dens, integrals)


def shards(three_center, density, block_mask, density_mask, basis_count, ri_count):
    ncols = lax.axis_size("col")
    row = lax.axis_index("row")
    col = lax.axis_index("col")
    atoms = block_mask.shape[0]
    lam_atoms, sum_atoms = density_mask.shape
    own_count = lax.dynamic_slice_in_dim(basis_count, (row * ncols + col) * atoms, atoms)
    lam_count = lax.dynamic_slice_in_dim(basis_count, row * lam_atoms, lam_atoms)
    sum_count = lax.dynamic_slice_in_dim(basis_count, col * sum_atoms, sum_atoms)
    dens = screen_density(density, lam_count, sum_count, density_mask)
    screened = screen_integrals(three_center, own_count, ri_count, block_mask, ncols)
    dens_all = lax.all_gather(dens, "col")
    blocks = lax.all_to_all(screened, "col", split_axis=0, concat_axis=0, tiled=True)
    rows_all = lax.all_gather(blocks, "row")
    wide = blocks.shape[2]
    return contract(dens_all, rows_all.reshape(ncols, -1, wide))


def solution(mesh):
    in_specs = (
        P(("row", "col"), None),
        P("row", "col"),
        P(("row", "col"), None),
        P("row", "col"),
        P(),
        P(),
    )
    return jax.shard_map(
        shards, mesh=mesh, in_specs=in_specs, out_specs=P("row", "col"), check_vma=False
    )
```

time: 338 us -> 229 us (0.68)
  starting transfers between devices: 33.2 us -> 0.04 us
  matrix products: 32 us -> 0 us
  waiting for transfers between devices: 182 us -> 150 us
  other arithmetic: 21.6 us -> 0 us
  local copies, waits for them, and re-layouts: 23.8 us -> 4.64 us
  Pallas kernels: 0 us -> 16.4 us
  between operations: 0.13 us -> 13.4 us
    ppermute x19 -> x0, waiting for transfers between devices: 182 us -> none  [from_behind(): return lax.ppermute(x, axis, [(i, (i + by) % peers) for i in range(peers)])]
    all_gather x0 -> x2, waiting for transfers between devices: none -> 150 us  [the longest x1 83.7 us: shards(): dens_all = lax.all_gather(dens, 'col')]
    ppermute x19 -> x0, starting transfers between devices: 33.2 us -> none  [from_behind(): return lax.ppermute(x, axis, [(i, (i + by) % peers) for i in range(peers)])]
    dot_general x8 -> x0, matrix products: 32 us -> none  [the longest x7 29.6 us: one_turn(): jnp.dot(dcur, pairs[:half], preferred_element_type=jnp.float32)]
    pallas_call x0 -> x3, Pallas kernels: none -> 16.4 us  [the longest x1 13.4 us: contract(): pl.pallas_call(body, out_shape=jax.ShapeDtypeStruct((rows, cols), jnp.bfl...]
    concatenate x7 -> x0, other arithmetic: 8.65 us -> none  [one_turn(): pairs = jnp.concatenate([pairs[half:], front], axis=0)]
    while x7 -> x0, local copies, waits for them, and re-layouts: 8.58 us -> none
    slice x8 -> x0, local copies, waits for them, and re-layouts: 7.85 us -> none  [the longest x7 6.86 us: one_turn(): pairs = jnp.concatenate([pairs[half:], front], axis=0)]
  transfers between devices with their start and end apart: 19 -> 2, of which waited for: 10 -> 2; matrix products, arithmetic and copies ran while one was open for 17% -> 0% of each run, Pallas kernels for 0% -> 1%
where the time goes in v1:
time: 229 us
  waiting for transfers between devices  150 us (66%)
  blocking collectives  44.1 us (19%)
  Pallas kernels  16.4 us (7%)
  between operations  13.4 us (6%)
  local copies, waits for them, and re-layouts  4.64 us (2%)
    all_gather x1, waiting for transfers between devices, shards(): dens_all = lax.all_gather(dens, 'col')  83.7 us
    all_gather x1, waiting for transfers between devices, shards(): rows_all = lax.all_gather(blocks, 'row')  66.5 us
    all_to_all x1, blocking collectives, shards(): lax.all_to_all(screened, 'col', split_axis=0, concat_axis=0, tiled=True)  44.1 us
    pallas_call x1, Pallas kernels, contract(): pl.pallas_call(body, out_shape=jax.ShapeDtypeStruct((rows, cols), jnp.bfl...  13.4 us
  transfers between devices with their start and end apart: 2, of which 2 were waited for; matrix products, arithmetic and copies ran while one was open for 0% of the time, Pallas kernels for 1%

profile of v1, /device:TPU:0, one launch (start us, length us, event | category | flops | bytes accessed | tf_op | source)
XLA Modules:
  0.0 228.8 jit_solution(6340508872797203759)
XLA Ops:
  6.5 0.0 all-gather.7.cloned.1.call-start
  6.5 0.7 dynamic_slice.11.count_ref
  7.3 0.0 copy-start
  7.3 1.4 copy-done
  8.7 0.0 copy-start.2
  8.7 0.7 copy-done.2
  9.4 0.0 copy-start.3
  9.4 0.7 copy-done.3
  10.0 1.5 screen_integrals.1
  11.5 44.1 %all_to_all.5 = bf16[8,128,768]{2,1,0:T(8,128)(2,1)} all-to-all(bf16[8,128,768]{2,1,0:T(8,128)(2,1)S(1)} %screen_integrals.1), channel_id=1, replica_groups=mesh['row'=4,'col'=8] {'col'}, dimensions={0} | all-to-all | bytes 3145728 | tf_op jit(solution)/shard_map/all_to_all | solution.py:132
  55.6 0.0 all-gather.7.cloned.1.call-update
  55.6 0.0 all-gather.5.cloned.1.call-start
  55.7 0.6 copy-done.5
  56.2 0.1 dynamic-slice_bitcast_fusion
  56.3 0.1 copy.9.sum_ref
  56.4 0.0 copy-done.4
  56.4 0.1 copy.10.mask_ref
  56.5 0.1 dynamic-slice_bitcast_fusion.1.lam_ref
  56.5 0.3 copy-done.1
  56.8 1.5 screen_density.1
  58.3 0.0 all-gather.5.cloned.1.call-update
  58.4 66.5 %all-gather.7.cloned.1.call-done = bf16[32,128,768]{2,1,0:T(8,128)(2,1)} async-done(((bf16[8,128,768]{2,1,0:T(8,128)(2,1)}), bf16[32,128,768]{2,1,0:T(8,128)(2,1)}) %all-gather.7.cloned.1.call-update) | async-done | bytes 6291472 | tf_op jit(solution)/shard_map/all_gather | solution.py:133
  124.8 83.7 %all-gather.5.cloned.1.call-done = bf16[8192,512]{1,0:T(8,128)(2,1)} async-done(((bf16[1024,512]{1,0:T(8,128)(2,1)}), bf16[8192,512]{1,0:T(8,128)(2,1)}) %all-gather.5.cloned.1.call-update) | async-done | bytes 8388624 | tf_op jit(solution)/shard_map/all_gather | solution.py:131
  208.5 13.4 %contract.1 = bf16[1024,768]{1,0:T(8,128)(2,1)} custom-call(bf16[8,1024,512]{2,1,0:T(8,128)(2,1)} %bitcast.6, bf16[8,512,768]{2,1,0:T(8,128)(2,1)} %bitcast.7), custom_call_target="tpu_custom_call" | custom-call | flops 6442450944 | bytes 16252928 | tf_op jit(solution)/shard_map/contract/pallas_call | solution.py:100
  (3 shorter events, 0.0 us)
Async XLA Ops:
  6.5 118.3 %all-gather.7.cloned.1.call-start = ((), (), s32[]{:S(2)}) async-start(), calls=%async_computation.2 | async-start | bytes 7864320 | tf_op jit(solution)/shard_map/all_gather | solution.py:133
  7.3 1.4 copy-start
  8.7 0.7 copy-start.2
  9.4 0.7 copy-start.3
  55.6 0.7 copy-start.5
  55.6 0.8 copy-start.4
  55.6 1.3 copy-start.1
  55.6 152.9 %all-gather.5.cloned.1.call-start = ((), (), s32[]{:S(2)}) async-start(), calls=%async_computation.1 | async-start | bytes 9437184 | tf_op jit(solution)/shard_map/all_gather | solution.py:131
Sparse Core Ops, SparseCore 0:
  55.7 69.0 all-gather.6
  126.4 82.0 all-gather.4

commit v2 on v1

v2 whole, which is shorter than its diff:
```python
import jax
import jax.numpy as jnp
from jax import lax
from jax.experimental import pallas as pl
from jax.experimental.pallas import tpu as pltpu
from jax.sharding import PartitionSpec as P

BW = 32
RW = 128
CORES = 2
VMEM = 48 * 1024 * 1024
BF16 = jnp.bfloat16
F32 = jnp.float32
SMEM_SPEC = pl.BlockSpec(memory_space=pltpu.SMEM)
VMEM_SPEC = pl.BlockSpec(memory_space=pltpu.VMEM)
ANY_SPEC = pl.BlockSpec(memory_space=pl.ANY)


def params():
    return pltpu.CompilerParams(vmem_limit_bytes=VMEM)


def ones_where(cond):
    return jnp.where(cond, 1.0, 0.0).astype(BF16)


def iota(shape, axis):
    return lax.broadcasted_iota(jnp.int32, shape, axis)


def place_row(count_ref, base, atoms, width):
    lane = iota((1, atoms * width), 1)
    place = jnp.full(lane.shape, -1, jnp.int32)
    offset = jnp.int32(0)
    for a in range(atoms):
        count = count_ref[base + a]
        inside = (lane >= a * width) & (lane < a * width + count)
        place = jnp.where(inside, lane - a * width + offset, place)
        offset = offset + count
    return place


def pack_rows(count_ref, base, atoms, width, size):
    place = place_row(count_ref, base, atoms, width)
    return ones_where(iota((size, atoms * width), 0) == place)


def pack_cols(count_ref, base, atoms, width, size, out):
    gap = iota((width, size), 1) - iota((width, size), 0)
    slot = iota((width, size), 0)
    offset = jnp.int32(0)
    for a in range(atoms):
        count = count_ref[base + a]
        out[pl.ds(a * width, width), :] = ones_where((gap == offset) & (slot < count))
        offset = offset + count


def keep_mask(lam_count, sum_count, mask, rows, cols):
    def member(atoms, size, count, axis):
        shape = (size, atoms) if axis == 0 else (atoms, size)
        first = iota(shape, 1 - axis) * BW
        at = iota(shape, axis)
        return ones_where((at >= first) & (at < first + count))

    left = member(mask.shape[0], rows, lam_count, 0)
    right = member(mask.shape[1], cols, sum_count, 1)
    keep = jnp.dot(left, ones_where(mask > 0), preferred_element_type=F32).astype(BF16)
    return jnp.dot(keep, right, preferred_element_type=F32)


def screen_integrals(tc, own_count, ri_count, block_mask, ncols):
    rows, cols = tc.shape
    atoms = rows // BW
    wide = cols // ncols
    blocks = wide // RW

    def body(count_ref, ri_ref, mask_ref, x_ref, o_ref):
        dest = pl.program_id(0)
        row = iota((BW, RW), 0)
        col = iota((BW, RW), 1)
        for b in range(blocks):
            block = dest * blocks + b
            inside = col < ri_ref[block]
            for a in range(atoms):
                limit = jnp.where(mask_ref[a, block] > 0, count_ref[a], 0)
                at = (pl.ds(a * BW, BW), pl.ds(b * RW, RW))
                x = x_ref[at].astype(F32)
                o_ref[(0,) + at] = jnp.where(inside & (row < limit), x, 0.0).astype(BF16)

    return pl.pallas_call(
        body,
        out_shape=jax.ShapeDtypeStruct((ncols, rows, wide), BF16),
        grid=(ncols,),
        in_specs=[SMEM_SPEC, SMEM_SPEC, SMEM_SPEC, pl.BlockSpec((rows, wide), lambda i: (0, i))],
        out_specs=pl.BlockSpec((1, rows, wide), lambda i: (i, 0, 0)),
        compiler_params=params(),
        name="screen_integrals",
    )(own_count, ri_count, block_mask, tc)


def screen_density(dens, lam_count, sum_count, mask):
    rows, cols = dens.shape

    def body(lam_ref, sum_ref, mask_ref, x_ref, o_ref):
        keep = keep_mask(lam_ref[...], sum_ref[...], mask_ref[...], rows, cols)
        o_ref[...] = jnp.where(keep > 0.5, x_ref[...].astype(F32), 0.0).astype(BF16)

    return pl.pallas_call(
        body,
        out_shape=jax.ShapeDtypeStruct((rows, cols), BF16),
        compiler_params=params(),
        name="screen_density",
    )(lam_count.reshape(1, -1), sum_count.reshape(-1, 1), mask, dens)


def contract_dense(dens, integrals):
    parts, rows, depth = dens.shape
    cols = integrals.shape[2]

    def body(d_ref, s_ref, o_ref, total):
        step = pl.program_id(0)
        part = jnp.dot(d_ref[0], s_ref[0], preferred_element_type=F32)

        @pl.when(step == 0)
        def _():
            total[...] = part

        @pl.when(step > 0)
        def _():
            total[...] += part

        @pl.when(step == parts - 1)
        def _():
            o_ref[...] = total[...].astype(BF16)

    return pl.pallas_call(
        body,
        out_shape=jax.ShapeDtypeStruct((rows, cols), BF16),
        grid=(parts,),
        in_specs=[
            pl.BlockSpec((1, rows, depth), lambda i: (i, 0, 0)),
            pl.BlockSpec((1, depth, cols), lambda i: (i, 0, 0)),
        ],
        out_specs=pl.BlockSpec((rows, cols), lambda i: (0, 0)),
        scratch_shapes=[pltpu.VMEM((rows, cols), F32)],
        compiler_params=params(),
        name="contract_dense",
    )(dens, integrals)


def dense(three_center, density, block_mask, density_mask, basis_count, ri_count):
    ncols = lax.axis_size("col")
    row = lax.axis_index("row")
    col = lax.axis_index("col")
    atoms = block_mask.shape[0]
    lam_atoms, sum_atoms = density_mask.shape
    own_count = lax.dynamic_slice_in_dim(basis_count, (row * ncols + col) * atoms, atoms)
    lam_count = lax.dynamic_slice_in_dim(basis_count, row * lam_atoms, lam_atoms)
    sum_count = lax.dynamic_slice_in_dim(basis_count, col * sum_atoms, sum_atoms)
    dens = screen_density(density, lam_count, sum_count, density_mask)
    screened = screen_integrals(three_center, own_count, ri_count, block_mask, ncols)
    dens_all = lax.all_gather(dens, "col")
    blocks = lax.all_to_all(screened, "col", split_axis=0, concat_axis=0, tiled=True)
    rows_all = lax.all_gather(blocks, "row")
    wide = blocks.shape[2]
    return contract_dense(dens_all, rows_all.reshape(ncols, -1, wide))


def pack_integrals(tc, block_mask, basis_count, ri_count, ncols, packed):
    rows, cols = tc.shape
    atoms = rows // BW
    wide = cols // ncols
    blocks = wide // RW
    chips = ncols // CORES

    def body(count_ref, ri_ref, mask_ref, x_ref, *refs):
        outs, held, hot = refs[:ncols], refs[ncols], refs[ncols + 1]
        row, col = lax.axis_index("row"), lax.axis_index("col")
        base = (row * ncols + col) * atoms
        slot = iota((BW, RW), 0)
        for n in range(ncols):
            up, other = n // CORES, n % CORES
            chip = lax.rem(col // CORES + up, chips)
            core = lax.rem(col + other, CORES)
            dest = chip * CORES + core
            for b in range(blocks):
                for a in range(atoms):
                    limit = jnp.where(mask_ref[a, dest * blocks + b] > 0, count_ref[base + a], 0)
                    lanes = pl.multiple_of(dest * wide + b * RW, RW)
                    x = x_ref[pl.ds(a * BW, BW), pl.ds(lanes, RW)].astype(F32)
                    held[pl.ds(a * BW, BW), pl.ds(b * RW, RW)] = jnp.where(slot < limit, x, 0.0).astype(BF16)
            pack_cols(ri_ref, dest * blocks, blocks, RW, packed, hot)
            outs[n][...] = jnp.dot(held[...], hot[...], preferred_element_type=F32).astype(BF16)

    return pl.pallas_call(
        body,
        out_shape=[jax.ShapeDtypeStruct((rows, packed), BF16)] * ncols,
        in_specs=[SMEM_SPEC, SMEM_SPEC, SMEM_SPEC, VMEM_SPEC],
        out_specs=[VMEM_SPEC] * ncols,
        scratch_shapes=[pltpu.VMEM((rows, wide), BF16), pltpu.VMEM((wide, packed), BF16)],
        compiler_params=params(),
        name="pack_integrals",
    )(basis_count, ri_count, block_mask, tc)


def pack_density(dens, mask, basis_count, lam_size, sum_size):
    rows, cols = dens.shape
    lam_atoms, sum_atoms = mask.shape

    def body(count_ref, mask_ref, x_ref, o_ref, hot):
        row, col = lax.axis_index("row"), lax.axis_index("col")
        keep = keep_mask(BW, BW, mask_ref[...], rows, cols)
        x = jnp.where(keep > 0.5, x_ref[...].astype(F32), 0.0).astype(BF16)
        left = pack_rows(count_ref, col * sum_atoms, sum_atoms, BW, sum_size)
        x = lax.dot_general(left, x, (((1,), (1,)), ((), ())), preferred_element_type=F32).astype(BF16)
        pack_cols(count_ref, row * lam_atoms, lam_atoms, BW, lam_size, hot)
        o_ref[...] = jnp.dot(x, hot[...], preferred_element_type=F32).astype(BF16)

    return pl.pallas_call(
        body,
        out_shape=jax.ShapeDtypeStruct((sum_size, lam_size), BF16),
        in_specs=[SMEM_SPEC, VMEM_SPEC, VMEM_SPEC],
        out_specs=VMEM_SPEC,
        scratch_shapes=[pltpu.VMEM((rows, lam_size), BF16)],
        compiler_params=params(),
        name="pack_density",
    )(basis_count, mask, dens)


def exchange(pieces, ncols):
    chips = ncols // CORES

    def dest(col, n):
        return (col // CORES + n // CORES) % chips * CORES + (col + n) % CORES

    got = [pieces[0]]
    for n in range(1, ncols):
        got.append(lax.ppermute(pieces[n], "col", [(c, dest(c, n)) for c in range(ncols)]))
    return got


def double(own, bits):
    nrows = lax.axis_size("row")
    have = {0: own}
    for bit in bits:
        for far in sorted(have):
            have[far | bit] = lax.ppermute(have[far], "row", [(r, r ^ bit) for r in range(nrows)])
    return have


def pack_sums(groups, basis_count, ncols, rows, depth, size):
    nrows = len(groups[0])
    cols = groups[0][0].shape[1]
    per = ncols // len(groups)
    parts = nrows * ncols * rows // depth
    atoms = depth // BW
    order = [(far, g) for far in range(nrows) for g in range(len(groups))]

    def body(count_ref, *refs):
        blocks = refs[: len(order)]
        o_ref, full, sem = refs[len(order):]
        row, col = lax.axis_index("row"), lax.axis_index("col")
        copies = []
        for i, (far, g) in enumerate(order):
            for j in range(per):
                n = g * per + j
                chips = ncols // CORES
                chip = lax.rem(col // CORES - n // CORES + chips, chips)
                core = lax.rem(col + n, CORES)
                start = ((row ^ far) * ncols + chip * CORES + core) * rows
                copies.append(
                    pltpu.make_async_copy(
                        blocks[i].at[pl.ds(j * rows, rows), :],
                        full.at[pl.ds(pl.multiple_of(start, rows), rows), :],
                        sem.at[i * per + j],
                    )
                )
        for copy in copies:
            copy.start()
        for copy in copies:
            copy.wait()
        for part in range(parts):
            hot = pack_rows(count_ref, part * atoms, atoms, BW, size)
            x = full[pl.ds(part * depth, depth), :]
            o_ref[part] = jnp.dot(hot, x, preferred_element_type=F32).astype(BF16)

    return pl.pallas_call(
        body,
        out_shape=jax.ShapeDtypeStruct((parts, size, cols), BF16),
        in_specs=[SMEM_SPEC] + [ANY_SPEC] * len(order),
        out_specs=VMEM_SPEC,
        scratch_shapes=[
            pltpu.VMEM((parts * depth, cols), BF16),
            pltpu.SemaphoreType.DMA((len(order) * per,)),
        ],
        compiler_params=params(),
        name="pack_sums",
    )(basis_count, *[groups[g][far] for far, g in order])


def contract(dens, integrals, basis_count, ri_count, rows, wide):
    parts, depth, lam = dens.shape
    cols = integrals.shape[2]
    lam_atoms, blocks = rows // BW, wide // RW

    def body(count_ref, ri_ref, d_ref, s_ref, o_ref, total, lam_hot, col_hot):
        step = pl.program_id(0)
        part = lax.dot_general(d_ref[0], s_ref[0], (((0,), (0,)), ((), ())), preferred_element_type=F32)

        @pl.when(step == 0)
        def _():
            total[...] = part
            row, col = lax.axis_index("row"), lax.axis_index("col")
            pack_cols(count_ref, row * lam_atoms, lam_atoms, BW, lam, lam_hot)
            col_hot[...] = pack_rows(ri_ref, col * blocks, blocks, RW, cols)

        @pl.when(step > 0)
        def _():
            total[...] += part

        @pl.when(step == parts - 1)
        def _():
            x = jnp.dot(total[...].astype(BF16), col_hot[...], preferred_element_type=F32).astype(BF16)
            o_ref[...] = jnp.dot(lam_hot[...], x, preferred_element_type=F32).astype(BF16)

    return pl.pallas_call(
        body,
        out_shape=jax.ShapeDtypeStruct((rows, wide), BF16),
        grid=(parts,),
        in_specs=[
            SMEM_SPEC,
            SMEM_SPEC,
            pl.BlockSpec((1, depth, lam), lambda i: (i, 0, 0)),
            pl.BlockSpec((1, depth, cols), lambda i: (i, 0, 0)),
        ],
        out_specs=pl.BlockSpec((rows, wide), lambda i: (0, 0)),
        scratch_shapes=[
            pltpu.VMEM((lam, cols), F32),
            pltpu.VMEM((rows, lam), BF16),
            pltpu.VMEM((cols, wide), BF16),
        ],
        compiler_params=params(),
        name="contract",
    )(basis_count, ri_count, dens, integrals)


def sizes(density, three_center, ncols):
    rows, depth = density.shape
    wide = three_center.shape[1] // ncols
    return rows * 3 // 4, depth * 13 // 16, wide * 5 // 6


def compact(three_center, density, block_mask, density_mask, basis_count, ri_count):
    ncols = lax.axis_size("col")
    nrows = lax.axis_size("row")
    rows, depth = density.shape
    lam_size, sum_size, col_size = sizes(density, three_center, ncols)
    pieces = pack_integrals(three_center, block_mask, basis_count, ri_count, ncols, col_size)
    dens = pack_density(density, density_mask, basis_count, lam_size, sum_size)
    dens_all = lax.all_gather(dens, "col")
    got = exchange(pieces, ncols)
    half = ncols // 2
    bits = [1 << b for b in range(nrows.bit_length() - 1)]
    groups = [
        double(jnp.concatenate(got[:half], axis=0), bits),
        double(jnp.concatenate(got[half:], axis=0), bits[::-1]),
    ]
    packed = pack_sums(groups, basis_count, ncols, three_center.shape[0], depth, sum_size)
    return contract(dens_all, packed, basis_count, ri_count, rows, three_center.shape[1] // ncols)


def shards(three_center, density, block_mask, density_mask, basis_count, ri_count):
    ncols = lax.axis_size("col")
    nrows = lax.axis_size("row")
    lam_size, sum_size, col_size = sizes(density, three_center, ncols)
    fits = (
        (basis_count.reshape(nrows, -1).sum(axis=1).max() <= lam_size)
        & (basis_count.reshape(ncols, -1).sum(axis=1).max() <= sum_size)
        & (ri_count.reshape(ncols, -1).sum(axis=1).max() <= col_size)
    )
    args = (three_center, density, block_mask, density_mask, basis_count, ri_count)
    return lax.cond(fits, compact, dense, *args)


def solution(mesh):
    in_specs = (
        P(("row", "col"), None),
        P("row", "col"),
        P(("row", "col"), None),
        P("row", "col"),
        P(),
        P(),
    )
    return jax.shard_map(
        shards, mesh=mesh, in_specs=in_specs, out_specs=P("row", "col"), check_vma=False
    )
```

time: 229 us -> 167 us (0.73)
  the two profiles are of different devices: /device:TPU:0 before, /device:TPU:10 now
where the time goes in v2:
time: 167 us; the launch traced here: 166 us
  waiting for transfers between devices  95 us (57%)
  Pallas kernels  33.9 us (20%)
  between operations  15.4 us (9%)
  starting transfers between devices  12.9 us (8%)
  local copies, waits for them, and re-layouts  6.6 us (4%)
  other arithmetic  2.27 us (1%)
    ppermute x7, waiting for transfers between devices, exchange(): lax.ppermute(pieces[n], 'col', [(c, dest(c, n)) for c in range(ncols)])  54.7 us
    ppermute x6, waiting for transfers between devices, double(): lax.ppermute(have[far], 'row', [(r, r ^ bit) for r in range(nrows)])  40.2 us
    pallas_call x1, Pallas kernels, pack_sums(): pl.pallas_call(body, out_shape=jax.ShapeDtypeStruct((parts, size, cols),...  13.8 us
    pallas_call x1, Pallas kernels, contract(): pl.pallas_call(body, out_shape=jax.ShapeDtypeStruct((rows, wide), BF16),...  12.5 us
    ppermute x7, starting transfers between devices, exchange(): lax.ppermute(pieces[n], 'col', [(c, dest(c, n)) for c in range(ncols)])  7.46 us
    ppermute x6, starting transfers between devices, double(): lax.ppermute(have[far], 'row', [(r, r ^ bit) for r in range(nrows)])  5.37 us
    pallas_call x1, Pallas kernels, pack_density(): pl.pallas_call(body, out_shape=jax.ShapeDtypeStruct((sum_size, lam_size),...  3.9 us
    pallas_call x1, Pallas kernels, pack_integrals(): pl.pallas_call(body, out_shape=[jax.ShapeDtypeStruct((rows, packed), BF16...  3.72 us
  transfers between devices with their start and end apart: 14, of which 8 were waited for; matrix products, arithmetic and copies ran while one was open for 0% of the time, Pallas kernels for 11%

profile of v2, /device:TPU:10, one launch (start us, length us, event | category | flops | bytes accessed | tf_op | source)
XLA Modules:
  0.0 166.5 jit_solution(17365678652741857034)
XLA Ops:
  6.5 0.7 reshape.18
  13.0 145.5 %conditional.1 = (bf16[1024,768]{1,0:T(8,128)(2,1)S(1)}) conditional(s32[]{:T(128)} %convert_element_type.3, (s32[128]{0:T(128)}, s32[32,16]{0,1:T(8,128)}, bf16[1024,512]{1,0:T(8,128)(2,1)}, s32[48]{0:T(128)}, s32[4,48]{1,0:T(4,128)}, /*index=5*/bf16[128,6144]{1,0:T(8,128)(2,1)}) %tuple.11, (s32[128]{0:T(128)}, s32[32,16]{0,1:T(8,128)}, ...), branch_computations={%region_6.0_spmd, %region_7.0_spmd} | conditional | flops 19 | bytes 63531460 | solution.py:382
  13.1 0.9 copy.14.mask_ref
  14.0 3.9 %pack_density.1 = bf16[416,768]{1,0:T(8,128)(2,1)} custom-call(s32[128]{0:T(128)} %get-tuple-element.38.count_ref, s32[32,16]{1,0:T(8,128)S(1)} %copy.14.mask_ref, bf16[1024,512]{1,0:T(8,128)(2,1)} %get-tuple-element.41.x_ref), custom_call_target="tpu_custom_call" | custom-call | tf_op jit(solution)/shard_map/cond/branch_1_fun/pack_density/pallas_call | solution.py:219
  17.9 3.7 %pack_integrals.1 = (bf16[128,640]{1,0:T(8,128)(2,1)S(1)}, bf16[128,640]{1,0:T(8,128)(2,1)S(1)}, bf16[128,640]{1,0:T(8,128)(2,1)S(1)}, bf16[128,640]{1,0:T(8,128...) custom-call(s32[128]{0:T(128)S(1)} %copy-done.6, ...), custom_call_target="tpu_custom_call" | custom-call | tf_op jit(solution)/shard_map/cond/branch_1_fun/pack_integrals/pallas_call | solution.py:195
  21.7 1.6 collective-permute-start.1
  23.4 1.4 collective-permute-start.2
  24.7 1.2 collective-permute-start.3
  26.0 1.4 collective-permute-start.4
  27.9 0.9 collective-permute-done.1
  28.8 1.3 collective-permute-start.6
  30.2 10.8 %collective-permute-done.2 = bf16[128,640]{1,0:T(8,128)(2,1)S(1)} collective-permute-done((bf16[128,640]{1,0:T(8,128)(2,1)S(1)}, bf16[128,640]{1,0:T(8,128)(2,1)S(1)}, u32[]{:S(2)}, u32[]{:S(2)}) %collective-permute-start.2) | collective-permute-done | bytes 163872 | tf_op jit(solution)/shard_map/cond/branch_1_fun/ppermute | solution.py:238
  41.7 24.0 %collective-permute-done.3 = bf16[128,640]{1,0:T(8,128)(2,1)S(1)} collective-permute-done((bf16[128,640]{1,0:T(8,128)(2,1)S(1)}, bf16[128,640]{1,0:T(8,128)(2,1)S(1)}, u32[]{:S(2)}, u32[]{:S(2)}) %collective-permute-start.3) | collective-permute-done | bytes 163872 | tf_op jit(solution)/shard_map/cond/branch_1_fun/ppermute | solution.py:238
  65.7 13.9 %collective-permute-done.4 = bf16[128,640]{1,0:T(8,128)(2,1)S(1)} collective-permute-done((bf16[128,640]{1,0:T(8,128)(2,1)S(1)}, bf16[128,640]{1,0:T(8,128)(2,1)S(1)}, u32[]{:S(2)}, u32[]{:S(2)}) %collective-permute-start.4) | collective-permute-done | bytes 163872 | tf_op jit(solution)/shard_map/cond/branch_1_fun/ppermute | solution.py:238
  79.6 5.2 %collective-permute-done.6 = bf16[128,640]{1,0:T(8,128)(2,1)S(1)} collective-permute-done((bf16[128,640]{1,0:T(8,128)(2,1)S(1)}, bf16[128,640]{1,0:T(8,128)(2,1)S(1)}, u32[]{:S(2)}, u32[]{:S(2)}) %collective-permute-start.6) | collective-permute-done | bytes 163872 | tf_op jit(solution)/shard_map/cond/branch_1_fun/ppermute | solution.py:238
  84.8 1.6 collective-permute-start.10
  87.4 1.5 collective-permute-start.11
  88.9 13.5 %collective-permute-done.10.refs_5_ = bf16[512,640]{1,0:T(8,128)(2,1)S(1)} collective-permute-done((bf16[512,640]{1,0:T(8,128)(2,1)S(1)}, bf16[512,640]{1,0:T(8,128)(2,1)S(1)}, u32[]{:S(2)}, u32[]{:S(2)}) %collective-permute-start.10) | collective-permute-done | bytes 655392 | tf_op jit(solution)/shard_map/cond/branch_1_fun/ppermute | solution.py:247
  103.0 13.5 %collective-permute-done.9.refs_4_ = bf16[512,640]{1,0:T(8,128)(2,1)S(1)} collective-permute-done((bf16[512,640]{1,0:T(8,128)(2,1)S(1)}, bf16[512,640]{1,0:T(8,128)(2,1)S(1)}, u32[]{:S(2)}, u32[]{:S(2)}) %collective-permute-start.9) | collective-permute-done | bytes 655392 | tf_op jit(solution)/shard_map/cond/branch_1_fun/ppermute | solution.py:247
  116.5 13.2 %collective-permute-done.11.refs_6_ = bf16[512,640]{1,0:T(8,128)(2,1)S(1)} collective-permute-done((bf16[512,640]{1,0:T(8,128)(2,1)S(1)}, bf16[512,640]{1,0:T(8,128)(2,1)S(1)}, u32[]{:S(2)}, u32[]{:S(2)}) %collective-permute-start.11) | collective-permute-done | bytes 655392 | tf_op jit(solution)/shard_map/cond/branch_1_fun/ppermute | solution.py:247
  129.7 13.8 %pack_sums.1.s_ref = bf16[8,416,640]{2,1,0:T(8,128)(2,1)} custom-call(s32[128]{0:T(128)S(1)} %copy-done.6, bf16[512,640]{1,0:T(8,128)(2,1)S(1)} %constant_dynamic-update-slice_fusion.refs_0_, bf16[512,640]{1,0:T(8,128)(2,1)S(1)} %constant_dynamic-update-slice_fusion.4.refs_1_, bf16[512,640]{1,0:T(8,128)(2,1)S(1)} %collective-permute-done.7.refs_2_, ...), custom_call_target="tpu_custom_call" | custom-call | tf_op jit(solution)/shard_map/cond/branch_1_fun/pack_sums/pallas_call | solution.py:287
  143.6 2.2 %copy-done = bf16[8,416,640]{2,1,0:T(8,128)(2,1)S(1)} copy-done((bf16[8,416,640]{2,1,0:T(8,128)(2,1)S(1)}, bf16[8,416,640]{2,1,0:T(8,128)(2,1)}, u32[]{:S(2)}) %copy-start) | copy-done | bytes 4259864 | tf_op jit(solution)/shard_map/cond
  145.8 12.5 %contract.1 = bf16[1024,768]{1,0:T(8,128)(2,1)S(1)} custom-call(s32[128]{0:T(128)S(1)} %copy-done.6, s32[48]{0:T(128)S(1)} %copy-done.8, bf16[8,416,768]{2,1,0:T(8,128)(2,1)} %bitcast.9, bf16[8,416,640]{2,1,0:T(8,128)(2,1)S(1)} %copy-done), custom_call_target="tpu_custom_call" | custom-call | tf_op jit(solution)/shard_map/cond/branch_1_fun/contract/pallas_call | solution.py:326
  158.5 1.1 copy-done.3
  (40 shorter events, 6.8 us)
Async XLA Ops:
  13.0 4.9 %copy-start.1 = (bf16[128,6144]{1,0:T(8,128)(2,1)S(1)}, bf16[128,6144]{1,0:T(8,128)(2,1)}, u32[]{:S(2)}) copy-start(bf16[128,6144]{1,0:T(8,128)(2,1)} %get-tuple-element.43.x_ref) | copy-start | bytes 4718596 | tf_op jit(solution)/shard_map/cond
  13.0 4.9 %copy-start.6 = (s32[128]{0:T(128)S(1)}, s32[128]{0:T(128)}, u32[]{:S(2)}) copy-start(s32[128]{0:T(128)} %get-tuple-element.38.count_ref) | copy-start | bytes 1540 | tf_op jit(solution)/shard_map/cond
  13.0 4.9 %copy-start.7 = (s32[4,48]{1,0:T(4,128)S(1)}, s32[4,48]{1,0:T(4,128)}, u32[]{:S(2)}) copy-start(s32[4,48]{1,0:T(4,128)} %get-tuple-element.42.mask_ref) | copy-start | bytes 2308 | tf_op jit(solution)/shard_map/cond
  13.0 4.9 %copy-start.8 = (s32[48]{0:T(128)S(1)}, s32[48]{0:T(128)}, u32[]{:S(2)}) copy-start(s32[48]{0:T(128)} %get-tuple-element.39.ri_ref) | copy-start | bytes 580 | tf_op jit(solution)/shard_map/cond
  13.1 130.5 %all-gather.11.cloned.1.call-start = ((), (), s32[]{:S(2)}) async-start(), calls=%async_computation.3 | async-start | bytes 5750784 | tf_op jit(solution)/shard_map/cond/branch_1_fun/all_gather | solution.py:360
  21.7 5.7 %collective-permute-start = (bf16[128,640]{1,0:T(8,128)(2,1)S(1)}, bf16[128,640]{1,0:T(8,128)(2,1)S(1)}, u32[]{:S(2)}, u32[]{:S(2)}) collective-permute-start(bf16[128,640]{1,0:T(8,128)(2,1)S(1)} %get-tuple-element.45), channel_id=1, source_target_pairs={{0,1},{1,0},{2,3},{3,2},{4,5},{5,4},{6,7},{7,6},{8,9},{9,8},{10,11... | collective-permute-start | bytes 491528 | tf_op jit(solution)/shard_map/cond/branch_1_fun/ppermute | solution.py:238
  21.7 7.1 %collective-permute-start.1 = (bf16[128,640]{1,0:T(8,128)(2,1)S(1)}, bf16[128,640]{1,0:T(8,128)(2,1)S(1)}, u32[]{:S(2)}, u32[]{:S(2)}) collective-permute-start(bf16[128,640]{1,0:T(8,128)(2,1)S(1)} %get-tuple-element.46), channel_id=1, source_target_pairs={{0,2},{1,3},{2,4},{3,5},{4,6},{5,7},{6,0},{7,1},{8,10},{9,11},{10,... | collective-permute-start | bytes 491528 | tf_op jit(solution)/shard_map/cond/branch_1_fun/ppermute | solution.py:238
  23.4 17.6 %collective-permute-start.2 = (bf16[128,640]{1,0:T(8,128)(2,1)S(1)}, bf16[128,640]{1,0:T(8,128)(2,1)S(1)}, u32[]{:S(2)}, u32[]{:S(2)}) collective-permute-start(bf16[128,640]{1,0:T(8,128)(2,1)S(1)} %get-tuple-element.47), channel_id=1, source_target_pairs={{0,3},{1,2},{2,5},{3,4},{4,7},{5,6},{6,1},{7,0},{8,11},{9,10},{10,... | collective-permute-start | bytes 491528 | tf_op jit(solution)/shard_map/cond/branch_1_fun/ppermute | solution.py:238
  24.7 40.9 %collective-permute-start.3 = (bf16[128,640]{1,0:T(8,128)(2,1)S(1)}, bf16[128,640]{1,0:T(8,128)(2,1)S(1)}, u32[]{:S(2)}, u32[]{:S(2)}) collective-permute-start(bf16[128,640]{1,0:T(8,128)(2,1)S(1)} %get-tuple-element.48), channel_id=1, source_target_pairs={{0,4},{1,5},{2,6},{3,7},{4,0},{5,1},{6,2},{7,3},{8,12},{9,13},{10,... | collective-permute-start | bytes 491528 | tf_op jit(solution)/shard_map/cond/branch_1_fun/ppermute | solution.py:238
  26.0 53.6 %collective-permute-start.4 = (bf16[128,640]{1,0:T(8,128)(2,1)S(1)}, bf16[128,640]{1,0:T(8,128)(2,1)S(1)}, u32[]{:S(2)}, u32[]{:S(2)}) collective-permute-start(bf16[128,640]{1,0:T(8,128)(2,1)S(1)} %get-tuple-element.49), channel_id=1, source_target_pairs={{0,5},{1,4},{2,7},{3,6},{4,1},{5,0},{6,3},{7,2},{8,13},{9,12},{10,... | collective-permute-start | bytes 491528 | tf_op jit(solution)/shard_map/cond/branch_1_fun/ppermute | solution.py:238
  27.3 52.2 %collective-permute-start.5 = (bf16[128,640]{1,0:T(8,128)(2,1)S(1)}, bf16[128,640]{1,0:T(8,128)(2,1)S(1)}, u32[]{:S(2)}, u32[]{:S(2)}) collective-permute-start(bf16[128,640]{1,0:T(8,128)(2,1)S(1)} %get-tuple-element.50), channel_id=1, source_target_pairs={{0,6},{1,7},{2,0},{3,1},{4,2},{5,3},{6,4},{7,5},{8,14},{9,15},{10,... | collective-permute-start | bytes 491528 | tf_op jit(solution)/shard_map/cond/branch_1_fun/ppermute | solution.py:238
  28.8 56.0 %collective-permute-start.6 = (bf16[128,640]{1,0:T(8,128)(2,1)S(1)}, bf16[128,640]{1,0:T(8,128)(2,1)S(1)}, u32[]{:S(2)}, u32[]{:S(2)}) collective-permute-start(bf16[128,640]{1,0:T(8,128)(2,1)S(1)} %get-tuple-element.51), channel_id=1, source_target_pairs={{0,7},{1,6},{2,1},{3,0},{4,3},{5,2},{6,5},{7,4},{8,15},{9,14},{10,... | collective-permute-start | bytes 491528 | tf_op jit(solution)/shard_map/cond/branch_1_fun/ppermute | solution.py:238
  41.0 46.4 %collective-permute-start.7 = (bf16[512,640]{1,0:T(8,128)(2,1)S(1)}, bf16[512,640]{1,0:T(8,128)(2,1)S(1)}, u32[]{:S(2)}, u32[]{:S(2)}) collective-permute-start(bf16[512,640]{1,0:T(8,128)(2,1)S(1)} %constant_dynamic-update-slice_fusion.refs_0_), channel_id=1, source_target_pairs={{0,8},{8,0},{16,24},{24,16},{1,9},{9,1},{17,25},{25,17},{2,10},{10... | collective-permute-start | bytes 1966088 | tf_op jit(solution)/shard_map/cond/branch_1_fun/ppermute | solution.py:247
  84.8 17.6 %collective-permute-start.10 = (bf16[512,640]{1,0:T(8,128)(2,1)S(1)}, bf16[512,640]{1,0:T(8,128)(2,1)S(1)}, u32[]{:S(2)}, u32[]{:S(2)}) collective-permute-start(bf16[512,640]{1,0:T(8,128)(2,1)S(1)} %constant_dynamic-update-slice_fusion.4.refs_1_), channel_id=1, source_target_pairs={{0,16},{8,24},{16,0},{24,8},{1,17},{9,25},{17,1},{25,9},{2,18},{10... | collective-permute-start | bytes 1966088 | tf_op jit(solution)/shard_map/cond/branch_1_fun/ppermute | solution.py:247
  86.4 30.1 %collective-permute-start.9 = (bf16[512,640]{1,0:T(8,128)(2,1)S(1)}, bf16[512,640]{1,0:T(8,128)(2,1)S(1)}, u32[]{:S(2)}, u32[]{:S(2)}) collective-permute-start(bf16[512,640]{1,0:T(8,128)(2,1)S(1)} %constant_dynamic-update-slice_fusion.refs_0_), channel_id=1, source_target_pairs={{0,16},{8,24},{16,0},{24,8},{1,17},{9,25},{17,1},{25,9},{2,18},{10... | collective-permute-start | bytes 1966088 | tf_op jit(solution)/shard_map/cond/branch_1_fun/ppermute | solution.py:247
  86.9 29.6 %collective-permute-start.8 = (bf16[512,640]{1,0:T(8,128)(2,1)S(1)}, bf16[512,640]{1,0:T(8,128)(2,1)S(1)}, u32[]{:S(2)}, u32[]{:S(2)}) collective-permute-start(bf16[512,640]{1,0:T(8,128)(2,1)S(1)} %constant_dynamic-update-slice_fusion.4.refs_1_), channel_id=1, source_target_pairs={{0,8},{8,0},{16,24},{24,16},{1,9},{9,1},{17,25},{25,17},{2,10},{10... | collective-permute-start | bytes 1966088 | tf_op jit(solution)/shard_map/cond/branch_1_fun/ppermute | solution.py:247
  87.4 42.3 %collective-permute-start.11 = (bf16[512,640]{1,0:T(8,128)(2,1)S(1)}, bf16[512,640]{1,0:T(8,128)(2,1)S(1)}, u32[]{:S(2)}, u32[]{:S(2)}) collective-permute-start(bf16[512,640]{1,0:T(8,128)(2,1)S(1)} %collective-permute-done.7.refs_2_), channel_id=1, source_target_pairs={{0,16},{8,24},{16,0},{24,8},{1,17},{9,25},{17,1},{25,9},{2,18},{10... | collective-permute-start | bytes 1966088 | tf_op jit(solution)/shard_map/cond/branch_1_fun/ppermute | solution.py:247
  102.4 27.3 %collective-permute-start.12 = (bf16[512,640]{1,0:T(8,128)(2,1)S(1)}, bf16[512,640]{1,0:T(8,128)(2,1)S(1)}, u32[]{:S(2)}, u32[]{:S(2)}) collective-permute-start(bf16[512,640]{1,0:T(8,128)(2,1)S(1)} %collective-permute-done.10.refs_5_), channel_id=1, source_target_pairs={{0,8},{8,0},{16,24},{24,16},{1,9},{9,1},{17,25},{25,17},{2,10},{10... | collective-permute-start | bytes 1966088 | tf_op jit(solution)/shard_map/cond/branch_1_fun/ppermute | solution.py:247
  143.6 2.2 %copy-start = (bf16[8,416,640]{2,1,0:T(8,128)(2,1)S(1)}, bf16[8,416,640]{2,1,0:T(8,128)(2,1)}, u32[]{:S(2)}) copy-start(bf16[8,416,640]{2,1,0:T(8,128)(2,1)} %pack_sums.1.s_ref) | copy-start | bytes 12779524 | tf_op jit(solution)/shard_map/cond
  158.5 1.1 copy-start.3
Sparse Core Ops, SparseCore 0:
  18.0 76.8 all-gather.10

commit v3 on v0

v3 whole, which is shorter than its diff:
```python
import jax
import jax.numpy as jnp
from jax import lax
from jax.experimental import pallas as pl
from jax.experimental.pallas import tpu as pltpu
from jax.sharding import PartitionSpec as P

BW = 32
RW = 128
CORES = 2
VMEM = 48 * 1024 * 1024
BF16 = jnp.bfloat16
F32 = jnp.float32
SMEM_SPEC = pl.BlockSpec(memory_space=pltpu.SMEM)
VMEM_SPEC = pl.BlockSpec(memory_space=pltpu.VMEM)
ANY_SPEC = pl.BlockSpec(memory_space=pl.ANY)


def params():
    return pltpu.CompilerParams(vmem_limit_bytes=VMEM)


def cost(flops, bytes_accessed):
    return pl.CostEstimate(flops=flops, bytes_accessed=bytes_accessed, transcendentals=0)


def ones_where(cond):
    return jnp.where(cond, 1.0, 0.0).astype(BF16)


def iota(shape, axis):
    return lax.broadcasted_iota(jnp.int32, shape, axis)


def place_row(count_ref, base, atoms, width):
    lane = iota((1, atoms * width), 1)
    place = jnp.full(lane.shape, -1, jnp.int32)
    offset = jnp.int32(0)
    for a in range(atoms):
        count = count_ref[base + a]
        inside = (lane >= a * width) & (lane < a * width + count)
        place = jnp.where(inside, lane - a * width + offset, place)
        offset = offset + count
    return place


def pack_rows(count_ref, base, atoms, width, size):
    place = place_row(count_ref, base, atoms, width)
    return ones_where(iota((size, atoms * width), 0) == place)


def pack_cols(count_ref, base, atoms, width, size, out):
    gap = iota((width, size), 1) - iota((width, size), 0)
    slot = iota((width, size), 0)
    offset = jnp.int32(0)
    for a in range(atoms):
        count = count_ref[base + a]
        out[pl.ds(a * width, width), :] = ones_where((gap == offset) & (slot < count))
        offset = offset + count


def keep_mask(lam_count, sum_count, mask, rows, cols):
    def member(atoms, size, count, axis):
        shape = (size, atoms) if axis == 0 else (atoms, size)
        first = iota(shape, 1 - axis) * BW
        at = iota(shape, axis)
        return ones_where((at >= first) & (at < first + count))

    left = member(mask.shape[0], rows, lam_count, 0)
    right = member(mask.shape[1], cols, sum_count, 1)
    keep = jnp.dot(left, ones_where(mask > 0), preferred_element_type=F32).astype(BF16)
    return jnp.dot(keep, right, preferred_element_type=F32)


def pack_integrals(tc, block_mask, basis_count, ri_count, ncols, packed):
    rows, cols = tc.shape
    atoms = rows // BW
    wide = cols // ncols
    blocks = wide // RW

    def body(count_ref, ri_ref, mask_ref, x_ref, *refs):
        outs, held, hot = refs[:ncols], refs[ncols], refs[ncols + 1]
        row, col = lax.axis_index("row"), lax.axis_index("col")
        base = (row * ncols + col) * atoms
        slot = iota((BW, RW), 0)
        for n in range(ncols):
            dest = col ^ n
            for b in range(blocks):
                for a in range(atoms):
                    limit = jnp.where(mask_ref[a, dest * blocks + b] > 0, count_ref[base + a], 0)
                    lanes = pl.multiple_of(dest * wide + b * RW, RW)
                    x = x_ref[pl.ds(a * BW, BW), pl.ds(lanes, RW)].astype(F32)
                    held[pl.ds(a * BW, BW), pl.ds(b * RW, RW)] = jnp.where(slot < limit, x, 0.0).astype(BF16)
            pack_cols(ri_ref, dest * blocks, blocks, RW, packed, hot)
            outs[n][...] = jnp.dot(held[...], hot[...], preferred_element_type=F32).astype(BF16)

    return pl.pallas_call(
        body,
        out_shape=[jax.ShapeDtypeStruct((rows, packed), BF16)] * ncols,
        in_specs=[SMEM_SPEC, SMEM_SPEC, SMEM_SPEC, VMEM_SPEC],
        out_specs=[VMEM_SPEC] * ncols,
        scratch_shapes=[pltpu.VMEM((rows, wide), BF16), pltpu.VMEM((wide, packed), BF16)],
        compiler_params=params(),
        cost_estimate=cost(2 * rows * cols * packed, 2 * rows * (cols + ncols * packed)),
        name="pack_integrals",
    )(basis_count, ri_count, block_mask, tc)


def pack_density(dens, mask, basis_count, lam_size, sum_size):
    rows, cols = dens.shape
    lam_atoms, sum_atoms = mask.shape

    def body(count_ref, mask_ref, x_ref, o_ref, hot):
        row, col = lax.axis_index("row"), lax.axis_index("col")
        keep = keep_mask(BW, BW, mask_ref[...], rows, cols)
        x = jnp.where(keep > 0.5, x_ref[...].astype(F32), 0.0).astype(BF16)
        left = pack_rows(count_ref, col * sum_atoms, sum_atoms, BW, sum_size)
        x = lax.dot_general(left, x, (((1,), (1,)), ((), ())), preferred_element_type=F32).astype(BF16)
        pack_cols(count_ref, row * lam_atoms, lam_atoms, BW, lam_size, hot)
        o_ref[...] = jnp.dot(x, hot[...], preferred_element_type=F32).astype(BF16)

    return pl.pallas_call(
        body,
        out_shape=jax.ShapeDtypeStruct((sum_size, lam_size), BF16),
        in_specs=[SMEM_SPEC, VMEM_SPEC, VMEM_SPEC],
        out_specs=VMEM_SPEC,
        scratch_shapes=[pltpu.VMEM((rows, lam_size), BF16)],
        compiler_params=params(),
        cost_estimate=cost(2 * rows * sum_size * (cols + lam_size), 2 * rows * cols),
        name="pack_density",
    )(basis_count, mask, dens)


def pack_part(pieces, basis_count, first, ncols, size):
    rows, cols = pieces[0].shape
    per = len(pieces)
    depth = per * rows
    atoms = depth // BW

    def body(count_ref, *refs):
        blocks, o_ref, full = refs[:per], refs[per], refs[per + 1]
        row, col = lax.axis_index("row"), lax.axis_index("col")
        for i in range(per):
            at = lax.rem(col ^ (first + i), per) * rows
            full[pl.ds(pl.multiple_of(at, rows), rows), :] = blocks[i][...]
        part = (row * ncols + (col ^ first)) * rows // depth
        hot = pack_rows(count_ref, part * atoms, atoms, BW, size)
        o_ref[...] = jnp.dot(hot, full[...], preferred_element_type=F32).astype(BF16)

    return pl.pallas_call(
        body,
        out_shape=jax.ShapeDtypeStruct((size, cols), BF16),
        in_specs=[SMEM_SPEC] + [VMEM_SPEC] * per,
        out_specs=VMEM_SPEC,
        scratch_shapes=[pltpu.VMEM((depth, cols), BF16)],
        compiler_params=params(),
        cost_estimate=cost(2 * size * depth * cols, 2 * cols * (depth + size)),
        name="pack_part",
    )(basis_count, *pieces)


def exchange(pieces, ncols):
    return [pieces[0]] + [
        lax.ppermute(pieces[n], "col", [(c, c ^ n) for c in range(ncols)]) for n in range(1, ncols)
    ]


def double(own, bits):
    nrows = lax.axis_size("row")
    have = {0: own}
    for bit in bits:
        for far in sorted(have):
            have[far | bit] = lax.ppermute(have[far], "row", [(r, r ^ bit) for r in range(nrows)])
    return have


def swap_cores(x, ncols, chips):
    return lax.ppermute(x, "col", [(c, c ^ 1) for c in range(ncols) if c // CORES in chips])


def gather_line(own, ncols):
    chips = ncols // CORES
    have = {0: (own, swap_cores(own, ncols, range(chips)))}
    up = down = own
    for t in range(1, chips):
        up = lax.ppermute(up, "col", [(c, c + CORES) for c in range((t - 1) * CORES, ncols - CORES)])
        down = lax.ppermute(down, "col", [(c, c - CORES) for c in range(CORES, ncols - (t - 1) * CORES)])
        have[t] = (up, swap_cores(up, ncols, range(t, chips)))
        have[-t] = (down, swap_cores(down, ncols, range(chips - t)))
    return have


def contract(dens, integrals, basis_count, ri_count, ncols, rows, wide):
    depth, lam = dens[0][0].shape
    cols = integrals[0][0].shape[1]
    groups, nrows = len(integrals), len(integrals[0])
    parts = groups * nrows
    chips = ncols // CORES
    lam_atoms, blocks = rows // BW, wide // RW
    lines = [(t, other) for t in range(-(chips - 1), chips) for other in range(CORES)]
    halves = [(far, g) for far in range(nrows) for g in range(groups)]
    tile = 256

    def body(count_ref, ri_ref, *refs):
        d_refs, refs = refs[: len(lines)], refs[len(lines):]
        s_refs, refs = refs[: len(halves)], refs[len(halves):]
        o_ref, d_all, s_all, packed, lam_hot, col_hot, d_sem, s_sem = refs
        row, col = lax.axis_index("row"), lax.axis_index("col")
        chip = col // CORES

        def place(part):
            return pl.ds(pl.multiple_of(part * depth, 16), depth)

        for i, (far, g) in enumerate(halves):
            part = (row ^ far) * groups + (col // (ncols // groups) ^ g)
            pltpu.make_async_copy(s_refs[i], s_all.at[place(part), :], s_sem.at[part]).start()
        for i, (t, other) in enumerate(lines):

            @pl.when((chip >= t) & (chip - t < chips))
            def _():
                part = (chip - t) * CORES + (col % CORES ^ other)
                pltpu.make_async_copy(d_refs[i], d_all.at[place(part), :], d_sem.at[part]).start()

        pack_cols(count_ref, row * lam_atoms, lam_atoms, BW, lam, lam_hot)
        col_hot[...] = pack_rows(ri_ref, col * blocks, blocks, RW, cols)
        for part in range(parts):
            pltpu.make_async_copy(s_refs[0], s_all.at[place(part), :], s_sem.at[part]).wait()
            pltpu.make_async_copy(d_refs[0], d_all.at[place(part), :], d_sem.at[part]).wait()
        for at in range(0, lam, tile):
            x = lax.dot_general(
                d_all[:, pl.ds(at, tile)], s_all[...], (((0,), (0,)), ((), ())), preferred_element_type=F32
            ).astype(BF16)
            packed[pl.ds(at, tile), :] = jnp.dot(x, col_hot[...], preferred_element_type=F32).astype(BF16)
        for at in range(0, rows, tile):
            o_ref[pl.ds(at, tile), :] = jnp.dot(
                lam_hot[pl.ds(at, tile), :], packed[...], preferred_element_type=F32
            ).astype(BF16)

    return pl.pallas_call(
        body,
        out_shape=jax.ShapeDtypeStruct((rows, wide), BF16),
        in_specs=[SMEM_SPEC, SMEM_SPEC] + [ANY_SPEC] * (len(lines) + len(halves)),
        out_specs=VMEM_SPEC,
        scratch_shapes=[
            pltpu.VMEM((parts * depth, lam), BF16),
            pltpu.VMEM((parts * depth, cols), BF16),
            pltpu.VMEM((lam, wide), BF16),
            pltpu.VMEM((rows, lam), BF16),
            pltpu.VMEM((cols, wide), BF16),
            pltpu.SemaphoreType.DMA((parts,)),
            pltpu.SemaphoreType.DMA((parts,)),
        ],
        compiler_params=params(),
        cost_estimate=cost(2 * parts * depth * lam * cols, 2 * parts * depth * (lam + cols)),
        name="contract",
    )(basis_count, ri_count, *[dens[t][o] for t, o in lines], *[integrals[g][f] for f, g in halves])


def program(lam_size, sum_size, col_size):
    def run(three_center, density, block_mask, density_mask, basis_count, ri_count):
        ncols = lax.axis_size("col")
        nrows = lax.axis_size("row")
        rows, depth = density.shape
        pieces = pack_integrals(three_center, block_mask, basis_count, ri_count, ncols, col_size)
        dens = pack_density(density, density_mask, basis_count, lam_size, sum_size)
        got = exchange(pieces, ncols)
        line = gather_line(dens, ncols)
        per = depth // three_center.shape[0]
        bits = [1 << b for b in range(nrows.bit_length() - 1)]
        groups = []
        for g in range(ncols // per):
            own = pack_part(got[g * per : (g + 1) * per], basis_count, g * per, ncols, sum_size)
            groups.append(double(own, bits if g % 2 == 0 else bits[::-1]))
        wide = three_center.shape[1] // ncols
        return contract(line, groups, basis_count, ri_count, ncols, rows, wide)

    return run


def all_fit(basis_count, ri_count, limits):
    def body(count_ref, ri_ref, o_ref):
        fits = jnp.int32(1)
        for ref, groups, limit in ((count_ref, *limits[0]), (count_ref, *limits[1]), (ri_ref, *limits[2])):
            per = ref.shape[0] // groups
            for g in range(groups):
                total = jnp.int32(0)
                for i in range(per):
                    total = total + ref[g * per + i]
                fits = jnp.where(total > limit, 0, fits)
        o_ref[0] = fits

    return pl.pallas_call(
        body,
        out_shape=jax.ShapeDtypeStruct((1,), jnp.int32),
        in_specs=[SMEM_SPEC, SMEM_SPEC],
        out_specs=SMEM_SPEC,
        name="all_fit",
    )(basis_count, ri_count)


def shards(three_center, density, block_mask, density_mask, basis_count, ri_count):
    ncols = lax.axis_size("col")
    nrows = lax.axis_size("row")
    rows, depth = density.shape
    wide = three_center.shape[1] // ncols
    lam_size, sum_size, col_size = rows * 3 // 4, depth * 13 // 16, wide * 5 // 6
    fits = all_fit(basis_count, ri_count, ((nrows, lam_size), (ncols, sum_size), (ncols, col_size)))
    args = (three_center, density, block_mask, density_mask, basis_count, ri_count)
    return lax.cond(
        fits[0] > 0, program(lam_size, sum_size, col_size), program(rows, depth, wide), *args
    )


def solution(mesh):
    in_specs = (
        P(("row", "col"), None),
        P("row", "col"),
        P(("row", "col"), None),
        P("row", "col"),
        P(),
        P(),
    )
    return jax.shard_map(
        shards, mesh=mesh, in_specs=in_specs, out_specs=P("row", "col"), check_vma=False
    )
```

time: 338 us -> 127 us (0.38)
  waiting for transfers between devices: 182 us -> 60.6 us
  blocking collectives: 44 us -> 0 us
  matrix products: 32 us -> 0 us
  local copies, waits for them, and re-layouts: 23.8 us -> 0.14 us
  Pallas kernels: 0 us -> 21.9 us
  other arithmetic: 21.6 us -> 0 us
  starting transfers between devices: 33.2 us -> 42.6 us
    ppermute x19 -> x26, waiting for transfers between devices: 182 us -> 60.6 us  [the longest x7 30 us: exchange(): lax.ppermute(pieces[n], 'col', [(c, c ^ n) for c in range(ncols)])]
    all_to_all x1 -> x0, blocking collectives: 44 us -> none  [shards(): lax.all_to_all(screened, 'col', split_axis=1, concat_axis=0, tiled=True)]
    dot_general x8 -> x0, matrix products: 32 us -> none  [the longest x7 29.6 us: one_turn(): jnp.dot(dcur, pairs[:half], preferred_element_type=jnp.float32)]
    pallas_call x0 -> x6, Pallas kernels: none -> 21.9 us  [the longest x1 11.4 us: contract(): pl.pallas_call(body, out_shape=jax.ShapeDtypeStruct((rows, wide), BF16),...]
    ppermute x19 -> x26, starting transfers between devices: 33.2 us -> 42.6 us  [the longest x7 16.4 us: exchange(): lax.ppermute(pieces[n], 'col', [(c, c ^ n) for c in range(ncols)])]
    concatenate x7 -> x0, other arithmetic: 8.65 us -> none  [one_turn(): pairs = jnp.concatenate([pairs[half:], front], axis=0)]
    while x7 -> x0, local copies, waits for them, and re-layouts: 8.58 us -> none
    slice x8 -> x0, local copies, waits for them, and re-layouts: 7.85 us -> none  [the longest x7 6.86 us: one_turn(): pairs = jnp.concatenate([pairs[half:], front], axis=0)]
  transfers between devices with their start and end apart: 19 -> 26, of which waited for: 10 -> 8; matrix products, arithmetic and copies ran while one was open for 17% -> 0% of each run, Pallas kernels for 0% -> 4%
where the time goes in v3:
time: 127 us
  waiting for transfers between devices  60.6 us (48%)
  starting transfers between devices  42.6 us (34%)
  Pallas kernels  21.9 us (17%)
    ppermute x7, waiting for transfers between devices, exchange(): lax.ppermute(pieces[n], 'col', [(c, c ^ n) for c in range(ncols)])  30 us
    ppermute x6, waiting for transfers between devices, double(): lax.ppermute(have[far], 'row', [(r, r ^ bit) for r in range(nrows)])  28.7 us
    ppermute x7, starting transfers between devices, exchange(): lax.ppermute(pieces[n], 'col', [(c, c ^ n) for c in range(ncols)])  16.4 us
    pallas_call x1, Pallas kernels, contract(): pl.pallas_call(body, out_shape=jax.ShapeDtypeStruct((rows, wide), BF16),...  11.4 us
    ppermute x7, starting transfers between devices, swap_cores(): lax.ppermute(x, 'col', [(c, c ^ 1) for c in range(ncols) if c // CORES in...  11.1 us
    ppermute x6, starting transfers between devices, double(): lax.ppermute(have[far], 'row', [(r, r ^ bit) for r in range(nrows)])  6.25 us
    ppermute x3, starting transfers between devices, gather_line(): lax.ppermute(up, 'col', [(c, c + CORES) for c in range((t - 1) * CORES, n...  5.05 us
    pallas_call x1, Pallas kernels, pack_integrals(): pl.pallas_call(body, out_shape=[jax.ShapeDtypeStruct((rows, packed), BF16...  4.61 us
  transfers between devices with their start and end apart: 26, of which 8 were waited for; matrix products, arithmetic and copies ran while one was open for 0% of the time, Pallas kernels for 4%

profile of v3, /device:TPU:0, one launch (start us, length us, event | category | flops | bytes accessed | tf_op | source)
XLA Modules:
  0.0 127.1 jit_solution(10209264073261070819)
XLA Ops:
  2.0 124.9 %conditional.1 = (bf16[1024,768]{1,0:T(8,128)(2,1)}) conditional(s32[]{:T(128)} %bitcast, (s32[128]{0:T(128)}, s32[32,16]{0,1:T(8,128)}, bf16[1024,512]{1,0:T(8,128)(2,1)}, s32[48]{0:T(128)}, s32[4,48]{1,0:T(4,128)}, /*index=5*/bf16[128,6144]{1,0:T(8,128)(2,1)}) %tuple.11, (s32[128]{0:T(128)}, s32[32,16]{0,1:T(8,128)}, bf16[1024,512]{1,0:T(8,128)(2,1)}, ...), branch_computations={%region_0.0_spmd, %region_1.0_spmd} | conditional | flops 10066329600 | bytes 164900064 | solution.py:309
  2.2 4.6 %pack_integrals.3 = (bf16[128,640]{1,0:T(8,128)(2,1)S(1)}, bf16[128,640]{1,0:T(8,128)(2,1)S(1)}, bf16[128,640]{1,0:T(8,128)(2,1)S(1)}, bf16[128,640]{1,0:T(8,128...) custom-call(s32[128]{0:T(128)} %get-tuple-element.46.count_ref, ...), custom_call_target="tpu_custom_call" | custom-call | flops 1006632960 | bytes 2883584 | tf_op jit(solution)/shard_map/cond/branch_1_fun/pack_integrals/pallas_call | solution.py:97
  6.9 4.1 %collective-permute-start.42 = (bf16[128,640]{1,0:T(8,128)(2,1)S(1)}, bf16[128,640]{1,0:T(8,128)(2,1)S(1)}, u32[]{:S(2)}, u32[]{:S(2)}) collective-permute-start(bf16[128,640]{1,0:T(8,128)(2,1)S(1)} %get-tuple-element.56), channel_id=1, source_target_pairs={{0,4},{1,5},{2,6},{3,7},{4,0},{5,1},{6,2},{7,3},{8,12},{9,13},{10,... | collective-permute-start | bytes 491528 | tf_op jit(solution)/shard_map/cond/branch_1_fun/ppermute | solution.py:164
  11.0 2.4 %pack_density.3.refs_6_ = bf16[416,768]{1,0:T(8,128)(2,1)S(1)} custom-call(s32[128]{0:T(128)S(1)} %copy-done.14, s32[32,16]{1,0:T(8,128)S(1)} %copy.10.mask_ref, bf16[1024,512]{1,0:T(8,128)(2,1)S(1)} %copy-done.18), custom_call_target="tpu_custom_call" | custom-call | flops 1090519040 | bytes 1048576 | tf_op jit(solution)/shard_map/cond/branch_1_fun/pack_density/pallas_call | solution.py:122
  13.4 3.7 %collective-permute-start.33 = (bf16[416,768]{1,0:T(8,128)(2,1)S(1)}, bf16[416,768]{1,0:T(8,128)(2,1)S(1)}, u32[]{:S(2)}, u32[]{:S(2)}) collective-permute-start(bf16[416,768]{1,0:T(8,128)(2,1)S(1)} %pack_density.3.refs_6_), channel_id=1, source_target_pairs={{0,2},{1,3},{2,4},{3,5},{4,6},{5,7},{8,10},{9,11},{10,12},{11,13},... | collective-permute-start | bytes 1916936 | tf_op jit(solution)/shard_map/cond/branch_1_fun/ppermute | solution.py:186
  19.4 2.7 %collective-permute-start.44 = (bf16[128,640]{1,0:T(8,128)(2,1)S(1)}, bf16[128,640]{1,0:T(8,128)(2,1)S(1)}, u32[]{:S(2)}, u32[]{:S(2)}) collective-permute-start(bf16[128,640]{1,0:T(8,128)(2,1)S(1)} %get-tuple-element.58), channel_id=1, source_target_pairs={{0,6},{1,7},{2,4},{3,5},{4,2},{5,3},{6,0},{7,1},{8,14},{9,15},{10,... | collective-permute-start | bytes 491528 | tf_op jit(solution)/shard_map/cond/branch_1_fun/ppermute | solution.py:164
  22.1 1.7 %collective-permute-start.45 = (bf16[128,640]{1,0:T(8,128)(2,1)S(1)}, bf16[128,640]{1,0:T(8,128)(2,1)S(1)}, u32[]{:S(2)}, u32[]{:S(2)}) collective-permute-start(bf16[128,640]{1,0:T(8,128)(2,1)S(1)} %get-tuple-element.59), channel_id=1, source_target_pairs={{0,7},{1,6},{2,5},{3,4},{4,3},{5,2},{6,1},{7,0},{8,15},{9,14},{10,... | collective-permute-start | bytes 491528 | tf_op jit(solution)/shard_map/cond/branch_1_fun/ppermute | solution.py:164
  23.8 23.0 %collective-permute-done.43.refs_1_ = bf16[128,640]{1,0:T(8,128)(2,1)S(1)} collective-permute-done((bf16[128,640]{1,0:T(8,128)(2,1)S(1)}, bf16[128,640]{1,0:T(8,128)(2,1)S(1)}, u32[]{:S(2)}, u32[]{:S(2)}) %collective-permute-start.43) | collective-permute-done | bytes 163872 | tf_op jit(solution)/shard_map/cond/branch_1_fun/ppermute | solution.py:164
  46.8 2.8 %collective-permute-start.32 = (bf16[416,768]{1,0:T(8,128)(2,1)S(1)}, bf16[416,768]{1,0:T(8,128)(2,1)S(1)}, u32[]{:S(2)}, u32[]{:S(2)}) collective-permute-start(bf16[416,768]{1,0:T(8,128)(2,1)S(1)} %pack_density.3.refs_6_), channel_id=1, source_target_pairs={{0,1},{1,0},{2,3},{3,2},{4,5},{5,4},{6,7},{7,6},{8,9},{9,8},{10,11... | collective-permute-start | bytes 1916936 | tf_op jit(solution)/shard_map/cond/branch_1_fun/ppermute | solution.py:178
  50.7 1.6 %collective-permute-start.49 = (bf16[416,640]{1,0:T(8,128)(2,1)S(1)}, bf16[416,640]{1,0:T(8,128)(2,1)S(1)}, u32[]{:S(2)}, u32[]{:S(2)}) collective-permute-start(bf16[416,640]{1,0:T(8,128)(2,1)S(1)} %pack_part.7.refs_15_), channel_id=1, source_target_pairs={{0,16},{8,24},{16,0},{24,8},{1,17},{9,25},{17,1},{25,9},{2,18},{10... | collective-permute-start | bytes 1597448 | tf_op jit(solution)/shard_map/cond/branch_1_fun/ppermute | solution.py:173
  52.3 4.8 %collective-permute-start.40 = (bf16[128,640]{1,0:T(8,128)(2,1)S(1)}, bf16[128,640]{1,0:T(8,128)(2,1)S(1)}, u32[]{:S(2)}, u32[]{:S(2)}) collective-permute-start(bf16[128,640]{1,0:T(8,128)(2,1)S(1)} %get-tuple-element.54), channel_id=1, source_target_pairs={{0,2},{1,3},{2,0},{3,1},{4,6},{5,7},{6,4},{7,5},{8,10},{9,11},{10,... | collective-permute-start | bytes 491528 | tf_op jit(solution)/shard_map/cond/branch_1_fun/ppermute | solution.py:164
  57.1 4.7 %collective-permute-done.40.refs_2_ = bf16[128,640]{1,0:T(8,128)(2,1)S(1)} collective-permute-done((bf16[128,640]{1,0:T(8,128)(2,1)S(1)}, bf16[128,640]{1,0:T(8,128)(2,1)S(1)}, u32[]{:S(2)}, u32[]{:S(2)}) %collective-permute-start.40) | collective-permute-done | bytes 163872 | tf_op jit(solution)/shard_map/cond/branch_1_fun/ppermute | solution.py:164
  61.8 2.1 %collective-permute-start.41 = (bf16[128,640]{1,0:T(8,128)(2,1)S(1)}, bf16[128,640]{1,0:T(8,128)(2,1)S(1)}, u32[]{:S(2)}, u32[]{:S(2)}) collective-permute-start(bf16[128,640]{1,0:T(8,128)(2,1)S(1)} %get-tuple-element.55), channel_id=1, source_target_pairs={{0,3},{1,2},{2,1},{3,0},{4,7},{5,6},{6,5},{7,4},{8,11},{9,10},{10,... | collective-permute-start | bytes 491528 | tf_op jit(solution)/shard_map/cond/branch_1_fun/ppermute | solution.py:164
  65.9 2.3 %collective-permute-done.41.refs_3_ = bf16[128,640]{1,0:T(8,128)(2,1)S(1)} collective-permute-done((bf16[128,640]{1,0:T(8,128)(2,1)S(1)}, bf16[128,640]{1,0:T(8,128)(2,1)S(1)}, u32[]{:S(2)}, u32[]{:S(2)}) %collective-permute-start.41) | collective-permute-done | bytes 163872 | tf_op jit(solution)/shard_map/cond/branch_1_fun/ppermute | solution.py:164
  68.2 1.5 %collective-permute-start.47 = (bf16[416,640]{1,0:T(8,128)(2,1)S(1)}, bf16[416,640]{1,0:T(8,128)(2,1)S(1)}, u32[]{:S(2)}, u32[]{:S(2)}) collective-permute-start(bf16[416,640]{1,0:T(8,128)(2,1)S(1)} %pack_part.7.refs_15_), channel_id=1, source_target_pairs={{0,8},{8,0},{16,24},{24,16},{1,9},{9,1},{17,25},{25,17},{2,10},{10... | collective-permute-start | bytes 1597448 | tf_op jit(solution)/shard_map/cond/branch_1_fun/ppermute | solution.py:173
  72.0 11.2 %collective-permute-done.47.refs_17_ = bf16[416,640]{1,0:T(8,128)(2,1)S(1)} collective-permute-done((bf16[416,640]{1,0:T(8,128)(2,1)S(1)}, bf16[416,640]{1,0:T(8,128)(2,1)S(1)}, u32[]{:S(2)}, u32[]{:S(2)}) %collective-permute-start.47) | collective-permute-done | bytes 532512 | tf_op jit(solution)/shard_map/cond/branch_1_fun/ppermute | solution.py:173
  85.9 1.6 %collective-permute-start.51 = (bf16[416,640]{1,0:T(8,128)(2,1)S(1)}, bf16[416,640]{1,0:T(8,128)(2,1)S(1)}, u32[]{:S(2)}, u32[]{:S(2)}) collective-permute-start(bf16[416,640]{1,0:T(8,128)(2,1)S(1)} %collective-permute-done.49.refs_19_), channel_id=1, source_target_pairs={{0,8},{8,0},{16,24},{24,16},{1,9},{9,1},{17,25},{25,17},{2,10},{10... | collective-permute-start | bytes 1597448 | tf_op jit(solution)/shard_map/cond/branch_1_fun/ppermute | solution.py:173
  87.5 7.1 %collective-permute-done.46.refs_16_ = bf16[416,640]{1,0:T(8,128)(2,1)S(1)} collective-permute-done((bf16[416,640]{1,0:T(8,128)(2,1)S(1)}, bf16[416,640]{1,0:T(8,128)(2,1)S(1)}, u32[]{:S(2)}, u32[]{:S(2)}) %collective-permute-start.46) | collective-permute-done | bytes 532512 | tf_op jit(solution)/shard_map/cond/branch_1_fun/ppermute | solution.py:173
  95.1 10.2 %collective-permute-done.51.refs_21_ = bf16[416,640]{1,0:T(8,128)(2,1)S(1)} collective-permute-done((bf16[416,640]{1,0:T(8,128)(2,1)S(1)}, bf16[416,640]{1,0:T(8,128)(2,1)S(1)}, u32[]{:S(2)}, u32[]{:S(2)}) %collective-permute-start.51) | collective-permute-done | bytes 532512 | tf_op jit(solution)/shard_map/cond/branch_1_fun/ppermute | solution.py:173
  105.3 1.9 %collective-permute-start.31 = (bf16[416,768]{1,0:T(8,128)(2,1)S(1)}, bf16[416,768]{1,0:T(8,128)(2,1)S(1)}, u32[]{:S(2)}, u32[]{:S(2)}) collective-permute-start(bf16[416,768]{1,0:T(8,128)(2,1)S(1)} %collective-permute-done.26.refs_4_), channel_id=1, source_target_pairs={{0,1},{1,0},{2,3},{3,2},{4,5},{5,4},{8,9},{9,8},{10,11},{11,10},{1... | collective-permute-start | bytes 1916936 | tf_op jit(solution)/shard_map/cond/branch_1_fun/ppermute | solution.py:178
  108.1 2.3 %collective-permute-start.30 = (bf16[416,768]{1,0:T(8,128)(2,1)S(1)}, bf16[416,768]{1,0:T(8,128)(2,1)S(1)}, u32[]{:S(2)}, u32[]{:S(2)}) collective-permute-start(bf16[416,768]{1,0:T(8,128)(2,1)S(1)} %collective-permute-done.27.refs_2_), channel_id=1, source_target_pairs={{0,1},{1,0},{2,3},{3,2},{8,9},{9,8},{10,11},{11,10},{16,17},{17,16... | collective-permute-start | bytes 1916936 | tf_op jit(solution)/shard_map/cond/branch_1_fun/ppermute | solution.py:178
  111.1 2.0 %collective-permute-start.29 = (bf16[416,768]{1,0:T(8,128)(2,1)S(1)}, bf16[416,768]{1,0:T(8,128)(2,1)S(1)}, u32[]{:S(2)}, u32[]{:S(2)}) collective-permute-start(bf16[416,768]{1,0:T(8,128)(2,1)S(1)} %collective-permute-done.28.refs_0_), channel_id=1, source_target_pairs={{0,1},{1,0},{8,9},{9,8},{16,17},{17,16},{24,25},{25,24}} | collective-permute-start | bytes 1916936 | tf_op jit(solution)/shard_map/cond/branch_1_fun/ppermute | solution.py:178
  113.3 1.8 %collective-permute-done.29.refs_1_ = bf16[416,768]{1,0:T(8,128)(2,1)S(1)} collective-permute-done((bf16[416,768]{1,0:T(8,128)(2,1)S(1)}, bf16[416,768]{1,0:T(8,128)(2,1)S(1)}, u32[]{:S(2)}, u32[]{:S(2)}) %collective-permute-start.29) | collective-permute-done | bytes 639008 | tf_op jit(solution)/shard_map/cond/branch_1_fun/ppermute | solution.py:178
  115.2 11.4 %contract.3 = bf16[1024,768]{1,0:T(8,128)(2,1)} custom-call(s32[128]{0:T(128)S(1)} %copy-done.14, s32[48]{0:T(128)S(1)} %copy-done.16, bf16[416,768]{1,0:T(8,128)(2,1)S(1)} %collective-permute-done.28.refs_0_, bf16[416,768]{1,0:T(8,128)(2,1)S(1)} %collective-permute-done.29.refs_1_, bf16[416,768]{1,0:T(8,128)(2,1)S(1)} %collective-permute-done.27.refs_2_, ...), custom_call_target="tpu_custom_call" | custom-call | flops 3271557120 | bytes 9371648 | tf_op jit(solution)/shard_map/cond/branch_1_fun/contract/pallas_call | solution.py:239
  (66 shorter events, 13.9 us)
Async XLA Ops:
  6.9 15.2 %collective-permute-start.42 = (bf16[128,640]{1,0:T(8,128)(2,1)S(1)}, bf16[128,640]{1,0:T(8,128)(2,1)S(1)}, u32[]{:S(2)}, u32[]{:S(2)}) collective-permute-start(bf16[128,640]{1,0:T(8,128)(2,1)S(1)} %get-tuple-element.56), channel_id=1, source_target_pairs={{0,4},{1,5},{2,6},{3,7},{4,0},{5,1},{6,2},{7,3},{8,12},{9,13},{10,... | collective-permute-start | bytes 491528 | tf_op jit(solution)/shard_map/cond/branch_1_fun/ppermute | solution.py:164
  13.4 50.5 %collective-permute-start.33 = (bf16[416,768]{1,0:T(8,128)(2,1)S(1)}, bf16[416,768]{1,0:T(8,128)(2,1)S(1)}, u32[]{:S(2)}, u32[]{:S(2)}) collective-permute-start(bf16[416,768]{1,0:T(8,128)(2,1)S(1)} %pack_density.3.refs_6_), channel_id=1, source_target_pairs={{0,2},{1,3},{2,4},{3,5},{4,6},{5,7},{8,10},{9,11},{10,12},{11,13},... | collective-permute-start | bytes 1916936 | tf_op jit(solution)/shard_map/cond/branch_1_fun/ppermute | solution.py:186
  17.1 47.5 %collective-permute-start.26 = (bf16[416,768]{1,0:T(8,128)(2,1)S(1)}, bf16[416,768]{1,0:T(8,128)(2,1)S(1)}, u32[]{:S(2)}, u32[]{:S(2)}) collective-permute-start(bf16[416,768]{1,0:T(8,128)(2,1)S(1)} %pack_density.3.refs_6_), channel_id=1, source_target_pairs={{2,0},{3,1},{4,2},{5,3},{6,4},{7,5},{10,8},{11,9},{12,10},{13,11},... | collective-permute-start | bytes 1916936 | tf_op jit(solution)/shard_map/cond/branch_1_fun/ppermute | solution.py:187
  18.4 28.4 %collective-permute-start.43 = (bf16[128,640]{1,0:T(8,128)(2,1)S(1)}, bf16[128,640]{1,0:T(8,128)(2,1)S(1)}, u32[]{:S(2)}, u32[]{:S(2)}) collective-permute-start(bf16[128,640]{1,0:T(8,128)(2,1)S(1)} %get-tuple-element.57), channel_id=1, source_target_pairs={{0,5},{1,4},{2,7},{3,6},{4,1},{5,0},{6,3},{7,2},{8,13},{9,12},{10,... | collective-permute-start | bytes 491528 | tf_op jit(solution)/shard_map/cond/branch_1_fun/ppermute | solution.py:164
  19.4 30.2 %collective-permute-start.44 = (bf16[128,640]{1,0:T(8,128)(2,1)S(1)}, bf16[128,640]{1,0:T(8,128)(2,1)S(1)}, u32[]{:S(2)}, u32[]{:S(2)}) collective-permute-start(bf16[128,640]{1,0:T(8,128)(2,1)S(1)} %get-tuple-element.58), channel_id=1, source_target_pairs={{0,6},{1,7},{2,4},{3,5},{4,2},{5,3},{6,0},{7,1},{8,14},{9,15},{10,... | collective-permute-start | bytes 491528 | tf_op jit(solution)/shard_map/cond/branch_1_fun/ppermute | solution.py:164
  22.1 27.5 %collective-permute-start.45 = (bf16[128,640]{1,0:T(8,128)(2,1)S(1)}, bf16[128,640]{1,0:T(8,128)(2,1)S(1)}, u32[]{:S(2)}, u32[]{:S(2)}) collective-permute-start(bf16[128,640]{1,0:T(8,128)(2,1)S(1)} %get-tuple-element.59), channel_id=1, source_target_pairs={{0,7},{1,6},{2,5},{3,4},{4,3},{5,2},{6,1},{7,0},{8,15},{9,14},{10,... | collective-permute-start | bytes 491528 | tf_op jit(solution)/shard_map/cond/branch_1_fun/ppermute | solution.py:164
  46.8 24.0 %collective-permute-start.32 = (bf16[416,768]{1,0:T(8,128)(2,1)S(1)}, bf16[416,768]{1,0:T(8,128)(2,1)S(1)}, u32[]{:S(2)}, u32[]{:S(2)}) collective-permute-start(bf16[416,768]{1,0:T(8,128)(2,1)S(1)} %pack_density.3.refs_6_), channel_id=1, source_target_pairs={{0,1},{1,0},{2,3},{3,2},{4,5},{5,4},{6,7},{7,6},{8,9},{9,8},{10,11... | collective-permute-start | bytes 1916936 | tf_op jit(solution)/shard_map/cond/branch_1_fun/ppermute | solution.py:178
  50.7 20.7 %collective-permute-start.49 = (bf16[416,640]{1,0:T(8,128)(2,1)S(1)}, bf16[416,640]{1,0:T(8,128)(2,1)S(1)}, u32[]{:S(2)}, u32[]{:S(2)}) collective-permute-start(bf16[416,640]{1,0:T(8,128)(2,1)S(1)} %pack_part.7.refs_15_), channel_id=1, source_target_pairs={{0,16},{8,24},{16,0},{24,8},{1,17},{9,25},{17,1},{25,9},{2,18},{10... | collective-permute-start | bytes 1597448 | tf_op jit(solution)/shard_map/cond/branch_1_fun/ppermute | solution.py:173
  52.3 9.5 %collective-permute-start.40 = (bf16[128,640]{1,0:T(8,128)(2,1)S(1)}, bf16[128,640]{1,0:T(8,128)(2,1)S(1)}, u32[]{:S(2)}, u32[]{:S(2)}) collective-permute-start(bf16[128,640]{1,0:T(8,128)(2,1)S(1)} %get-tuple-element.54), channel_id=1, source_target_pairs={{0,2},{1,3},{2,0},{3,1},{4,6},{5,7},{6,4},{7,5},{8,10},{9,11},{10,... | collective-permute-start | bytes 491528 | tf_op jit(solution)/shard_map/cond/branch_1_fun/ppermute | solution.py:164
  61.8 6.4 %collective-permute-start.41 = (bf16[128,640]{1,0:T(8,128)(2,1)S(1)}, bf16[128,640]{1,0:T(8,128)(2,1)S(1)}, u32[]{:S(2)}, u32[]{:S(2)}) collective-permute-start(bf16[128,640]{1,0:T(8,128)(2,1)S(1)} %get-tuple-element.55), channel_id=1, source_target_pairs={{0,3},{1,2},{2,1},{3,0},{4,7},{5,6},{6,5},{7,4},{8,11},{9,10},{10,... | collective-permute-start | bytes 491528 | tf_op jit(solution)/shard_map/cond/branch_1_fun/ppermute | solution.py:164
  63.9 19.9 %collective-permute-start.35 = (bf16[416,768]{1,0:T(8,128)(2,1)S(1)}, bf16[416,768]{1,0:T(8,128)(2,1)S(1)}, u32[]{:S(2)}, u32[]{:S(2)}) collective-permute-start(bf16[416,768]{1,0:T(8,128)(2,1)S(1)} %collective-permute-done.33.refs_8_), channel_id=1, source_target_pairs={{2,4},{3,5},{4,6},{5,7},{10,12},{11,13},{12,14},{13,15},{18,20},{1... | collective-permute-start | bytes 1916936 | tf_op jit(solution)/shard_map/cond/branch_1_fun/ppermute | solution.py:186
  64.6 19.9 %collective-permute-start.27 = (bf16[416,768]{1,0:T(8,128)(2,1)S(1)}, bf16[416,768]{1,0:T(8,128)(2,1)S(1)}, u32[]{:S(2)}, u32[]{:S(2)}) collective-permute-start(bf16[416,768]{1,0:T(8,128)(2,1)S(1)} %collective-permute-done.26.refs_4_), channel_id=1, source_target_pairs={{2,0},{3,1},{4,2},{5,3},{10,8},{11,9},{12,10},{13,11},{18,16},{19,... | collective-permute-start | bytes 1916936 | tf_op jit(solution)/shard_map/cond/branch_1_fun/ppermute | solution.py:187
  68.2 14.9 %collective-permute-start.47 = (bf16[416,640]{1,0:T(8,128)(2,1)S(1)}, bf16[416,640]{1,0:T(8,128)(2,1)S(1)}, u32[]{:S(2)}, u32[]{:S(2)}) collective-permute-start(bf16[416,640]{1,0:T(8,128)(2,1)S(1)} %pack_part.7.refs_15_), channel_id=1, source_target_pairs={{0,8},{8,0},{16,24},{24,16},{1,9},{9,1},{17,25},{25,17},{2,10},{10... | collective-permute-start | bytes 1597448 | tf_op jit(solution)/shard_map/cond/branch_1_fun/ppermute | solution.py:173
  70.9 15.0 %collective-permute-start.48 = (bf16[416,640]{1,0:T(8,128)(2,1)S(1)}, bf16[416,640]{1,0:T(8,128)(2,1)S(1)}, u32[]{:S(2)}, u32[]{:S(2)}) collective-permute-start(bf16[416,640]{1,0:T(8,128)(2,1)S(1)} %pack_part.6.refs_14_), channel_id=1, source_target_pairs={{0,16},{8,24},{16,0},{24,8},{1,17},{9,25},{17,1},{25,9},{2,18},{10... | collective-permute-start | bytes 1597448 | tf_op jit(solution)/shard_map/cond/branch_1_fun/ppermute | solution.py:173
  71.5 23.1 %collective-permute-start.46 = (bf16[416,640]{1,0:T(8,128)(2,1)S(1)}, bf16[416,640]{1,0:T(8,128)(2,1)S(1)}, u32[]{:S(2)}, u32[]{:S(2)}) collective-permute-start(bf16[416,640]{1,0:T(8,128)(2,1)S(1)} %pack_part.6.refs_14_), channel_id=1, source_target_pairs={{0,8},{8,0},{16,24},{24,16},{1,9},{9,1},{17,25},{25,17},{2,10},{10... | collective-permute-start | bytes 1597448 | tf_op jit(solution)/shard_map/cond/branch_1_fun/ppermute | solution.py:173
  83.2 24.9 %collective-permute-start.34 = (bf16[416,768]{1,0:T(8,128)(2,1)S(1)}, bf16[416,768]{1,0:T(8,128)(2,1)S(1)}, u32[]{:S(2)}, u32[]{:S(2)}) collective-permute-start(bf16[416,768]{1,0:T(8,128)(2,1)S(1)} %collective-permute-done.33.refs_8_), channel_id=1, source_target_pairs={{2,3},{3,2},{4,5},{5,4},{6,7},{7,6},{10,11},{11,10},{12,13},{13,12... | collective-permute-start | bytes 1916936 | tf_op jit(solution)/shard_map/cond/branch_1_fun/ppermute | solution.py:178
  83.9 26.5 %collective-permute-start.37 = (bf16[416,768]{1,0:T(8,128)(2,1)S(1)}, bf16[416,768]{1,0:T(8,128)(2,1)S(1)}, u32[]{:S(2)}, u32[]{:S(2)}) collective-permute-start(bf16[416,768]{1,0:T(8,128)(2,1)S(1)} %collective-permute-done.35.refs_10_), channel_id=1, source_target_pairs={{4,6},{5,7},{12,14},{13,15},{20,22},{21,23},{28,30},{29,31}} | collective-permute-start | bytes 1916936 | tf_op jit(solution)/shard_map/cond/branch_1_fun/ppermute | solution.py:186
  84.6 26.5 %collective-permute-start.28 = (bf16[416,768]{1,0:T(8,128)(2,1)S(1)}, bf16[416,768]{1,0:T(8,128)(2,1)S(1)}, u32[]{:S(2)}, u32[]{:S(2)}) collective-permute-start(bf16[416,768]{1,0:T(8,128)(2,1)S(1)} %collective-permute-done.27.refs_2_), channel_id=1, source_target_pairs={{2,0},{3,1},{10,8},{11,9},{18,16},{19,17},{26,24},{27,25}} | collective-permute-start | bytes 1916936 | tf_op jit(solution)/shard_map/cond/branch_1_fun/ppermute | solution.py:187
  85.9 19.4 %collective-permute-start.51 = (bf16[416,640]{1,0:T(8,128)(2,1)S(1)}, bf16[416,640]{1,0:T(8,128)(2,1)S(1)}, u32[]{:S(2)}, u32[]{:S(2)}) collective-permute-start(bf16[416,640]{1,0:T(8,128)(2,1)S(1)} %collective-permute-done.49.refs_19_), channel_id=1, source_target_pairs={{0,8},{8,0},{16,24},{24,16},{1,9},{9,1},{17,25},{25,17},{2,10},{10... | collective-permute-start | bytes 1597448 | tf_op jit(solution)/shard_map/cond/branch_1_fun/ppermute | solution.py:173
  94.6 12.8 %collective-permute-start.50 = (bf16[416,640]{1,0:T(8,128)(2,1)S(1)}, bf16[416,640]{1,0:T(8,128)(2,1)S(1)}, u32[]{:S(2)}, u32[]{:S(2)}) collective-permute-start(bf16[416,640]{1,0:T(8,128)(2,1)S(1)} %collective-permute-done.46.refs_16_), channel_id=1, source_target_pairs={{0,16},{8,24},{16,0},{24,8},{1,17},{9,25},{17,1},{25,9},{2,18},{10... | collective-permute-start | bytes 1597448 | tf_op jit(solution)/shard_map/cond/branch_1_fun/ppermute | solution.py:173
  105.3 7.9 %collective-permute-start.31 = (bf16[416,768]{1,0:T(8,128)(2,1)S(1)}, bf16[416,768]{1,0:T(8,128)(2,1)S(1)}, u32[]{:S(2)}, u32[]{:S(2)}) collective-permute-start(bf16[416,768]{1,0:T(8,128)(2,1)S(1)} %collective-permute-done.26.refs_4_), channel_id=1, source_target_pairs={{0,1},{1,0},{2,3},{3,2},{4,5},{5,4},{8,9},{9,8},{10,11},{11,10},{1... | collective-permute-start | bytes 1916936 | tf_op jit(solution)/shard_map/cond/branch_1_fun/ppermute | solution.py:178
  107.4 5.8 %collective-permute-start.36 = (bf16[416,768]{1,0:T(8,128)(2,1)S(1)}, bf16[416,768]{1,0:T(8,128)(2,1)S(1)}, u32[]{:S(2)}, u32[]{:S(2)}) collective-permute-start(bf16[416,768]{1,0:T(8,128)(2,1)S(1)} %collective-permute-done.35.refs_10_), channel_id=1, source_target_pairs={{4,5},{5,4},{6,7},{7,6},{12,13},{13,12},{14,15},{15,14},{20,21},{2... | collective-permute-start | bytes 1916936 | tf_op jit(solution)/shard_map/cond/branch_1_fun/ppermute | solution.py:178
  108.1 5.1 %collective-permute-start.30 = (bf16[416,768]{1,0:T(8,128)(2,1)S(1)}, bf16[416,768]{1,0:T(8,128)(2,1)S(1)}, u32[]{:S(2)}, u32[]{:S(2)}) collective-permute-start(bf16[416,768]{1,0:T(8,128)(2,1)S(1)} %collective-permute-done.27.refs_2_), channel_id=1, source_target_pairs={{0,1},{1,0},{2,3},{3,2},{8,9},{9,8},{10,11},{11,10},{16,17},{17,16... | collective-permute-start | bytes 1916936 | tf_op jit(solution)/shard_map/cond/branch_1_fun/ppermute | solution.py:178
  111.1 4.0 %collective-permute-start.29 = (bf16[416,768]{1,0:T(8,128)(2,1)S(1)}, bf16[416,768]{1,0:T(8,128)(2,1)S(1)}, u32[]{:S(2)}, u32[]{:S(2)}) collective-permute-start(bf16[416,768]{1,0:T(8,128)(2,1)S(1)} %collective-permute-done.28.refs_0_), channel_id=1, source_target_pairs={{0,1},{1,0},{8,9},{9,8},{16,17},{17,16},{24,25},{25,24}} | collective-permute-start | bytes 1916936 | tf_op jit(solution)/shard_map/cond/branch_1_fun/ppermute | solution.py:178
  (17 other events, 432.2 us)

commit v4 on v3

--- a/solution.py
+++ b/solution.py
@@ -72,19 +72,22 @@
     return jnp.dot(keep, right, preferred_element_type=F32)
 
 
-def pack_integrals(tc, block_mask, basis_count, ri_count, ncols, packed):
+def pack_integrals(tc, block_mask, basis_count, ri_count, ncols, packed, arrived=None):
     rows, cols = tc.shape
     atoms = rows // BW
     wide = cols // ncols
     blocks = wide // RW
+    chips = ncols // CORES
+    first = arrived is None
 
     def body(count_ref, ri_ref, mask_ref, x_ref, *refs):
-        outs, held, hot = refs[:ncols], refs[ncols], refs[ncols + 1]
+        held, hot = refs[-2:]
         row, col = lax.axis_index("row"), lax.axis_index("col")
+        core = lax.rem(col, CORES)
         base = (row * ncols + col) * atoms
         slot = iota((BW, RW), 0)
-        for n in range(ncols):
-            dest = col ^ n
+        for t in range(chips):
+            dest = col ^ (CORES * t + (1 if first else 0))
             for b in range(blocks):
                 for a in range(atoms):
                     limit = jnp.where(mask_ref[a, dest * blocks + b] > 0, count_ref[base + a], 0)
@@ -92,18 +95,25 @@
                     x = x_ref[pl.ds(a * BW, BW), pl.ds(lanes, RW)].astype(F32)
                     held[pl.ds(a * BW, BW), pl.ds(b * RW, RW)] = jnp.where(slot < limit, x, 0.0).astype(BF16)
             pack_cols(ri_ref, dest * blocks, blocks, RW, packed, hot)
-            outs[n][...] = jnp.dot(held[...], hot[...], preferred_element_type=F32).astype(BF16)
-
-    return pl.pallas_call(
-        body,
-        out_shape=[jax.ShapeDtypeStruct((rows, packed), BF16)] * ncols,
-        in_specs=[SMEM_SPEC, SMEM_SPEC, SMEM_SPEC, VMEM_SPEC],
-        out_specs=[VMEM_SPEC] * ncols,
+            x = jnp.dot(held[...], hot[...], preferred_element_type=F32).astype(BF16)
+            if first:
+                refs[0][t] = x
+            else:
+                refs[1 + t][pl.ds(pl.multiple_of(core * rows, rows), rows), :] = x
+                refs[1 + t][pl.ds(pl.multiple_of((1 - core) * rows, rows), rows), :] = refs[0][t]
+
+    shape = jax.ShapeDtypeStruct((chips, rows, packed), BF16)
+    merged = jax.ShapeDtypeStruct((CORES * rows, packed), BF16)
+    return pl.pallas_call(
+        body,
+        out_shape=shape if first else [merged] * chips,
+        in_specs=[SMEM_SPEC, SMEM_SPEC, SMEM_SPEC] + [VMEM_SPEC] * (1 if first else 2),
+        out_specs=VMEM_SPEC if first else [VMEM_SPEC] * chips,
         scratch_shapes=[pltpu.VMEM((rows, wide), BF16), pltpu.VMEM((wide, packed), BF16)],
         compiler_params=params(),
-        cost_estimate=cost(2 * rows * cols * packed, 2 * rows * (cols + ncols * packed)),
-        name="pack_integrals",
-    )(basis_count, ri_count, block_mask, tc)
+        cost_estimate=cost(rows * cols * packed, rows * cols + 3 * chips * rows * packed),
+        name="pack_other_core" if first else "pack_own_core",
+    )(basis_count, ri_count, block_mask, tc, *([] if first else [arrived]))
 
 
 def pack_density(dens, mask, basis_count, lam_size, sum_size):
@@ -139,11 +149,11 @@
 
     def body(count_ref, *refs):
         blocks, o_ref, full = refs[:per], refs[per], refs[per + 1]
-        row, col = lax.axis_index("row"), lax.axis_index("col")
+        row, chip = lax.axis_index("row"), lax.axis_index("col") // CORES
         for i in range(per):
-            at = lax.rem(col ^ (first + i), per) * rows
+            at = lax.rem(chip ^ (first + i), per) * rows
             full[pl.ds(pl.multiple_of(at, rows), rows), :] = blocks[i][...]
-        part = (row * ncols + (col ^ first)) * rows // depth
+        part = (row * (ncols // CORES) + (chip ^ first)) * rows // depth
         hot = pack_rows(count_ref, part * atoms, atoms, BW, size)
         o_ref[...] = jnp.dot(hot, full[...], preferred_element_type=F32).astype(BF16)
 
@@ -159,120 +169,142 @@
     )(basis_count, *pieces)
 
 
-def exchange(pieces, ncols):
-    return [pieces[0]] + [
-        lax.ppermute(pieces[n], "col", [(c, c ^ n) for c in range(ncols)]) for n in range(1, ncols)
-    ]
-
-
-def double(own, bits):
-    nrows = lax.axis_size("row")
+def exchange(x, axis, bit):
+    peers = lax.axis_size(axis)
+    return lax.ppermute(x, axis, [(i, i ^ bit) for i in range(peers)])
+
+
+def double(own, axis, bits):
     have = {0: own}
     for bit in bits:
         for far in sorted(have):
-            have[far | bit] = lax.ppermute(have[far], "row", [(r, r ^ bit) for r in range(nrows)])
+            have[far | bit] = exchange(have[far], axis, bit)
     return have
 
 
-def swap_cores(x, ncols, chips):
-    return lax.ppermute(x, "col", [(c, c ^ 1) for c in range(ncols) if c // CORES in chips])
-
-
-def gather_line(own, ncols):
-    chips = ncols // CORES
-    have = {0: (own, swap_cores(own, ncols, range(chips)))}
-    up = down = own
-    for t in range(1, chips):
-        up = lax.ppermute(up, "col", [(c, c + CORES) for c in range((t - 1) * CORES, ncols - CORES)])
-        down = lax.ppermute(down, "col", [(c, c - CORES) for c in range(CORES, ncols - (t - 1) * CORES)])
-        have[t] = (up, swap_cores(up, ncols, range(t, chips)))
-        have[-t] = (down, swap_cores(down, ncols, range(chips - t)))
-    return have
-
-
-def contract(dens, integrals, basis_count, ri_count, ncols, rows, wide):
-    depth, lam = dens[0][0].shape
+def contract(dens, integrals, basis_count, ri_count, ncols, rows, wide, before=None):
+    keys = sorted(dens)
+    depth, lam = dens[keys[0]].shape
     cols = integrals[0][0].shape[1]
     groups, nrows = len(integrals), len(integrals[0])
     parts = groups * nrows
-    chips = ncols // CORES
     lam_atoms, blocks = rows // BW, wide // RW
-    lines = [(t, other) for t in range(-(chips - 1), chips) for other in range(CORES)]
     halves = [(far, g) for far in range(nrows) for g in range(groups)]
+    last = before is not None
     tile = 256
 
     def body(count_ref, ri_ref, *refs):
-        d_refs, refs = refs[: len(lines)], refs[len(lines):]
+        d_refs, refs = refs[: len(keys)], refs[len(keys):]
         s_refs, refs = refs[: len(halves)], refs[len(halves):]
-        o_ref, d_all, s_all, packed, lam_hot, col_hot, d_sem, s_sem = refs
+        if last:
+            before_ref, o_ref, d_all, s_all, d_sem, s_sem, b_sem, total, packed, lam_hot, col_hot = refs
+            pltpu.make_async_copy(before_ref, total, b_sem).start()
+        else:
+            o_ref, d_all, s_all, d_sem, s_sem = refs
         row, col = lax.axis_index("row"), lax.axis_index("col")
-        chip = col // CORES
-
-        def place(part):
-            return pl.ds(pl.multiple_of(part * depth, 16), depth)
-
-        for i, (far, g) in enumerate(halves):
-            part = (row ^ far) * groups + (col // (ncols // groups) ^ g)
-            pltpu.make_async_copy(s_refs[i], s_all.at[place(part), :], s_sem.at[part]).start()
-        for i, (t, other) in enumerate(lines):
-
-            @pl.when((chip >= t) & (chip - t < chips))
-            def _():
-                part = (chip - t) * CORES + (col % CORES ^ other)
-                pltpu.make_async_copy(d_refs[i], d_all.at[place(part), :], d_sem.at[part]).start()
-
-        pack_cols(count_ref, row * lam_atoms, lam_atoms, BW, lam, lam_hot)
-        col_hot[...] = pack_rows(ri_ref, col * blocks, blocks, RW, cols)
-        for part in range(parts):
-            pltpu.make_async_copy(s_refs[0], s_all.at[place(part), :], s_sem.at[part]).wait()
-            pltpu.make_async_copy(d_refs[0], d_all.at[place(part), :], d_sem.at[part]).wait()
+
+        def place(i):
+            return pl.ds(i * depth, depth)
+
+        for i, far in enumerate(keys):
+            pltpu.make_async_copy(d_refs[i], d_all.at[place(i), :], d_sem.at[i]).start()
+            part = col ^ far
+            for j, (away, g) in enumerate(halves):
+
+                @pl.when(part == (row ^ away) * groups + (col // (ncols // groups) ^ g))
+                def _():
+                    pltpu.make_async_copy(s_refs[j], s_all.at[place(i), :], s_sem.at[i]).start()
+
+        if last:
+            pack_cols(count_ref, row * lam_atoms, lam_atoms, BW, lam, lam_hot)
+            col_hot[...] = pack_rows(ri_ref, col * blocks, blocks, RW, cols)
+            pltpu.make_async_copy(before_ref, total, b_sem).wait()
+        for i in range(len(keys)):
+            pltpu.make_async_copy(d_refs[i], d_all.at[place(i), :], d_sem.at[i]).wait()
+            pltpu.make_async_copy(s_refs[0], s_all.at[place(i), :], s_sem.at[i]).wait()
         for at in range(0, lam, tile):
             x = lax.dot_general(
                 d_all[:, pl.ds(at, tile)], s_all[...], (((0,), (0,)), ((), ())), preferred_element_type=F32
-            ).astype(BF16)
-            packed[pl.ds(at, tile), :] = jnp.dot(x, col_hot[...], preferred_element_type=F32).astype(BF16)
-        for at in range(0, rows, tile):
-            o_ref[pl.ds(at, tile), :] = jnp.dot(
-                lam_hot[pl.ds(at, tile), :], packed[...], preferred_element_type=F32
-            ).astype(BF16)
-
-    return pl.pallas_call(
-        body,
-        out_shape=jax.ShapeDtypeStruct((rows, wide), BF16),
-        in_specs=[SMEM_SPEC, SMEM_SPEC] + [ANY_SPEC] * (len(lines) + len(halves)),
-        out_specs=VMEM_SPEC,
-        scratch_shapes=[
-            pltpu.VMEM((parts * depth, lam), BF16),
-            pltpu.VMEM((parts * depth, cols), BF16),
+            )
+            if last:
+                x = (x + total[pl.ds(at, tile), :]).astype(BF16)
+                packed[pl.ds(at, tile), :] = jnp.dot(x, col_hot[...], preferred_element_type=F32).astype(BF16)
+            else:
+                o_ref[pl.ds(at, tile), :] = x
+        if last:
+            for at in range(0, rows, tile):
+                o_ref[pl.ds(at, tile), :] = jnp.dot(
+                    lam_hot[pl.ds(at, tile), :], packed[...], preferred_element_type=F32
+                ).astype(BF16)
+
+    n = len(keys)
+    scratch = [
+        pltpu.VMEM((n * depth, lam), BF16),
+        pltpu.VMEM((n * depth, cols), BF16),
+        pltpu.SemaphoreType.DMA((n,)),
+        pltpu.SemaphoreType.DMA((n,)),
+    ]
+    if last:
+        scratch += [
+            pltpu.SemaphoreType.DMA(()),
+            pltpu.VMEM((lam, cols), F32),
             pltpu.VMEM((lam, wide), BF16),
             pltpu.VMEM((rows, lam), BF16),
             pltpu.VMEM((cols, wide), BF16),
-            pltpu.SemaphoreType.DMA((parts,)),
-            pltpu.SemaphoreType.DMA((parts,)),
-        ],
+        ]
+    out = jax.ShapeDtypeStruct((rows, wide), BF16) if last else jax.ShapeDtypeStruct((lam, cols), F32)
+    return pl.pallas_call(
+        body,
+        out_shape=out,
+        in_specs=[SMEM_SPEC, SMEM_SPEC] + [ANY_SPEC] * (n + parts + (1 if last else 0)),
+        out_specs=VMEM_SPEC,
+        scratch_shapes=scratch,
         compiler_params=params(),
-        cost_estimate=cost(2 * parts * depth * lam * cols, 2 * parts * depth * (lam + cols)),
-        name="contract",
-    )(basis_count, ri_count, *[dens[t][o] for t, o in lines], *[integrals[g][f] for f, g in halves])
+        cost_estimate=cost(2 * n * depth * lam * cols, 2 * n * depth * (lam + cols)),
+        name="contract_last" if last else "contract_first",
+    )(
+        basis_count,
+        ri_count,
+        *[dens[far] for far in keys],
+        *[integrals[g][far] for far, g in halves],
+        *([before] if last else []),
+    )
 
 
 def program(lam_size, sum_size, col_size):
     def run(three_center, density, block_mask, density_mask, basis_count, ri_count):
         ncols = lax.axis_size("col")
         nrows = lax.axis_size("row")
+        chips = ncols // CORES
         rows, depth = density.shape
-        pieces = pack_integrals(three_center, block_mask, basis_count, ri_count, ncols, col_size)
-        dens = pack_density(density, density_mask, basis_count, lam_size, sum_size)
-        got = exchange(pieces, ncols)
-        line = gather_line(dens, ncols)
-        per = depth // three_center.shape[0]
-        bits = [1 << b for b in range(nrows.bit_length() - 1)]
-        groups = []
-        for g in range(ncols // per):
-            own = pack_part(got[g * per : (g + 1) * per], basis_count, g * per, ncols, sum_size)
-            groups.append(double(own, bits if g % 2 == 0 else bits[::-1]))
         wide = three_center.shape[1] // ncols
-        return contract(line, groups, basis_count, ri_count, ncols, rows, wide)
+        row_bits = [1 << b for b in range(nrows.bit_length() - 1)]
+        chip_bits = [CORES << b for b in range(chips.bit_length() - 1)][::-1]
+
+        own = pack_density(density, density_mask, basis_count, lam_size, sum_size)
+        counts = (block_mask, basis_count, ri_count, ncols, col_size)
+        other = exchange(pack_integrals(three_center, *counts), "col", 1)
+        line = {0: own, chip_bits[0]: exchange(own, "col", chip_bits[0])}
+        other, _ = lax.optimization_barrier((other, own))
+        pieces = pack_integrals(three_center, *counts, other)
+        got = [pieces[0]] + [exchange(pieces[t], "col", CORES * t) for t in range(1, chips)]
+        per = depth // pieces[0].shape[0]
+        parts, groups = [], []
+        for g in range(chips // per):
+            parts.append(pack_part(got[g * per : (g + 1) * per], basis_count, g * per, ncols, sum_size))
+            groups.append(double(parts[g], "row", row_bits if g % 2 == 0 else row_bits[::-1]))
+        for far in list(line):
+            line[far], _ = lax.optimization_barrier((line[far], parts[0] if far == 0 else parts[-1]))
+        for bit in chip_bits[1:]:
+            for far in sorted(line):
+                line[far | bit] = exchange(line[far], "col", bit)
+        blocks = {}
+        for far, block in line.items():
+            blocks[far] = block
+            blocks[far | 1] = exchange(block, "col", 1)
+        late = {far: blocks.pop(far) for far in (ncols - CORES, ncols - 1)}
+        ends = (groups, basis_count, ri_count, ncols, rows, wide)
+        return contract(late, *ends, contract(blocks, *ends))
 
     return run
 

time: 127 us -> 117 us (0.921); the launches traced: 127 us -> 115 us
  starting transfers between devices: 42.6 us -> 24.8 us
  Pallas kernels: 21.9 us -> 25.8 us
  waiting for transfers between devices: 60.6 us -> 62.1 us
    ppermute x26 -> x17, starting transfers between devices: 42.6 us -> 24.8 us  [exchange(): return lax.ppermute(x, axis, [(i, i ^ bit) for i in range(peers)])]
    pallas_call x2 -> x4, Pallas kernels: 16 us -> 19.8 us  [the longest x2 14.5 us: contract(): pl.pallas_call(body, out_shape=out, in_specs=[SMEM_SPEC, SMEM_SPEC] + [AN...]
    ppermute x26 -> x17, waiting for transfers between devices: 60.6 us -> 62.1 us  [exchange(): return lax.ppermute(x, axis, [(i, i ^ bit) for i in range(peers)])]
  transfers between devices with their start and end apart: 26 -> 17, of which waited for: 8 -> 7; matrix products, arithmetic and copies ran while one was open for 0% -> 0% of each run, Pallas kernels for 4% -> 11%
where the time goes in v4:
time: 117 us; the launch traced here: 115 us
  waiting for transfers between devices  62.1 us (53%)
  Pallas kernels  25.8 us (22%)
  starting transfers between devices  24.8 us (21%)
    ppermute x17, waiting for transfers between devices, exchange(): return lax.ppermute(x, axis, [(i, i ^ bit) for i in range(peers)])  62.1 us
    ppermute x17, starting transfers between devices, exchange(): return lax.ppermute(x, axis, [(i, i ^ bit) for i in range(peers)])  24.8 us
    pallas_call x2, Pallas kernels, contract(): pl.pallas_call(body, out_shape=out, in_specs=[SMEM_SPEC, SMEM_SPEC] + [AN...  14.5 us
    pallas_call x2, Pallas kernels, pack_integrals(): pl.pallas_call(body, out_shape=shape if first else [merged] * chips, in_s...  5.31 us
    pallas_call x1, Pallas kernels, pack_density(): pl.pallas_call(body, out_shape=jax.ShapeDtypeStruct((sum_size, lam_size),...  2.37 us
  transfers between devices with their start and end apart: 17, of which 7 were waited for; matrix products, arithmetic and copies ran while one was open for 0% of the time, Pallas kernels for 11%

profile of v4, /device:TPU:0, one launch (start us, length us, event | category | flops | bytes accessed | tf_op | source)
XLA Modules:
  0.0 115.2 jit_solution(5589533243505218097)
XLA Ops:
  0.0 1.3 %all_fit.1 = s32[1]{0:T(128)} custom-call(s32[128]{0:T(128)} %count_ref.1, s32[48]{0:T(128)} %ri_ref.1), custom_call_target="tpu_custom_call" | custom-call | tf_op jit(solution)/shard_map/all_fit/pallas_call | solution.py:324
  2.0 113.0 %conditional.1 = (bf16[1024,768]{1,0:T(8,128)(2,1)}) conditional(s32[]{:T(128)} %bitcast, (s32[128]{0:T(128)}, s32[32,16]{0,1:T(8,128)}, bf16[1024,512]{1,0:T(8,128)(2,1)}, s32[48]{0:T(128)}, s32[4,48]{1,0:T(4,128)}, /*index=5*/bf16[128,6144]{1,0:T(8,128)(2,1)}) %tuple.17, (s32[128]{0:T(128)}, s32[32,16]{0,1:T(8,128)}, bf16[1024,512]{1,0:T(8,128)(2,1)}, ...), branch_computations={%region_0.0_spmd, %region_1.0_spmd} | conditional | flops 10066329600 | bytes 126110544 | solution.py:341
  2.2 3.1 %pack_other_core.3 = bf16[4,128,640]{2,1,0:T(8,128)(2,1)S(1)} custom-call(s32[128]{0:T(128)} %get-tuple-element.45.count_ref, s32[48]{0:T(128)} %get-tuple-element.46.ri_ref, s32[4,48]{1,0:T(4,128)} %get-tuple-element.49.mask_ref, bf16[128,6144]{1,0:T(8,128)(2,1)} %get-tuple-element.50.x_ref), custom_call_target="tpu_custom_call" | custom-call | flops 503316480 | bytes 1769472 | tf_op jit(solution)/shard_map/cond/branch_1_fun/pack_other_core/pallas_call | solution.py:107
  6.0 2.4 %pack_density.3.refs_0_ = bf16[416,768]{1,0:T(8,128)(2,1)S(1)} custom-call(s32[128]{0:T(128)S(1)} %copy-done.10, s32[32,16]{1,0:T(8,128)S(1)} %copy.10.mask_ref, bf16[1024,512]{1,0:T(8,128)(2,1)S(1)} %copy-done.18), custom_call_target="tpu_custom_call" | custom-call | flops 1090519040 | bytes 1048576 | tf_op jit(solution)/shard_map/cond/branch_1_fun/pack_density/pallas_call | solution.py:132
  8.4 2.2 %pack_own_core.3 = (bf16[256,640]{1,0:T(8,128)(2,1)S(1)}, bf16[256,640]{1,0:T(8,128)(2,1)S(1)}, bf16[256,640]{1,0:T(8,128)(2,1)S(1)}, bf16[256,640]{1,0:T(8,128)(2,1)S(1)}) custom-call(s32[128]{0:T(128)S(1)} %copy-done.10, s32[48]{0:T(128)S(1)} %copy-done.16, s32[4,48]{1,0:T(4,128)S(1)} %copy-done.12, bf16[128,6144]{1,0:T(8,128)(2,1)S(1)} %copy-done.2, ...), custom_call_target="tpu_custom_call" | custom-call | flops 503316480 | bytes 1769472 | tf_op jit(solution)/shard_map/cond/branch_1_fun/pack_own_core/pallas_call | solution.py:107
  10.6 2.7 %collective-permute-start.23 = (bf16[256,640]{1,0:T(8,128)(2,1)S(1)}, bf16[256,640]{1,0:T(8,128)(2,1)S(1)}, u32[]{:S(2)}, u32[]{:S(2)}) collective-permute-start(bf16[256,640]{1,0:T(8,128)(2,1)S(1)} %get-tuple-element.56), channel_id=1, source_target_pairs={{0,2},{1,3},{2,0},{3,1},{4,6},{5,7},{6,4},{7,5},{8,10},{9,11},{10,... | collective-permute-start | bytes 983048 | tf_op jit(solution)/shard_map/cond/branch_1_fun/ppermute | solution.py:174
  13.3 2.6 %collective-permute-start.17 = (bf16[416,768]{1,0:T(8,128)(2,1)S(1)}, bf16[416,768]{1,0:T(8,128)(2,1)S(1)}, u32[]{:S(2)}, u32[]{:S(2)}) collective-permute-start(bf16[416,768]{1,0:T(8,128)(2,1)S(1)} %pack_density.3.refs_0_), channel_id=1, source_target_pairs={{0,4},{1,5},{2,6},{3,7},{4,0},{5,1},{6,2},{7,3},{8,12},{9,13},{10,... | collective-permute-start | bytes 1916936 | tf_op jit(solution)/shard_map/cond/branch_1_fun/ppermute | solution.py:174
  16.2 12.3 %collective-permute-done.23.refs_1_ = bf16[256,640]{1,0:T(8,128)(2,1)S(1)} collective-permute-done((bf16[256,640]{1,0:T(8,128)(2,1)S(1)}, bf16[256,640]{1,0:T(8,128)(2,1)S(1)}, u32[]{:S(2)}, u32[]{:S(2)}) %collective-permute-start.23) | collective-permute-done | bytes 327712 | tf_op jit(solution)/shard_map/cond/branch_1_fun/ppermute | solution.py:174
  29.7 1.8 %collective-permute-start.26 = (bf16[416,640]{1,0:T(8,128)(2,1)S(1)}, bf16[416,640]{1,0:T(8,128)(2,1)S(1)}, u32[]{:S(2)}, u32[]{:S(2)}) collective-permute-start(bf16[416,640]{1,0:T(8,128)(2,1)S(1)} %pack_part.7.refs_6_.refs_2_), channel_id=1, source_target_pairs={{0,16},{8,24},{16,0},{24,8},{1,17},{9,25},{17,1},{25,9},{2,18},{10... | collective-permute-start | bytes 1597448 | tf_op jit(solution)/shard_map/cond/branch_1_fun/ppermute | solution.py:174
  31.4 1.5 %collective-permute-start.24 = (bf16[416,640]{1,0:T(8,128)(2,1)S(1)}, bf16[416,640]{1,0:T(8,128)(2,1)S(1)}, u32[]{:S(2)}, u32[]{:S(2)}) collective-permute-start(bf16[416,640]{1,0:T(8,128)(2,1)S(1)} %pack_part.7.refs_6_.refs_2_), channel_id=1, source_target_pairs={{0,8},{8,0},{16,24},{24,16},{1,9},{9,1},{17,25},{25,17},{2,10},{10... | collective-permute-start | bytes 1597448 | tf_op jit(solution)/shard_map/cond/branch_1_fun/ppermute | solution.py:174
  32.9 2.5 %collective-permute-start.20 = (bf16[256,640]{1,0:T(8,128)(2,1)S(1)}, bf16[256,640]{1,0:T(8,128)(2,1)S(1)}, u32[]{:S(2)}, u32[]{:S(2)}) collective-permute-start(bf16[256,640]{1,0:T(8,128)(2,1)S(1)} %get-tuple-element.53), channel_id=1, source_target_pairs={{0,6},{1,7},{2,4},{3,5},{4,2},{5,3},{6,0},{7,1},{8,14},{9,15},{10,... | collective-permute-start | bytes 983048 | tf_op jit(solution)/shard_map/cond/branch_1_fun/ppermute | solution.py:174
  35.4 30.8 %collective-permute-done.19.refs_0_ = bf16[256,640]{1,0:T(8,128)(2,1)S(1)} collective-permute-done((bf16[256,640]{1,0:T(8,128)(2,1)S(1)}, bf16[256,640]{1,0:T(8,128)(2,1)S(1)}, u32[]{:S(2)}, u32[]{:S(2)}) %collective-permute-start.19) | collective-permute-done | bytes 327712 | tf_op jit(solution)/shard_map/cond/branch_1_fun/ppermute | solution.py:174
  67.4 1.6 %collective-permute-start.27 = (bf16[416,640]{1,0:T(8,128)(2,1)S(1)}, bf16[416,640]{1,0:T(8,128)(2,1)S(1)}, u32[]{:S(2)}, u32[]{:S(2)}) collective-permute-start(bf16[416,640]{1,0:T(8,128)(2,1)S(1)} %pack_part.6.refs_7_.refs_3_), channel_id=1, source_target_pairs={{0,16},{8,24},{16,0},{24,8},{1,17},{9,25},{17,1},{25,9},{2,18},{10... | collective-permute-start | bytes 1597448 | tf_op jit(solution)/shard_map/cond/branch_1_fun/ppermute | solution.py:174
  69.0 1.6 %collective-permute-start.25 = (bf16[416,640]{1,0:T(8,128)(2,1)S(1)}, bf16[416,640]{1,0:T(8,128)(2,1)S(1)}, u32[]{:S(2)}, u32[]{:S(2)}) collective-permute-start(bf16[416,640]{1,0:T(8,128)(2,1)S(1)} %pack_part.6.refs_7_.refs_3_), channel_id=1, source_target_pairs={{0,8},{8,0},{16,24},{24,16},{1,9},{9,1},{17,25},{25,17},{2,10},{10... | collective-permute-start | bytes 1597448 | tf_op jit(solution)/shard_map/cond/branch_1_fun/ppermute | solution.py:174
  70.5 6.8 %collective-permute-start.21 = (bf16[416,768]{1,0:T(8,128)(2,1)S(1)}, bf16[416,768]{1,0:T(8,128)(2,1)S(1)}, u32[]{:S(2)}, u32[]{:S(2)}) collective-permute-start(bf16[416,768]{1,0:T(8,128)(2,1)S(1)} %collective-permute-done.17.refs_4_), channel_id=1, source_target_pairs={{0,2},{1,3},{2,0},{3,1},{4,6},{5,7},{6,4},{7,5},{8,10},{9,11},{10,... | collective-permute-start | bytes 1916936 | tf_op jit(solution)/shard_map/cond/branch_1_fun/ppermute | solution.py:174
  77.4 2.7 %collective-permute-done.27.refs_11_.refs_7_ = bf16[416,640]{1,0:T(8,128)(2,1)S(1)} collective-permute-done((bf16[416,640]{1,0:T(8,128)(2,1)S(1)}, bf16[416,640]{1,0:T(8,128)(2,1)S(1)}, u32[]{:S(2)}, u32[]{:S(2)}) %collective-permute-start.27) | collective-permute-done | bytes 532512 | tf_op jit(solution)/shard_map/cond/branch_1_fun/ppermute | solution.py:174
  80.1 3.5 %collective-permute-done.31.refs_2_ = bf16[416,768]{1,0:T(8,128)(2,1)S(1)} collective-permute-done((bf16[416,768]{1,0:T(8,128)(2,1)S(1)}, bf16[416,768]{1,0:T(8,128)(2,1)S(1)}, u32[]{:S(2)}, u32[]{:S(2)}) %collective-permute-start.31) | collective-permute-done | bytes 639008 | tf_op jit(solution)/shard_map/cond/branch_1_fun/ppermute | solution.py:174
  83.5 1.5 %collective-permute-start.28 = (bf16[416,640]{1,0:T(8,128)(2,1)S(1)}, bf16[416,640]{1,0:T(8,128)(2,1)S(1)}, u32[]{:S(2)}, u32[]{:S(2)}) collective-permute-start(bf16[416,640]{1,0:T(8,128)(2,1)S(1)} %collective-permute-done.24.refs_8_.refs_4_), channel_id=1, source_target_pairs={{0,16},{8,24},{16,0},{24,8},{1,17},{9,25},{17,1},{25,9},{2,18},{10... | collective-permute-start | bytes 1597448 | tf_op jit(solution)/shard_map/cond/branch_1_fun/ppermute | solution.py:174
  85.1 1.5 %collective-permute-start.29 = (bf16[416,640]{1,0:T(8,128)(2,1)S(1)}, bf16[416,640]{1,0:T(8,128)(2,1)S(1)}, u32[]{:S(2)}, u32[]{:S(2)}) collective-permute-start(bf16[416,640]{1,0:T(8,128)(2,1)S(1)} %collective-permute-done.27.refs_11_.refs_7_), channel_id=1, source_target_pairs={{0,8},{8,0},{16,24},{24,16},{1,9},{9,1},{17,25},{25,17},{2,10},{10... | collective-permute-start | bytes 1597448 | tf_op jit(solution)/shard_map/cond/branch_1_fun/ppermute | solution.py:174
  86.6 8.3 %collective-permute-done.21.refs_0_ = bf16[416,768]{1,0:T(8,128)(2,1)S(1)} collective-permute-done((bf16[416,768]{1,0:T(8,128)(2,1)S(1)}, bf16[416,768]{1,0:T(8,128)(2,1)S(1)}, u32[]{:S(2)}, u32[]{:S(2)}) %collective-permute-start.21) | collective-permute-done | bytes 639008 | tf_op jit(solution)/shard_map/cond/branch_1_fun/ppermute | solution.py:174
  94.9 3.2 %collective-permute-done.28.refs_12_.refs_8_ = bf16[416,640]{1,0:T(8,128)(2,1)S(1)} collective-permute-done((bf16[416,640]{1,0:T(8,128)(2,1)S(1)}, bf16[416,640]{1,0:T(8,128)(2,1)S(1)}, u32[]{:S(2)}, u32[]{:S(2)}) %collective-permute-start.28) | collective-permute-done | bytes 532512 | tf_op jit(solution)/shard_map/cond/branch_1_fun/ppermute | solution.py:174
  98.1 1.2 %collective-permute-done.29.refs_13_.refs_9_ = bf16[416,640]{1,0:T(8,128)(2,1)S(1)} collective-permute-done((bf16[416,640]{1,0:T(8,128)(2,1)S(1)}, bf16[416,640]{1,0:T(8,128)(2,1)S(1)}, u32[]{:S(2)}, u32[]{:S(2)}) %collective-permute-start.29) | collective-permute-done | bytes 532512 | tf_op jit(solution)/shard_map/cond/branch_1_fun/ppermute | solution.py:174
  100.1 7.6 %contract_first.3.refs_10_ = f32[768,640]{1,0:T(8,128)} custom-call(s32[128]{0:T(128)S(1)} %copy-done.10, s32[48]{0:T(128)S(1)} %copy-done.16, bf16[416,768]{1,0:T(8,128)(2,1)S(1)} %pack_density.3.refs_0_, bf16[416,768]{1,0:T(8,128)(2,1)S(1)} %collective-permute-done.30.refs_1_, bf16[416,768]{1,0:T(8,128)(2,1)S(1)} %collective-permute-done.31.refs_2_, ...), custom_call_target="tpu_custom_call" | custom-call | flops 2453667840 | bytes 7028736 | tf_op jit(solution)/shard_map/cond/branch_1_fun/contract_first/pallas_call | solution.py:256
  107.7 6.9 %contract_last.3 = bf16[1024,768]{1,0:T(8,128)(2,1)} custom-call(s32[128]{0:T(128)S(1)} %copy-done.10, s32[48]{0:T(128)S(1)} %copy-done.16, bf16[416,768]{1,0:T(8,128)(2,1)S(1)} %collective-permute-done.21.refs_0_, bf16[416,768]{1,0:T(8,128)(2,1)S(1)} %collective-permute-done.22.refs_1_, bf16[416,640]{1,0:T(8,128)(2,1)S(1)} %pack_part.7.refs_6_.refs_2_, ...), custom_call_target="tpu_custom_call" | custom-call | flops 817889280 | bytes 2342912 | tf_op jit(solution)/shard_map/cond/branch_1_fun/contract_last/pallas_call | solution.py:256
  (38 shorter events, 4.1 us)
Async XLA Ops:
  2.2 3.7 %copy-start.14 = (s32[32,16]{0,1:T(8,128)S(1)}, s32[32,16]{0,1:T(8,128)}, u32[]{:S(2)}) copy-start(s32[32,16]{0,1:T(8,128)} %get-tuple-element.66) | copy-start | bytes 6148 | tf_op jit(solution)/shard_map/cond
  2.2 3.7 %copy-start.10 = (s32[128]{0:T(128)S(1)}, s32[128]{0:T(128)}, u32[]{:S(2)}) copy-start(s32[128]{0:T(128)} %get-tuple-element.45.count_ref) | copy-start | bytes 1540 | tf_op jit(solution)/shard_map/cond
  2.2 3.7 %copy-start.18 = (bf16[1024,512]{1,0:T(8,128)(2,1)S(1)}, bf16[1024,512]{1,0:T(8,128)(2,1)}, u32[]{:S(2)}) copy-start(bf16[1024,512]{1,0:T(8,128)(2,1)} %get-tuple-element.48.x_ref) | copy-start | bytes 3145732 | tf_op jit(solution)/shard_map/cond
  5.4 3.0 %collective-permute-start.18 = (bf16[4,128,640]{2,1,0:T(8,128)(2,1)S(1)}, bf16[4,128,640]{2,1,0:T(8,128)(2,1)S(1)}, u32[]{:S(2)}, u32[]{:S(2)}) collective-permute-start(bf16[4,128,640]{2,1,0:T(8,128)(2,1)S(1)} %pack_other_core.3), channel_id=1, source_target_pairs={{0,1},{1,0},{2,3},{3,2},{4,5},{5,4},{6,7},{7,6},{8,9},{9,8},{10,11... | collective-permute-start | bytes 1966088 | tf_op jit(solution)/shard_map/cond/branch_1_fun/ppermute | solution.py:174
  6.0 2.4 %copy-start.12 = (s32[4,48]{1,0:T(4,128)S(1)}, s32[4,48]{1,0:T(4,128)}, u32[]{:S(2)}) copy-start(s32[4,48]{1,0:T(4,128)} %get-tuple-element.49.mask_ref) | copy-start | bytes 2308 | tf_op jit(solution)/shard_map/cond
  6.0 2.4 %copy-start.16 = (s32[48]{0:T(128)S(1)}, s32[48]{0:T(128)}, u32[]{:S(2)}) copy-start(s32[48]{0:T(128)} %get-tuple-element.46.ri_ref) | copy-start | bytes 580 | tf_op jit(solution)/shard_map/cond
  10.6 17.9 %collective-permute-start.23 = (bf16[256,640]{1,0:T(8,128)(2,1)S(1)}, bf16[256,640]{1,0:T(8,128)(2,1)S(1)}, u32[]{:S(2)}, u32[]{:S(2)}) collective-permute-start(bf16[256,640]{1,0:T(8,128)(2,1)S(1)} %get-tuple-element.56), channel_id=1, source_target_pairs={{0,2},{1,3},{2,0},{3,1},{4,6},{5,7},{6,4},{7,5},{8,10},{9,11},{10,... | collective-permute-start | bytes 983048 | tf_op jit(solution)/shard_map/cond/branch_1_fun/ppermute | solution.py:174
  13.3 55.6 %collective-permute-start.17 = (bf16[416,768]{1,0:T(8,128)(2,1)S(1)}, bf16[416,768]{1,0:T(8,128)(2,1)S(1)}, u32[]{:S(2)}, u32[]{:S(2)}) collective-permute-start(bf16[416,768]{1,0:T(8,128)(2,1)S(1)} %pack_density.3.refs_0_), channel_id=1, source_target_pairs={{0,4},{1,5},{2,6},{3,7},{4,0},{5,1},{6,2},{7,3},{8,12},{9,13},{10,... | collective-permute-start | bytes 1916936 | tf_op jit(solution)/shard_map/cond/branch_1_fun/ppermute | solution.py:174
  15.9 50.3 %collective-permute-start.19 = (bf16[256,640]{1,0:T(8,128)(2,1)S(1)}, bf16[256,640]{1,0:T(8,128)(2,1)S(1)}, u32[]{:S(2)}, u32[]{:S(2)}) collective-permute-start(bf16[256,640]{1,0:T(8,128)(2,1)S(1)} %get-tuple-element.52), channel_id=1, source_target_pairs={{0,4},{1,5},{2,6},{3,7},{4,0},{5,1},{6,2},{7,3},{8,12},{9,13},{10,... | collective-permute-start | bytes 983048 | tf_op jit(solution)/shard_map/cond/branch_1_fun/ppermute | solution.py:174
  29.7 39.3 %collective-permute-start.26 = (bf16[416,640]{1,0:T(8,128)(2,1)S(1)}, bf16[416,640]{1,0:T(8,128)(2,1)S(1)}, u32[]{:S(2)}, u32[]{:S(2)}) collective-permute-start(bf16[416,640]{1,0:T(8,128)(2,1)S(1)} %pack_part.7.refs_6_.refs_2_), channel_id=1, source_target_pairs={{0,16},{8,24},{16,0},{24,8},{1,17},{9,25},{17,1},{25,9},{2,18},{10... | collective-permute-start | bytes 1597448 | tf_op jit(solution)/shard_map/cond/branch_1_fun/ppermute | solution.py:174
  31.4 39.1 %collective-permute-start.24 = (bf16[416,640]{1,0:T(8,128)(2,1)S(1)}, bf16[416,640]{1,0:T(8,128)(2,1)S(1)}, u32[]{:S(2)}, u32[]{:S(2)}) collective-permute-start(bf16[416,640]{1,0:T(8,128)(2,1)S(1)} %pack_part.7.refs_6_.refs_2_), channel_id=1, source_target_pairs={{0,8},{8,0},{16,24},{24,16},{1,9},{9,1},{17,25},{25,17},{2,10},{10... | collective-permute-start | bytes 1597448 | tf_op jit(solution)/shard_map/cond/branch_1_fun/ppermute | solution.py:174
  32.9 33.3 %collective-permute-start.20 = (bf16[256,640]{1,0:T(8,128)(2,1)S(1)}, bf16[256,640]{1,0:T(8,128)(2,1)S(1)}, u32[]{:S(2)}, u32[]{:S(2)}) collective-permute-start(bf16[256,640]{1,0:T(8,128)(2,1)S(1)} %get-tuple-element.53), channel_id=1, source_target_pairs={{0,6},{1,7},{2,4},{3,5},{4,2},{5,3},{6,0},{7,1},{8,14},{9,15},{10,... | collective-permute-start | bytes 983048 | tf_op jit(solution)/shard_map/cond/branch_1_fun/ppermute | solution.py:174
  66.2 17.3 %collective-permute-start.31 = (bf16[416,768]{1,0:T(8,128)(2,1)S(1)}, bf16[416,768]{1,0:T(8,128)(2,1)S(1)}, u32[]{:S(2)}, u32[]{:S(2)}) collective-permute-start(bf16[416,768]{1,0:T(8,128)(2,1)S(1)} %pack_density.3.refs_0_), channel_id=1, source_target_pairs={{0,2},{1,3},{2,0},{3,1},{4,6},{5,7},{6,4},{7,5},{8,10},{9,11},{10,... | collective-permute-start | bytes 1916936 | tf_op jit(solution)/shard_map/cond/branch_1_fun/ppermute | solution.py:174
  67.4 12.7 %collective-permute-start.27 = (bf16[416,640]{1,0:T(8,128)(2,1)S(1)}, bf16[416,640]{1,0:T(8,128)(2,1)S(1)}, u32[]{:S(2)}, u32[]{:S(2)}) collective-permute-start(bf16[416,640]{1,0:T(8,128)(2,1)S(1)} %pack_part.6.refs_7_.refs_3_), channel_id=1, source_target_pairs={{0,16},{8,24},{16,0},{24,8},{1,17},{9,25},{17,1},{25,9},{2,18},{10... | collective-permute-start | bytes 1597448 | tf_op jit(solution)/shard_map/cond/branch_1_fun/ppermute | solution.py:174
  68.9 30.4 %copy-start.6 = (bf16[416,768]{1,0:T(8,128)(2,1)}, bf16[416,768]{1,0:T(8,128)(2,1)S(1)}, u32[]{:S(2)}) copy-start(bf16[416,768]{1,0:T(8,128)(2,1)S(1)} %collective-permute-done.17.refs_4_) | copy-start | bytes 1916932 | tf_op jit(solution)/shard_map/cond
  68.9 16.1 %collective-permute-start.30 = (bf16[416,768]{1,0:T(8,128)(2,1)S(1)}, bf16[416,768]{1,0:T(8,128)(2,1)S(1)}, u32[]{:S(2)}, u32[]{:S(2)}) collective-permute-start(bf16[416,768]{1,0:T(8,128)(2,1)S(1)} %pack_density.3.refs_0_), channel_id=1, source_target_pairs={{0,1},{1,0},{2,3},{3,2},{4,5},{5,4},{6,7},{7,6},{8,9},{9,8},{10,11... | collective-permute-start | bytes 1916936 | tf_op jit(solution)/shard_map/cond/branch_1_fun/ppermute | solution.py:174
  69.0 14.6 %collective-permute-start.25 = (bf16[416,640]{1,0:T(8,128)(2,1)S(1)}, bf16[416,640]{1,0:T(8,128)(2,1)S(1)}, u32[]{:S(2)}, u32[]{:S(2)}) collective-permute-start(bf16[416,640]{1,0:T(8,128)(2,1)S(1)} %pack_part.6.refs_7_.refs_3_), channel_id=1, source_target_pairs={{0,8},{8,0},{16,24},{24,16},{1,9},{9,1},{17,25},{25,17},{2,10},{10... | collective-permute-start | bytes 1597448 | tf_op jit(solution)/shard_map/cond/branch_1_fun/ppermute | solution.py:174
  70.5 24.3 %collective-permute-start.21 = (bf16[416,768]{1,0:T(8,128)(2,1)S(1)}, bf16[416,768]{1,0:T(8,128)(2,1)S(1)}, u32[]{:S(2)}, u32[]{:S(2)}) collective-permute-start(bf16[416,768]{1,0:T(8,128)(2,1)S(1)} %collective-permute-done.17.refs_4_), channel_id=1, source_target_pairs={{0,2},{1,3},{2,0},{3,1},{4,6},{5,7},{6,4},{7,5},{8,10},{9,11},{10,... | collective-permute-start | bytes 1916936 | tf_op jit(solution)/shard_map/cond/branch_1_fun/ppermute | solution.py:174
  80.1 14.8 %collective-permute-start.33 = (bf16[416,768]{1,0:T(8,128)(2,1)S(1)}, bf16[416,768]{1,0:T(8,128)(2,1)S(1)}, u32[]{:S(2)}, u32[]{:S(2)}) collective-permute-start(bf16[416,768]{1,0:T(8,128)(2,1)S(1)} %collective-permute-done.17.refs_4_), channel_id=1, source_target_pairs={{0,1},{1,0},{2,3},{3,2},{4,5},{5,4},{6,7},{7,6},{8,9},{9,8},{10,11... | collective-permute-start | bytes 1916936 | tf_op jit(solution)/shard_map/cond/branch_1_fun/ppermute | solution.py:174
  83.5 15.8 %collective-permute-start.32 = (bf16[416,768]{1,0:T(8,128)(2,1)S(1)}, bf16[416,768]{1,0:T(8,128)(2,1)S(1)}, u32[]{:S(2)}, u32[]{:S(2)}) collective-permute-start(bf16[416,768]{1,0:T(8,128)(2,1)S(1)} %collective-permute-done.31.refs_2_), channel_id=1, source_target_pairs={{0,1},{1,0},{2,3},{3,2},{4,5},{5,4},{6,7},{7,6},{8,9},{9,8},{10,11... | collective-permute-start | bytes 1916936 | tf_op jit(solution)/shard_map/cond/branch_1_fun/ppermute | solution.py:174
  83.5 14.5 %collective-permute-start.28 = (bf16[416,640]{1,0:T(8,128)(2,1)S(1)}, bf16[416,640]{1,0:T(8,128)(2,1)S(1)}, u32[]{:S(2)}, u32[]{:S(2)}) collective-permute-start(bf16[416,640]{1,0:T(8,128)(2,1)S(1)} %collective-permute-done.24.refs_8_.refs_4_), channel_id=1, source_target_pairs={{0,16},{8,24},{16,0},{24,8},{1,17},{9,25},{17,1},{25,9},{2,18},{10... | collective-permute-start | bytes 1597448 | tf_op jit(solution)/shard_map/cond/branch_1_fun/ppermute | solution.py:174
  85.1 14.2 %collective-permute-start.29 = (bf16[416,640]{1,0:T(8,128)(2,1)S(1)}, bf16[416,640]{1,0:T(8,128)(2,1)S(1)}, u32[]{:S(2)}, u32[]{:S(2)}) collective-permute-start(bf16[416,640]{1,0:T(8,128)(2,1)S(1)} %collective-permute-done.27.refs_11_.refs_7_), channel_id=1, source_target_pairs={{0,8},{8,0},{16,24},{24,16},{1,9},{9,1},{17,25},{25,17},{2,10},{10... | collective-permute-start | bytes 1597448 | tf_op jit(solution)/shard_map/cond/branch_1_fun/ppermute | solution.py:174
  94.8 12.9 %collective-permute-start.22 = (bf16[416,768]{1,0:T(8,128)(2,1)S(1)}, bf16[416,768]{1,0:T(8,128)(2,1)S(1)}, u32[]{:S(2)}, u32[]{:S(2)}) collective-permute-start(bf16[416,768]{1,0:T(8,128)(2,1)S(1)} %collective-permute-done.21.refs_0_), channel_id=1, source_target_pairs={{0,1},{1,0},{2,3},{3,2},{4,5},{5,4},{6,7},{7,6},{8,9},{9,8},{10,11... | collective-permute-start | bytes 1916936 | tf_op jit(solution)/shard_map/cond/branch_1_fun/ppermute | solution.py:174
  94.8 4.5 %copy-start.7 = (bf16[416,768]{1,0:T(8,128)(2,1)}, bf16[416,768]{1,0:T(8,128)(2,1)S(1)}, u32[]{:S(2)}) copy-start(bf16[416,768]{1,0:T(8,128)(2,1)S(1)} %collective-permute-done.33.refs_5_) | copy-start | bytes 1916932 | tf_op jit(solution)/shard_map/cond
  (2 other events, 3.3 us)

commit v5 on v4

--- a/solution.py
+++ b/solution.py
@@ -124,17 +124,17 @@
         row, col = lax.axis_index("row"), lax.axis_index("col")
         keep = keep_mask(BW, BW, mask_ref[...], rows, cols)
         x = jnp.where(keep > 0.5, x_ref[...].astype(F32), 0.0).astype(BF16)
-        left = pack_rows(count_ref, col * sum_atoms, sum_atoms, BW, sum_size)
-        x = lax.dot_general(left, x, (((1,), (1,)), ((), ())), preferred_element_type=F32).astype(BF16)
-        pack_cols(count_ref, row * lam_atoms, lam_atoms, BW, lam_size, hot)
-        o_ref[...] = jnp.dot(x, hot[...], preferred_element_type=F32).astype(BF16)
-
-    return pl.pallas_call(
-        body,
-        out_shape=jax.ShapeDtypeStruct((sum_size, lam_size), BF16),
+        pack_cols(count_ref, col * sum_atoms, sum_atoms, BW, sum_size, hot)
+        x = jnp.dot(x, hot[...], preferred_element_type=F32).astype(BF16)
+        left = pack_rows(count_ref, row * lam_atoms, lam_atoms, BW, lam_size)
+        o_ref[...] = jnp.dot(left, x, preferred_element_type=F32).astype(BF16)
+
+    return pl.pallas_call(
+        body,
+        out_shape=jax.ShapeDtypeStruct((lam_size, sum_size), BF16),
         in_specs=[SMEM_SPEC, VMEM_SPEC, VMEM_SPEC],
         out_specs=VMEM_SPEC,
-        scratch_shapes=[pltpu.VMEM((rows, lam_size), BF16)],
+        scratch_shapes=[pltpu.VMEM((cols, sum_size), BF16)],
         compiler_params=params(),
         cost_estimate=cost(2 * rows * sum_size * (cols + lam_size), 2 * rows * cols),
         name="pack_density",
@@ -164,7 +164,7 @@
         out_specs=VMEM_SPEC,
         scratch_shapes=[pltpu.VMEM((depth, cols), BF16)],
         compiler_params=params(),
-        cost_estimate=cost(2 * size * depth * cols, 2 * cols * (depth + size)),
+        cost_estimate=cost((2 + 10 * first) * size * depth * cols, 2 * cols * (depth + size)),
         name="pack_part",
     )(basis_count, *pieces)
 
@@ -172,6 +172,10 @@
 def exchange(x, axis, bit):
     peers = lax.axis_size(axis)
     return lax.ppermute(x, axis, [(i, i ^ bit) for i in range(peers)])
+
+
+def after(x, *others):
+    return lax.optimization_barrier((x, *others))[0]
 
 
 def double(own, axis, bits):
@@ -183,8 +187,8 @@
 
 
 def contract(dens, integrals, basis_count, ri_count, ncols, rows, wide, before=None):
-    keys = sorted(dens)
-    depth, lam = dens[keys[0]].shape
+    keys = list(dens)
+    lam, depth = dens[keys[0]].shape
     cols = integrals[0][0].shape[1]
     groups, nrows = len(integrals), len(integrals[0])
     parts = groups * nrows
@@ -192,55 +196,53 @@
     halves = [(far, g) for far in range(nrows) for g in range(groups)]
     last = before is not None
     tile = 256
+    n = len(keys)
 
     def body(count_ref, ri_ref, *refs):
-        d_refs, refs = refs[: len(keys)], refs[len(keys):]
+        d_refs, refs = refs[:n], refs[n:]
         s_refs, refs = refs[: len(halves)], refs[len(halves):]
         if last:
             before_ref, o_ref, d_all, s_all, d_sem, s_sem, b_sem, total, packed, lam_hot, col_hot = refs
-            pltpu.make_async_copy(before_ref, total, b_sem).start()
+            begin = pltpu.make_async_copy(before_ref, total, b_sem)
+            begin.start()
         else:
-            o_ref, d_all, s_all, d_sem, s_sem = refs
+            total, d_all, s_all, d_sem, s_sem = refs
         row, col = lax.axis_index("row"), lax.axis_index("col")
-
-        def place(i):
-            return pl.ds(i * depth, depth)
-
         for i, far in enumerate(keys):
-            pltpu.make_async_copy(d_refs[i], d_all.at[place(i), :], d_sem.at[i]).start()
             part = col ^ far
             for j, (away, g) in enumerate(halves):
 
                 @pl.when(part == (row ^ away) * groups + (col // (ncols // groups) ^ g))
                 def _():
-                    pltpu.make_async_copy(s_refs[j], s_all.at[place(i), :], s_sem.at[i]).start()
+                    pltpu.make_async_copy(s_refs[j], s_all.at[i], s_sem.at[i]).start()
+
+            pltpu.make_async_copy(d_refs[i], d_all.at[i], d_sem.at[i]).start()
 
         if last:
             pack_cols(count_ref, row * lam_atoms, lam_atoms, BW, lam, lam_hot)
             col_hot[...] = pack_rows(ri_ref, col * blocks, blocks, RW, cols)
-            pltpu.make_async_copy(before_ref, total, b_sem).wait()
-        for i in range(len(keys)):
-            pltpu.make_async_copy(d_refs[i], d_all.at[place(i), :], d_sem.at[i]).wait()
-            pltpu.make_async_copy(s_refs[0], s_all.at[place(i), :], s_sem.at[i]).wait()
-        for at in range(0, lam, tile):
-            x = lax.dot_general(
-                d_all[:, pl.ds(at, tile)], s_all[...], (((0,), (0,)), ((), ())), preferred_element_type=F32
-            )
-            if last:
-                x = (x + total[pl.ds(at, tile), :]).astype(BF16)
-                packed[pl.ds(at, tile), :] = jnp.dot(x, col_hot[...], preferred_element_type=F32).astype(BF16)
-            else:
-                o_ref[pl.ds(at, tile), :] = x
+            begin.wait()
+        for i in range(n):
+            pltpu.make_async_copy(s_refs[0], s_all.at[i], s_sem.at[i]).wait()
+            pltpu.make_async_copy(d_refs[i], d_all.at[i], d_sem.at[i]).wait()
+            for at in range(0, lam, tile):
+                x = jnp.dot(d_all[i, pl.ds(at, tile), :], s_all[i], preferred_element_type=F32)
+                if i > 0 or last:
+                    x = x + total[pl.ds(at, tile), :]
+                if last and i == n - 1:
+                    x = x.astype(BF16)
+                    packed[pl.ds(at, tile), :] = jnp.dot(x, col_hot[...], preferred_element_type=F32).astype(BF16)
+                else:
+                    total[pl.ds(at, tile), :] = x
         if last:
             for at in range(0, rows, tile):
                 o_ref[pl.ds(at, tile), :] = jnp.dot(
                     lam_hot[pl.ds(at, tile), :], packed[...], preferred_element_type=F32
                 ).astype(BF16)
 
-    n = len(keys)
     scratch = [
-        pltpu.VMEM((n * depth, lam), BF16),
-        pltpu.VMEM((n * depth, cols), BF16),
+        pltpu.VMEM((n, lam, depth), BF16),
+        pltpu.VMEM((n, depth, cols), BF16),
         pltpu.SemaphoreType.DMA((n,)),
         pltpu.SemaphoreType.DMA((n,)),
     ]
@@ -281,20 +283,21 @@
         row_bits = [1 << b for b in range(nrows.bit_length() - 1)]
         chip_bits = [CORES << b for b in range(chips.bit_length() - 1)][::-1]
 
-        own = pack_density(density, density_mask, basis_count, lam_size, sum_size)
         counts = (block_mask, basis_count, ri_count, ncols, col_size)
         other = exchange(pack_integrals(three_center, *counts), "col", 1)
-        line = {0: own, chip_bits[0]: exchange(own, "col", chip_bits[0])}
-        other, _ = lax.optimization_barrier((other, own))
-        pieces = pack_integrals(three_center, *counts, other)
+        own = pack_density(density, density_mask, basis_count, lam_size, sum_size)
+        pieces = pack_integrals(three_center, *counts, after(other, own))
         got = [pieces[0]] + [exchange(pieces[t], "col", CORES * t) for t in range(1, chips)]
         per = depth // pieces[0].shape[0]
         parts, groups = [], []
         for g in range(chips // per):
-            parts.append(pack_part(got[g * per : (g + 1) * per], basis_count, g * per, ncols, sum_size))
-            groups.append(double(parts[g], "row", row_bits if g % 2 == 0 else row_bits[::-1]))
-        for far in list(line):
-            line[far], _ = lax.optimization_barrier((line[far], parts[0] if far == 0 else parts[-1]))
+            part = pack_part(got[g * per : (g + 1) * per], basis_count, g * per, ncols, sum_size)
+            if g > 0:
+                part = after(part, *[groups[0][bit] for bit in row_bits])
+            parts.append(part)
+            groups.append(double(part, "row", row_bits if g % 2 == 0 else row_bits[::-1]))
+        own = after(own, parts[-1])
+        line = {0: own, chip_bits[0]: exchange(own, "col", chip_bits[0])}
         for bit in chip_bits[1:]:
             for far in sorted(line):
                 line[far | bit] = exchange(line[far], "col", bit)
@@ -309,24 +312,27 @@
     return run
 
 
-def all_fit(basis_count, ri_count, limits):
+def first_fit(basis_count, ri_count, groups, levels):
     def body(count_ref, ri_ref, o_ref):
-        fits = jnp.int32(1)
-        for ref, groups, limit in ((count_ref, *limits[0]), (count_ref, *limits[1]), (ri_ref, *limits[2])):
-            per = ref.shape[0] // groups
-            for g in range(groups):
+        level = jnp.int32(0)
+        for axis, (ref, parts) in enumerate(zip((count_ref, count_ref, ri_ref), groups)):
+            per = ref.shape[0] // parts
+            most = jnp.int32(0)
+            for g in range(parts):
                 total = jnp.int32(0)
                 for i in range(per):
                     total = total + ref[g * per + i]
-                fits = jnp.where(total > limit, 0, fits)
-        o_ref[0] = fits
+                most = jnp.maximum(most, total)
+            for n, sizes in enumerate(levels[:-1]):
+                level = jnp.where(most > sizes[axis], jnp.maximum(level, n + 1), level)
+        o_ref[0] = level
 
     return pl.pallas_call(
         body,
         out_shape=jax.ShapeDtypeStruct((1,), jnp.int32),
         in_specs=[SMEM_SPEC, SMEM_SPEC],
         out_specs=SMEM_SPEC,
-        name="all_fit",
+        name="first_fit",
     )(basis_count, ri_count)
 
 
@@ -335,12 +341,14 @@
     nrows = lax.axis_size("row")
     rows, depth = density.shape
     wide = three_center.shape[1] // ncols
-    lam_size, sum_size, col_size = rows * 3 // 4, depth * 13 // 16, wide * 5 // 6
-    fits = all_fit(basis_count, ri_count, ((nrows, lam_size), (ncols, sum_size), (ncols, col_size)))
+    levels = (
+        (rows * 3 // 4, depth * 3 // 4, wide * 5 // 6),
+        (rows * 3 // 4, depth, wide),
+        (rows, depth, wide),
+    )
+    level = first_fit(basis_count, ri_count, (nrows, ncols, ncols), levels)
     args = (three_center, density, block_mask, density_mask, basis_count, ri_count)
-    return lax.cond(
-        fits[0] > 0, program(lam_size, sum_size, col_size), program(rows, depth, wide), *args
-    )
+    return lax.switch(level[0], [program(*sizes) for sizes in levels], *args)
 
 
 def solution(mesh):

time: 117 us -> 106 us (0.906); the launches traced: 115 us -> 106 us
  starting transfers between devices: 24.8 us -> 18.8 us
  waiting for transfers between devices: 62.1 us -> 56.5 us
  Pallas kernels: 25.8 us -> 27.6 us
    ppermute x17, starting transfers between devices: 24.8 us -> 18.8 us  [exchange(): return lax.ppermute(x, axis, [(i, i ^ bit) for i in range(peers)])]
    ppermute x17, waiting for transfers between devices: 62.1 us -> 56.5 us  [exchange(): return lax.ppermute(x, axis, [(i, i ^ bit) for i in range(peers)])]
    pallas_call x2, Pallas kernels: 14.5 us -> 16.2 us  [contract(): pl.pallas_call(body, out_shape=out, in_specs=[SMEM_SPEC, SMEM_SPEC] + [AN...]
  transfers between devices with their start and end apart: 17 -> 17, of which waited for: 7 -> 8; matrix products, arithmetic and copies ran while one was open for 0% -> 0% of each run, Pallas kernels for 11% -> 13%
where the time goes in v5:
time: 106 us
  waiting for transfers between devices  56.5 us (53%)
  Pallas kernels  27.6 us (26%)
  starting transfers between devices  18.8 us (18%)
  local copies, waits for them, and re-layouts  1.72 us (2%)
    ppermute x17, waiting for transfers between devices, exchange(): return lax.ppermute(x, axis, [(i, i ^ bit) for i in range(peers)])  56.5 us
    ppermute x17, starting transfers between devices, exchange(): return lax.ppermute(x, axis, [(i, i ^ bit) for i in range(peers)])  18.8 us
    pallas_call x2, Pallas kernels, contract(): pl.pallas_call(body, out_shape=out, in_specs=[SMEM_SPEC, SMEM_SPEC] + [AN...  16.2 us
    pallas_call x2, Pallas kernels, pack_integrals(): pl.pallas_call(body, out_shape=shape if first else [merged] * chips, in_s...  5.32 us
    pallas_call x1, Pallas kernels, pack_density(): pl.pallas_call(body, out_shape=jax.ShapeDtypeStruct((lam_size, sum_size),...  2.55 us
    pallas_call x2, Pallas kernels, pack_part(): pl.pallas_call(body, out_shape=jax.ShapeDtypeStruct((size, cols), BF16),...  2.25 us
  transfers between devices with their start and end apart: 17, of which 8 were waited for; matrix products, arithmetic and copies ran while one was open for 0% of the time, Pallas kernels for 13%

profile of v5, /device:TPU:0, one launch (start us, length us, event | category | flops | bytes accessed | tf_op | source)
XLA Modules:
  0.0 106.2 jit_solution(2740525906346009544)
XLA Ops:
  0.0 1.3 %first_fit.1 = s32[1]{0:T(128)} custom-call(s32[128]{0:T(128)} %count_ref.1, s32[48]{0:T(128)} %ri_ref.1), custom_call_target="tpu_custom_call" | custom-call | tf_op jit(solution)/shard_map/first_fit/pallas_call | solution.py:330
  2.0 104.0 %conditional.1 = (bf16[1024,768]{1,0:T(8,128)(2,1)}) conditional(s32[]{:T(128)} %bitcast, (s32[128]{0:T(128)}, s32[32,16]{0,1:T(8,128)}, bf16[1024,512]{1,0:T(8,128)(2,1)}, s32[48]{0:T(128)}, s32[4,48]{1,0:T(4,128)}, /*index=5*/bf16[128,6144]{1,0:T(8,128)(2,1)}) %tuple.23, (s32[128]{0:T(128)}, s32[32,16]{0,1:T(8,128)}, ...), branch_computations={%region_0.0_spmd, %region_1.0_spmd, %region_2.0_spmd} | conditional | flops 14092861440 | bytes 126110544 | solution.py:351
  2.0 3.1 %pack_other_core.3 = bf16[4,128,640]{2,1,0:T(8,128)(2,1)S(1)} custom-call(s32[128]{0:T(128)} %get-tuple-element.44.count_ref, s32[48]{0:T(128)} %get-tuple-element.46.ri_ref, s32[4,48]{1,0:T(4,128)} %get-tuple-element.49.mask_ref, bf16[128,6144]{1,0:T(8,128)(2,1)} %get-tuple-element.50.x_ref), custom_call_target="tpu_custom_call" | custom-call | flops 503316480 | bytes 1769472 | tf_op jit(solution)/shard_map/cond/branch_0_fun/pack_other_core/pallas_call | solution.py:107
  5.8 2.5 %pack_density.3.refs_0_ = bf16[768,384]{1,0:T(8,128)(2,1)S(1)} custom-call(s32[128]{0:T(128)S(1)} %copy-done.21, s32[32,16]{1,0:T(8,128)S(1)} %copy.10.mask_ref, bf16[1024,512]{1,0:T(8,128)(2,1)S(1)} %copy-done.33), custom_call_target="tpu_custom_call" | custom-call | flops 1006632960 | bytes 1048576 | tf_op jit(solution)/shard_map/cond/branch_0_fun/pack_density/pallas_call | solution.py:132
  8.4 2.2 %pack_own_core.3 = (bf16[256,640]{1,0:T(8,128)(2,1)S(1)}, bf16[256,640]{1,0:T(8,128)(2,1)S(1)}, bf16[256,640]{1,0:T(8,128)(2,1)S(1)}, bf16[256,640]{1,0:T(8,128)(2,1)S(1)}) custom-call(s32[128]{0:T(128)S(1)} %copy-done.21, s32[48]{0:T(128)S(1)} %copy-done.30, s32[4,48]{1,0:T(4,128)S(1)} %copy-done.24, bf16[128,6144]{1,0:T(8,128)(2,1)S(1)} %copy-done.9, ...), custom_call_target="tpu_custom_call" | custom-call | flops 503316480 | bytes 1769472 | tf_op jit(solution)/shard_map/cond/branch_0_fun/pack_own_core/pallas_call | solution.py:107
  10.6 2.7 %collective-permute-start.3 = (bf16[256,640]{1,0:T(8,128)(2,1)S(1)}, bf16[256,640]{1,0:T(8,128)(2,1)S(1)}, u32[]{:S(2)}, u32[]{:S(2)}) collective-permute-start(bf16[256,640]{1,0:T(8,128)(2,1)S(1)} %get-tuple-element.55), channel_id=1, source_target_pairs={{0,2},{1,3},{2,0},{3,1},{4,6},{5,7},{6,4},{7,5},{8,10},{9,11},{10,... | collective-permute-start | bytes 983048 | tf_op jit(solution)/shard_map/cond/branch_0_fun/ppermute | solution.py:174
  13.2 2.6 %collective-permute-start.1 = (bf16[256,640]{1,0:T(8,128)(2,1)S(1)}, bf16[256,640]{1,0:T(8,128)(2,1)S(1)}, u32[]{:S(2)}, u32[]{:S(2)}) collective-permute-start(bf16[256,640]{1,0:T(8,128)(2,1)S(1)} %get-tuple-element.52), channel_id=1, source_target_pairs={{0,4},{1,5},{2,6},{3,7},{4,0},{5,1},{6,2},{7,3},{8,12},{9,13},{10,... | collective-permute-start | bytes 983048 | tf_op jit(solution)/shard_map/cond/branch_0_fun/ppermute | solution.py:174
  15.8 12.4 %collective-permute-done.3.refs_1_ = bf16[256,640]{1,0:T(8,128)(2,1)S(1)} collective-permute-done((bf16[256,640]{1,0:T(8,128)(2,1)S(1)}, bf16[256,640]{1,0:T(8,128)(2,1)S(1)}, u32[]{:S(2)}, u32[]{:S(2)}) %collective-permute-start.3) | collective-permute-done | bytes 327712 | tf_op jit(solution)/shard_map/cond/branch_0_fun/ppermute | solution.py:174
  28.2 1.1 %pack_part.7.refs_6_.refs_2_ = bf16[384,640]{1,0:T(8,128)(2,1)S(1)} custom-call(s32[128]{0:T(128)S(1)} %copy-done.21, bf16[256,640]{1,0:T(8,128)(2,1)S(1)} %get-tuple-element.54.refs_0_, bf16[256,640]{1,0:T(8,128)(2,1)S(1)} %collective-permute-done.3.refs_1_), custom_call_target="tpu_custom_call" | custom-call | flops 251658240 | bytes 1146880 | tf_op jit(solution)/shard_map/cond/branch_0_fun/pack_part/pallas_call | solution.py:160
  29.3 1.7 %collective-permute-start.5 = (bf16[384,640]{1,0:T(8,128)(2,1)S(1)}, bf16[384,640]{1,0:T(8,128)(2,1)S(1)}, u32[]{:S(2)}, u32[]{:S(2)}) collective-permute-start(bf16[384,640]{1,0:T(8,128)(2,1)S(1)} %pack_part.7.refs_6_.refs_2_), channel_id=1, source_target_pairs={{0,16},{8,24},{16,0},{24,8},{1,17},{9,25},{17,1},{25,9},{2,18},{10... | collective-permute-start | bytes 1474568 | tf_op jit(solution)/shard_map/cond/branch_0_fun/ppermute | solution.py:174
  31.1 1.5 %collective-permute-start.4 = (bf16[384,640]{1,0:T(8,128)(2,1)S(1)}, bf16[384,640]{1,0:T(8,128)(2,1)S(1)}, u32[]{:S(2)}, u32[]{:S(2)}) collective-permute-start(bf16[384,640]{1,0:T(8,128)(2,1)S(1)} %pack_part.7.refs_6_.refs_2_), channel_id=1, source_target_pairs={{0,8},{8,0},{16,24},{24,16},{1,9},{9,1},{17,25},{25,17},{2,10},{10... | collective-permute-start | bytes 1474568 | tf_op jit(solution)/shard_map/cond/branch_0_fun/ppermute | solution.py:174
  32.6 6.2 %collective-permute-done.1.refs_0_ = bf16[256,640]{1,0:T(8,128)(2,1)S(1)} collective-permute-done((bf16[256,640]{1,0:T(8,128)(2,1)S(1)}, bf16[256,640]{1,0:T(8,128)(2,1)S(1)}, u32[]{:S(2)}, u32[]{:S(2)}) %collective-permute-start.1) | collective-permute-done | bytes 327712 | tf_op jit(solution)/shard_map/cond/branch_0_fun/ppermute | solution.py:174
  38.8 1.1 %pack_part.6.refs_7_.refs_3_ = bf16[384,640]{1,0:T(8,128)(2,1)S(1)} custom-call(s32[128]{0:T(128)S(1)} %copy-done.21, bf16[256,640]{1,0:T(8,128)(2,1)S(1)} %collective-permute-done.1.refs_0_, bf16[256,640]{1,0:T(8,128)(2,1)S(1)} %collective-permute-done.2.refs_1_), custom_call_target="tpu_custom_call" | custom-call | flops 2768240640 | bytes 1146880 | tf_op jit(solution)/shard_map/cond/branch_0_fun/pack_part/pallas_call | solution.py:160
  39.9 2.5 %collective-permute-done.5.refs_10_.refs_6_ = bf16[384,640]{1,0:T(8,128)(2,1)S(1)} collective-permute-done((bf16[384,640]{1,0:T(8,128)(2,1)S(1)}, bf16[384,640]{1,0:T(8,128)(2,1)S(1)}, u32[]{:S(2)}, u32[]{:S(2)}) %collective-permute-start.5) | collective-permute-done | bytes 491552 | tf_op jit(solution)/shard_map/cond/branch_0_fun/ppermute | solution.py:174
  42.5 1.2 %collective-permute-done.4.refs_8_.refs_4_ = bf16[384,640]{1,0:T(8,128)(2,1)S(1)} collective-permute-done((bf16[384,640]{1,0:T(8,128)(2,1)S(1)}, bf16[384,640]{1,0:T(8,128)(2,1)S(1)}, u32[]{:S(2)}, u32[]{:S(2)}) %collective-permute-start.4) | collective-permute-done | bytes 491552 | tf_op jit(solution)/shard_map/cond/branch_0_fun/ppermute | solution.py:174
  43.6 4.2 %collective-permute-start.6 = (bf16[768,384]{1,0:T(8,128)(2,1)S(1)}, bf16[768,384]{1,0:T(8,128)(2,1)S(1)}, u32[]{:S(2)}, u32[]{:S(2)}) collective-permute-start(bf16[768,384]{1,0:T(8,128)(2,1)S(1)} %pack_density.3.refs_0_), channel_id=1, source_target_pairs={{0,4},{1,5},{2,6},{3,7},{4,0},{5,1},{6,2},{7,3},{8,12},{9,13},{10,... | collective-permute-start | bytes 1769480 | tf_op jit(solution)/shard_map/cond/branch_0_fun/ppermute | solution.py:174
  47.9 1.5 %collective-permute-start.10 = (bf16[384,640]{1,0:T(8,128)(2,1)S(1)}, bf16[384,640]{1,0:T(8,128)(2,1)S(1)}, u32[]{:S(2)}, u32[]{:S(2)}) collective-permute-start(bf16[384,640]{1,0:T(8,128)(2,1)S(1)} %pack_part.6.refs_7_.refs_3_), channel_id=1, source_target_pairs={{0,16},{8,24},{16,0},{24,8},{1,17},{9,25},{17,1},{25,9},{2,18},{10... | collective-permute-start | bytes 1474568 | tf_op jit(solution)/shard_map/cond/branch_0_fun/ppermute | solution.py:174
  49.4 1.5 %collective-permute-start.9 = (bf16[384,640]{1,0:T(8,128)(2,1)S(1)}, bf16[384,640]{1,0:T(8,128)(2,1)S(1)}, u32[]{:S(2)}, u32[]{:S(2)}) collective-permute-start(bf16[384,640]{1,0:T(8,128)(2,1)S(1)} %pack_part.6.refs_7_.refs_3_), channel_id=1, source_target_pairs={{0,8},{8,0},{16,24},{24,16},{1,9},{9,1},{17,25},{25,17},{2,10},{10... | collective-permute-start | bytes 1474568 | tf_op jit(solution)/shard_map/cond/branch_0_fun/ppermute | solution.py:174
  51.4 22.1 %collective-permute-done.6.refs_2_ = bf16[768,384]{1,0:T(8,128)(2,1)S(1)} collective-permute-done((bf16[768,384]{1,0:T(8,128)(2,1)S(1)}, bf16[768,384]{1,0:T(8,128)(2,1)S(1)}, u32[]{:S(2)}, u32[]{:S(2)}) %collective-permute-start.6) | collective-permute-done | bytes 589856 | tf_op jit(solution)/shard_map/cond/branch_0_fun/ppermute | solution.py:174
  74.1 1.5 %collective-permute-start.12 = (bf16[384,640]{1,0:T(8,128)(2,1)S(1)}, bf16[384,640]{1,0:T(8,128)(2,1)S(1)}, u32[]{:S(2)}, u32[]{:S(2)}) collective-permute-start(bf16[384,640]{1,0:T(8,128)(2,1)S(1)} %collective-permute-done.10.refs_11_.refs_7_), channel_id=1, source_target_pairs={{0,8},{8,0},{16,24},{24,16},{1,9},{9,1},{17,25},{25,17},{2,10},{10... | collective-permute-start | bytes 1474568 | tf_op jit(solution)/shard_map/cond/branch_0_fun/ppermute | solution.py:174
  75.7 11.8 %collective-permute-done.7.refs_0_ = bf16[768,384]{1,0:T(8,128)(2,1)S(1)} collective-permute-done((bf16[768,384]{1,0:T(8,128)(2,1)S(1)}, bf16[768,384]{1,0:T(8,128)(2,1)S(1)}, u32[]{:S(2)}, u32[]{:S(2)}) %collective-permute-start.7) | collective-permute-done | bytes 589856 | tf_op jit(solution)/shard_map/cond/branch_0_fun/ppermute | solution.py:174
  88.5 0.8 copy-done.20
  89.3 9.1 %contract_first.3.refs_10_ = f32[768,640]{1,0:T(8,128)} custom-call(s32[128]{0:T(128)S(1)} %copy-done.21, s32[48]{0:T(128)S(1)} %copy-done.30, bf16[768,384]{1,0:T(8,128)(2,1)S(1)} %pack_density.3.refs_0_, bf16[768,384]{1,0:T(8,128)(2,1)S(1)} %collective-permute-done.13.refs_1_, bf16[768,384]{1,0:T(8,128)(2,1)S(1)} %collective-permute-done.6.refs_2_, ...), custom_call_target="tpu_custom_call" | custom-call | flops 2264924160 | bytes 6488064 | tf_op jit(solution)/shard_map/cond/branch_0_fun/contract_first/pallas_call | solution.py:258
  98.4 7.1 %contract_last.3 = bf16[1024,768]{1,0:T(8,128)(2,1)} custom-call(s32[128]{0:T(128)S(1)} %copy-done.21, s32[48]{0:T(128)S(1)} %copy-done.30, bf16[768,384]{1,0:T(8,128)(2,1)S(1)} %collective-permute-done.7.refs_0_, bf16[768,384]{1,0:T(8,128)(2,1)S(1)} %collective-permute-done.8.refs_1_, bf16[384,640]{1,0:T(8,128)(2,1)S(1)} %pack_part.7.refs_6_.refs_2_, ...), custom_call_target="tpu_custom_call" | custom-call | flops 754974720 | bytes 2162688 | tf_op jit(solution)/shard_map/cond/branch_0_fun/contract_last/pallas_call | solution.py:258
  (38 shorter events, 2.7 us)
Async XLA Ops:
  2.0 3.7 %copy-start.27 = (s32[32,16]{0,1:T(8,128)S(1)}, s32[32,16]{0,1:T(8,128)}, u32[]{:S(2)}) copy-start(s32[32,16]{0,1:T(8,128)} %get-tuple-element.86) | copy-start | bytes 6148 | tf_op jit(solution)/shard_map/cond
  2.0 3.7 %copy-start.21 = (s32[128]{0:T(128)S(1)}, s32[128]{0:T(128)}, u32[]{:S(2)}) copy-start(s32[128]{0:T(128)} %get-tuple-element.44.count_ref) | copy-start | bytes 1540 | tf_op jit(solution)/shard_map/cond
  2.0 3.7 %copy-start.33 = (bf16[1024,512]{1,0:T(8,128)(2,1)S(1)}, bf16[1024,512]{1,0:T(8,128)(2,1)}, u32[]{:S(2)}) copy-start(bf16[1024,512]{1,0:T(8,128)(2,1)} %get-tuple-element.48.x_ref) | copy-start | bytes 3145732 | tf_op jit(solution)/shard_map/cond
  5.1 3.2 %collective-permute-start = (bf16[4,128,640]{2,1,0:T(8,128)(2,1)S(1)}, bf16[4,128,640]{2,1,0:T(8,128)(2,1)S(1)}, u32[]{:S(2)}, u32[]{:S(2)}) collective-permute-start(bf16[4,128,640]{2,1,0:T(8,128)(2,1)S(1)} %pack_other_core.3), channel_id=1, source_target_pairs={{0,1},{1,0},{2,3},{3,2},{4,5},{5,4},{6,7},{7,6},{8,9},{9,8},{10,11... | collective-permute-start | bytes 1966088 | tf_op jit(solution)/shard_map/cond/branch_0_fun/ppermute | solution.py:174
  5.7 2.6 %copy-start.9 = (bf16[128,6144]{1,0:T(8,128)(2,1)S(1)}, bf16[128,6144]{1,0:T(8,128)(2,1)}, u32[]{:S(2)}) copy-start(bf16[128,6144]{1,0:T(8,128)(2,1)} %get-tuple-element.50.x_ref) | copy-start | bytes 4718596 | tf_op jit(solution)/shard_map/cond
  5.7 2.6 %copy-start.24 = (s32[4,48]{1,0:T(4,128)S(1)}, s32[4,48]{1,0:T(4,128)}, u32[]{:S(2)}) copy-start(s32[4,48]{1,0:T(4,128)} %get-tuple-element.49.mask_ref) | copy-start | bytes 2308 | tf_op jit(solution)/shard_map/cond
  5.8 2.6 %copy-start.30 = (s32[48]{0:T(128)S(1)}, s32[48]{0:T(128)}, u32[]{:S(2)}) copy-start(s32[48]{0:T(128)} %get-tuple-element.46.ri_ref) | copy-start | bytes 580 | tf_op jit(solution)/shard_map/cond
  10.6 17.6 %collective-permute-start.3 = (bf16[256,640]{1,0:T(8,128)(2,1)S(1)}, bf16[256,640]{1,0:T(8,128)(2,1)S(1)}, u32[]{:S(2)}, u32[]{:S(2)}) collective-permute-start(bf16[256,640]{1,0:T(8,128)(2,1)S(1)} %get-tuple-element.55), channel_id=1, source_target_pairs={{0,2},{1,3},{2,0},{3,1},{4,6},{5,7},{6,4},{7,5},{8,10},{9,11},{10,... | collective-permute-start | bytes 983048 | tf_op jit(solution)/shard_map/cond/branch_0_fun/ppermute | solution.py:174
  13.2 25.5 %collective-permute-start.1 = (bf16[256,640]{1,0:T(8,128)(2,1)S(1)}, bf16[256,640]{1,0:T(8,128)(2,1)S(1)}, u32[]{:S(2)}, u32[]{:S(2)}) collective-permute-start(bf16[256,640]{1,0:T(8,128)(2,1)S(1)} %get-tuple-element.52), channel_id=1, source_target_pairs={{0,4},{1,5},{2,6},{3,7},{4,0},{5,1},{6,2},{7,3},{8,12},{9,13},{10,... | collective-permute-start | bytes 983048 | tf_op jit(solution)/shard_map/cond/branch_0_fun/ppermute | solution.py:174
  15.8 22.9 %collective-permute-start.2 = (bf16[256,640]{1,0:T(8,128)(2,1)S(1)}, bf16[256,640]{1,0:T(8,128)(2,1)S(1)}, u32[]{:S(2)}, u32[]{:S(2)}) collective-permute-start(bf16[256,640]{1,0:T(8,128)(2,1)S(1)} %get-tuple-element.53), channel_id=1, source_target_pairs={{0,6},{1,7},{2,4},{3,5},{4,2},{5,3},{6,0},{7,1},{8,14},{9,15},{10,... | collective-permute-start | bytes 983048 | tf_op jit(solution)/shard_map/cond/branch_0_fun/ppermute | solution.py:174
  29.3 13.1 %collective-permute-start.5 = (bf16[384,640]{1,0:T(8,128)(2,1)S(1)}, bf16[384,640]{1,0:T(8,128)(2,1)S(1)}, u32[]{:S(2)}, u32[]{:S(2)}) collective-permute-start(bf16[384,640]{1,0:T(8,128)(2,1)S(1)} %pack_part.7.refs_6_.refs_2_), channel_id=1, source_target_pairs={{0,16},{8,24},{16,0},{24,8},{1,17},{9,25},{17,1},{25,9},{2,18},{10... | collective-permute-start | bytes 1474568 | tf_op jit(solution)/shard_map/cond/branch_0_fun/ppermute | solution.py:174
  31.1 12.5 %collective-permute-start.4 = (bf16[384,640]{1,0:T(8,128)(2,1)S(1)}, bf16[384,640]{1,0:T(8,128)(2,1)S(1)}, u32[]{:S(2)}, u32[]{:S(2)}) collective-permute-start(bf16[384,640]{1,0:T(8,128)(2,1)S(1)} %pack_part.7.refs_6_.refs_2_), channel_id=1, source_target_pairs={{0,8},{8,0},{16,24},{24,16},{1,9},{9,1},{17,25},{25,17},{2,10},{10... | collective-permute-start | bytes 1474568 | tf_op jit(solution)/shard_map/cond/branch_0_fun/ppermute | solution.py:174
  43.6 29.9 %collective-permute-start.6 = (bf16[768,384]{1,0:T(8,128)(2,1)S(1)}, bf16[768,384]{1,0:T(8,128)(2,1)S(1)}, u32[]{:S(2)}, u32[]{:S(2)}) collective-permute-start(bf16[768,384]{1,0:T(8,128)(2,1)S(1)} %pack_density.3.refs_0_), channel_id=1, source_target_pairs={{0,4},{1,5},{2,6},{3,7},{4,0},{5,1},{6,2},{7,3},{8,12},{9,13},{10,... | collective-permute-start | bytes 1769480 | tf_op jit(solution)/shard_map/cond/branch_0_fun/ppermute | solution.py:174
  47.9 25.7 %collective-permute-start.15 = (bf16[768,384]{1,0:T(8,128)(2,1)S(1)}, bf16[768,384]{1,0:T(8,128)(2,1)S(1)}, u32[]{:S(2)}, u32[]{:S(2)}) collective-permute-start(bf16[768,384]{1,0:T(8,128)(2,1)S(1)} %pack_density.3.refs_0_), channel_id=1, source_target_pairs={{0,2},{1,3},{2,0},{3,1},{4,6},{5,7},{6,4},{7,5},{8,10},{9,11},{10,... | collective-permute-start | bytes 1769480 | tf_op jit(solution)/shard_map/cond/branch_0_fun/ppermute | solution.py:174
  47.9 25.6 %collective-permute-start.10 = (bf16[384,640]{1,0:T(8,128)(2,1)S(1)}, bf16[384,640]{1,0:T(8,128)(2,1)S(1)}, u32[]{:S(2)}, u32[]{:S(2)}) collective-permute-start(bf16[384,640]{1,0:T(8,128)(2,1)S(1)} %pack_part.6.refs_7_.refs_3_), channel_id=1, source_target_pairs={{0,16},{8,24},{16,0},{24,8},{1,17},{9,25},{17,1},{25,9},{2,18},{10... | collective-permute-start | bytes 1474568 | tf_op jit(solution)/shard_map/cond/branch_0_fun/ppermute | solution.py:174
  49.4 24.6 %collective-permute-start.9 = (bf16[384,640]{1,0:T(8,128)(2,1)S(1)}, bf16[384,640]{1,0:T(8,128)(2,1)S(1)}, u32[]{:S(2)}, u32[]{:S(2)}) collective-permute-start(bf16[384,640]{1,0:T(8,128)(2,1)S(1)} %pack_part.6.refs_7_.refs_3_), channel_id=1, source_target_pairs={{0,8},{8,0},{16,24},{24,16},{1,9},{9,1},{17,25},{25,17},{2,10},{10... | collective-permute-start | bytes 1474568 | tf_op jit(solution)/shard_map/cond/branch_0_fun/ppermute | solution.py:174
  50.9 23.3 %collective-permute-start.11 = (bf16[384,640]{1,0:T(8,128)(2,1)S(1)}, bf16[384,640]{1,0:T(8,128)(2,1)S(1)}, u32[]{:S(2)}, u32[]{:S(2)}) collective-permute-start(bf16[384,640]{1,0:T(8,128)(2,1)S(1)} %collective-permute-done.4.refs_8_.refs_4_), channel_id=1, source_target_pairs={{0,16},{8,24},{16,0},{24,8},{1,17},{9,25},{17,1},{25,9},{2,18},{10... | collective-permute-start | bytes 1474568 | tf_op jit(solution)/shard_map/cond/branch_0_fun/ppermute | solution.py:174
  73.5 14.0 %collective-permute-start.7 = (bf16[768,384]{1,0:T(8,128)(2,1)S(1)}, bf16[768,384]{1,0:T(8,128)(2,1)S(1)}, u32[]{:S(2)}, u32[]{:S(2)}) collective-permute-start(bf16[768,384]{1,0:T(8,128)(2,1)S(1)} %collective-permute-done.6.refs_2_), channel_id=1, source_target_pairs={{0,2},{1,3},{2,0},{3,1},{4,6},{5,7},{6,4},{7,5},{8,10},{9,11},{10,... | collective-permute-start | bytes 1769480 | tf_op jit(solution)/shard_map/cond/branch_0_fun/ppermute | solution.py:174
  73.5 14.0 %collective-permute-start.13 = (bf16[768,384]{1,0:T(8,128)(2,1)S(1)}, bf16[768,384]{1,0:T(8,128)(2,1)S(1)}, u32[]{:S(2)}, u32[]{:S(2)}) collective-permute-start(bf16[768,384]{1,0:T(8,128)(2,1)S(1)} %pack_density.3.refs_0_), channel_id=1, source_target_pairs={{0,1},{1,0},{2,3},{3,2},{4,5},{5,4},{6,7},{7,6},{8,9},{9,8},{10,11... | collective-permute-start | bytes 1769480 | tf_op jit(solution)/shard_map/cond/branch_0_fun/ppermute | solution.py:174
  73.6 14.0 %copy-start.18 = (bf16[768,384]{1,0:T(8,128)(2,1)}, bf16[768,384]{1,0:T(8,128)(2,1)S(1)}, u32[]{:S(2)}) copy-start(bf16[768,384]{1,0:T(8,128)(2,1)S(1)} %collective-permute-done.15.refs_4_) | copy-start | bytes 1769476 | tf_op jit(solution)/shard_map/cond
  73.6 14.0 %collective-permute-start.16 = (bf16[768,384]{1,0:T(8,128)(2,1)S(1)}, bf16[768,384]{1,0:T(8,128)(2,1)S(1)}, u32[]{:S(2)}, u32[]{:S(2)}) collective-permute-start(bf16[768,384]{1,0:T(8,128)(2,1)S(1)} %collective-permute-done.15.refs_4_), channel_id=1, source_target_pairs={{0,1},{1,0},{2,3},{3,2},{4,5},{5,4},{6,7},{7,6},{8,9},{9,8},{10,11... | collective-permute-start | bytes 1769480 | tf_op jit(solution)/shard_map/cond/branch_0_fun/ppermute | solution.py:174
  74.0 13.7 %collective-permute-start.14 = (bf16[768,384]{1,0:T(8,128)(2,1)S(1)}, bf16[768,384]{1,0:T(8,128)(2,1)S(1)}, u32[]{:S(2)}, u32[]{:S(2)}) collective-permute-start(bf16[768,384]{1,0:T(8,128)(2,1)S(1)} %collective-permute-done.6.refs_2_), channel_id=1, source_target_pairs={{0,1},{1,0},{2,3},{3,2},{4,5},{5,4},{6,7},{7,6},{8,9},{9,8},{10,11... | collective-permute-start | bytes 1769480 | tf_op jit(solution)/shard_map/cond/branch_0_fun/ppermute | solution.py:174
  74.1 13.5 %collective-permute-start.12 = (bf16[384,640]{1,0:T(8,128)(2,1)S(1)}, bf16[384,640]{1,0:T(8,128)(2,1)S(1)}, u32[]{:S(2)}, u32[]{:S(2)}) collective-permute-start(bf16[384,640]{1,0:T(8,128)(2,1)S(1)} %collective-permute-done.10.refs_11_.refs_7_), channel_id=1, source_target_pairs={{0,8},{8,0},{16,24},{24,16},{1,9},{9,1},{17,25},{25,17},{2,10},{10... | collective-permute-start | bytes 1474568 | tf_op jit(solution)/shard_map/cond/branch_0_fun/ppermute | solution.py:174
  87.5 10.9 %collective-permute-start.8 = (bf16[768,384]{1,0:T(8,128)(2,1)S(1)}, bf16[768,384]{1,0:T(8,128)(2,1)S(1)}, u32[]{:S(2)}, u32[]{:S(2)}) collective-permute-start(bf16[768,384]{1,0:T(8,128)(2,1)S(1)} %collective-permute-done.7.refs_0_), channel_id=1, source_target_pairs={{0,1},{1,0},{2,3},{3,2},{4,5},{5,4},{6,7},{7,6},{8,9},{9,8},{10,11... | collective-permute-start | bytes 1769480 | tf_op jit(solution)/shard_map/cond/branch_0_fun/ppermute | solution.py:174
  (2 other events, 1.6 us)
